TPU v7x, 32 devices: a whole 2x2x4 slice. The times are simulated.
32 devices in a mesh: pipe: 2 (over core), dp: 16 (over z, y, x).
Axes of the slice: x: 2, y: 2, z: 4, core: 2. Of those that a mesh axis runs over, the one named last changes fastest.
Arguments:
- tokens: bfloat16 [2, 16, 512, 384], P(None, 'dp'), may hold values from -6 to 6
- prompts: bfloat16 [2, 16, 512, 384], P(None, 'dp'), may hold values from -6 to 6
- cotangent: bfloat16 [2, 16, 512, 384], P(None, 'dp'), may hold values from -6 to 6
- segments: int32 [2, 16, 512], P(None, 'dp'), may hold values from 0 to 7, never falling along the last dimension, each value on 1 to 256 neighbouring positions
- weight_in: float32 [2, 384, 1152], P('pipe', 'dp')
- weight_out: float32 [2, 384, 384], P('pipe', 'dp')
- weight_up: float32 [2, 384, 1536], P('pipe', 'dp')
- weight_down: float32 [2, 1536, 384], P('pipe', 'dp')
- first_in: float32 [2, 384, 1152], P('pipe', 'dp')
- first_out: float32 [2, 384, 384], P('pipe', 'dp')
- first_up: float32 [2, 384, 1536], P('pipe', 'dp')
- first_down: float32 [2, 1536, 384], P('pipe', 'dp')
- second_in: float32 [2, 384, 1152], P('pipe', 'dp'), as said below
- second_out: float32 [2, 384, 384], P('pipe', 'dp'), as said below
- second_up: float32 [2, 384, 1536], P('pipe', 'dp'), as said below
- second_down: float32 [2, 1536, 384], P('pipe', 'dp'), as said below
- gains: float32 [2, 2, 384], P('pipe'), as said below
- gain_first: float32 [2, 2, 384], P('pipe')
- gain_second: float32 [2, 2, 384], P('pipe'), as said below
Outputs:
- section_result: float32 [2, 2, 16, 512, 384], P('pipe', None, 'dp')
- drift_in: float32 [2, 384, 1152], P('pipe', 'dp')
- drift_out: float32 [2, 384, 384], P('pipe', 'dp')
- drift_up: float32 [2, 384, 1536], P('pipe', 'dp')
- drift_down: float32 [2, 1536, 384], P('pipe', 'dp')
- spread_in: float32 [2, 384, 1152], P('pipe', 'dp')
- spread_out: float32 [2, 384, 384], P('pipe', 'dp')
- spread_up: float32 [2, 384, 1536], P('pipe', 'dp')
- spread_down: float32 [2, 1536, 384], P('pipe', 'dp')
- updated_in: float32 [2, 384, 1152], P('pipe', 'dp')
- updated_out: float32 [2, 384, 384], P('pipe', 'dp')
- updated_up: float32 [2, 384, 1536], P('pipe', 'dp')
- updated_down: float32 [2, 1536, 384], P('pipe', 'dp')
- copied_in: bfloat16 [2, 384, 1152], P('pipe', 'dp')
- copied_out: bfloat16 [2, 384, 384], P('pipe', 'dp')
- copied_up: bfloat16 [2, 384, 1536], P('pipe', 'dp')
- copied_down: bfloat16 [2, 1536, 384], P('pipe', 'dp')
- gain_drift: float32 [2, 2, 384], P('pipe')
- gain_spread: float32 [2, 2, 384], P('pipe')
- gain_updated: float32 [2, 2, 384], P('pipe')
- norm_pairs: float32 [2, 6, 2], P('pipe')
Inputs may be any that keep to these rules, and one draw needn't show every extreme that they name: `segments`: segment numbers never fall along a sequence; each segment holds 1 to 256 rows. `second_in`: positive. `second_out`: positive. `second_up`: positive. `second_down`: positive. `gain_second`: positive. `gains`: positive.
All inputs are finite; a program needn't handle non-finite values.
Results may differ from a plain program's by a relative error of at most 0.025.
The roundings to bfloat16 on the way count: a program that leaves them out, or rounds other values in their place, can miss the bound.
Values may be sent and summed in bfloat16 or wider, within the bound.
No kernel may reach another device: no remote copies, remote signals or barrier semaphores. Data moves between devices by JAX's collectives and lax.ppermute only.
A program may use at most 128 MiB of HBM per device.

v0:
```python
import jax
import jax.numpy as jnp
from jax import lax
from jax.sharding import PartitionSpec as P

D = 384
HEADS = 6
HEAD_DIM = 64
STEP = 3


rate = 0.3
beta = 0.5
eps_adam = 1e-06
decay = 0.01
eps_norm = 1e-05
neg_large = -1e30
block_rows = 512


def from_behind(block, axis, distance):
    devices = range(lax.axis_size(axis))
    route = [(i - distance, i) for i in devices if i - distance in devices]
    return lax.ppermute(block, axis, route)


def norm_parts(inputs):
    average = jnp.mean(inputs, axis=-1, keepdims=True)
    centered = inputs - average
    variance = jnp.mean(centered * centered, axis=-1, keepdims=True)
    inverse = lax.rsqrt(variance + eps_norm)
    return (centered * inverse, inverse)


def norm_back(grad_unit, unit, inverse):
    first_mean = jnp.mean(grad_unit, axis=-1, keepdims=True)
    cross_mean = jnp.mean(grad_unit * unit, axis=-1, keepdims=True)
    return (grad_unit - first_mean - unit * cross_mean) * inverse


def split_heads(packed, member):
    length = packed.shape[0]
    return packed[:, member * D : (member + 1) * D].reshape(length, HEADS, HEAD_DIM)


def masked_scores(queries, key_rows, segment_row):
    row_count = queries.shape[0]
    length = key_rows.shape[0]
    products = jnp.einsum(
        "qhd,khd->hqk", queries, key_rows, preferred_element_type=jnp.float32
    ) * HEAD_DIM ** (-0.5)
    position = jnp.arange(row_count)
    allowed = (segment_row[:, None] == segment_row[None, :]) & (
        jnp.arange(length)[None, :] <= position[:, None]
    )
    return jnp.where(allowed[None], products, neg_large)


def attend(packed, segment_row):
    length = packed.shape[0]
    span = min(block_rows, length)
    queries_all = split_heads(packed, 0)
    key_rows = split_heads(packed, 1)
    value_rows = split_heads(packed, 2)
    scores = masked_scores(queries_all, key_rows, segment_row)
    largest = jnp.max(scores, axis=-1, keepdims=True)
    lifted = jnp.exp(scores - largest)
    summed = jnp.sum(lifted, axis=-1, keepdims=True)
    chances = (lifted / summed).astype(jnp.bfloat16)
    piece = jnp.einsum("hqk,khd->qhd", chances, value_rows, preferred_element_type=jnp.float32)
    pieces = piece.reshape(span, D)
    totals = largest + jnp.log(summed)
    return (pieces.astype(jnp.bfloat16), totals)


def attend_back(packed, segment_row, totals, grad_attended):
    length = packed.shape[0]
    span = min(block_rows, length)
    queries_all = split_heads(packed, 0)
    key_rows = split_heads(packed, 1)
    value_rows = split_heads(packed, 2)
    scale = HEAD_DIM ** (-0.5)
    scores = masked_scores(queries_all, key_rows, segment_row)
    chances = jnp.exp(scores - totals)
    grad_piece = grad_attended.reshape(span, HEADS, HEAD_DIM)
    grad_chances = jnp.einsum(
        "qhd,khd->hqk", grad_piece, value_rows, preferred_element_type=jnp.float32
    )
    inner = jnp.sum(chances * grad_chances, axis=-1, keepdims=True)
    grad_scores = (chances * (grad_chances - inner)).astype(jnp.bfloat16)
    grad_queries = (
        jnp.einsum("hqk,khd->qhd", grad_scores, key_rows, preferred_element_type=jnp.float32)
        * scale
    )
    grad_keys = (
        jnp.einsum("hqk,qhd->khd", grad_scores, queries_all, preferred_element_type=jnp.float32)
        * scale
    )
    grad_values = jnp.einsum(
        "hqk,qhd->khd", chances.astype(jnp.bfloat16), grad_piece, preferred_element_type=jnp.float32
    )
    joined = grad_queries.reshape(length, D)
    return jnp.concatenate(
        [joined, grad_keys.reshape(length, D), grad_values.reshape(length, D)], 1
    ).astype(jnp.bfloat16)


def block_states(inputs, segment_row, weights, gain_pair):
    matrix_in, matrix_out, matrix_up, matrix_down = weights
    unit_one, inverse_one = norm_parts(inputs)
    normed_one = (unit_one * gain_pair[0]).astype(jnp.bfloat16)
    packed = jnp.dot(normed_one, matrix_in, preferred_element_type=jnp.float32).astype(jnp.bfloat16)
    attended, totals = attend(packed, segment_row)
    middle = inputs + jnp.dot(attended, matrix_out, preferred_element_type=jnp.float32)
    unit_two, inverse_two = norm_parts(middle)
    normed_two = (unit_two * gain_pair[1]).astype(jnp.bfloat16)
    hidden = jnp.dot(normed_two, matrix_up, preferred_element_type=jnp.float32)
    active = jax.nn.gelu(hidden).astype(jnp.bfloat16)
    output = middle + jnp.dot(active, matrix_down, preferred_element_type=jnp.float32)
    kept = (
        unit_one,
        inverse_one,
        normed_one,
        packed,
        attended,
        totals,
        unit_two,
        inverse_two,
        normed_two,
        hidden,
        active,
    )
    return (output, kept)


def block_back(inputs, segment_row, weights, gain_pair, grad_output):
    matrix_in, matrix_out, matrix_up, matrix_down = weights
    output, kept = block_states(inputs, segment_row, weights, gain_pair)
    (
        unit_one,
        inverse_one,
        normed_one,
        packed,
        attended,
        totals,
        unit_two,
        inverse_two,
        normed_two,
        hidden,
        active,
    ) = kept
    grad_branch = grad_output.astype(jnp.bfloat16)
    grad_down = jnp.dot(active.T, grad_branch, preferred_element_type=jnp.float32)
    grad_active = jnp.dot(grad_branch, matrix_down.T, preferred_element_type=jnp.float32)
    grad_hidden = jax.vjp(jax.nn.gelu, hidden)[1](grad_active)[0].astype(jnp.bfloat16)
    grad_up = jnp.dot(normed_two.T, grad_hidden, preferred_element_type=jnp.float32)
    grad_normed_two = jnp.dot(grad_hidden, matrix_up.T, preferred_element_type=jnp.float32)
    grad_middle = grad_output + norm_back(grad_normed_two * gain_pair[1], unit_two, inverse_two)
    grad_middle_low = grad_middle.astype(jnp.bfloat16)
    grad_out = jnp.dot(attended.T, grad_middle_low, preferred_element_type=jnp.float32)
    grad_attended = jnp.dot(
        grad_middle_low, matrix_out.T, preferred_element_type=jnp.float32
    ).astype(jnp.bfloat16)
    grad_packed = attend_back(packed, segment_row, totals, grad_attended)
    grad_in = jnp.dot(normed_one.T, grad_packed, preferred_element_type=jnp.float32)
    grad_normed_one = jnp.dot(grad_packed, matrix_in.T, preferred_element_type=jnp.float32)
    grad_inputs = grad_middle + norm_back(grad_normed_one * gain_pair[0], unit_one, inverse_one)
    gain_grads = jnp.stack(
        [jnp.sum(grad_normed_one * unit_one, axis=0), jnp.sum(grad_normed_two * unit_two, axis=0)]
    )
    return (grad_inputs, (grad_in, grad_out, grad_up, grad_down), gain_grads)


def moments(master, grad, first, second):
    drift = beta * first + (1.0 - beta) * grad
    spread = beta * second + (1.0 - beta) * grad * grad
    correction = 1.0 - beta**STEP
    update = drift / correction / (jnp.sqrt(spread / correction) + eps_adam) + decay * master
    return (drift, spread, update)


def per_device(
    tokens,
    prompts,
    cotangent,
    segments,
    weight_in,
    weight_out,
    weight_up,
    weight_down,
    first_in,
    first_out,
    first_up,
    first_down,
    second_in,
    second_out,
    second_up,
    second_down,
    gains,
    gain_first,
    gain_second,
):
    section = lax.axis_index("pipe")
    leading = section == 0
    masters = (weight_in[0], weight_out[0], weight_up[0], weight_down[0])
    weight_sums = lax.psum(jnp.stack([jnp.sum(matrix * matrix) for matrix in masters]), "dp")
    weights = (
        lax.all_gather(masters[0].astype(jnp.bfloat16), "dp", axis=0, tiled=True),
        lax.all_gather(masters[1].astype(jnp.bfloat16), "dp", axis=0, tiled=True),
        lax.all_gather(masters[2].astype(jnp.bfloat16), "dp", axis=0, tiled=True),
        lax.all_gather(masters[3].astype(jnp.bfloat16), "dp", axis=0, tiled=True),
    )
    gain_pair = gains[0]
    batches = tokens.shape[0]
    length = tokens.shape[2]
    segment_rows = segments[:, 0]
    received = jnp.zeros((length, D), jnp.bfloat16)
    section_inputs = []
    section_outputs = []
    for turn_index in range(batches + 1):
        own_index = min(turn_index, batches - 1)
        later_index = max(turn_index - 1, 0)
        inputs = jnp.where(
            leading,
            tokens[own_index, 0].astype(jnp.float32),
            received.astype(jnp.float32) + prompts[later_index, 0].astype(jnp.float32),
        )
        segment_row = jnp.where(leading, segment_rows[own_index], segment_rows[later_index])
        output = block_states(inputs, segment_row, weights, gain_pair)[0]
        section_inputs.append((inputs, segment_row))
        section_outputs.append(output)
        if turn_index < batches:
            received = from_behind(output.astype(jnp.bfloat16), "pipe", 1)
    received = jnp.zeros((length, D), jnp.bfloat16)
    mat_totals = None
    gain_total = None
    returned = []
    for turn_index in range(batches + 1):
        late_index = min(turn_index, batches - 1)
        early_index = max(turn_index - 1, 0)
        inputs = jnp.where(
            leading, section_inputs[early_index][0], section_inputs[late_index + 1][0]
        )
        segment_row = jnp.where(
            leading, section_inputs[early_index][1], section_inputs[late_index + 1][1]
        )
        late_scale = 1.0 if turn_index < batches else 0.0
        grad_output = jnp.where(
            leading,
            received.astype(jnp.float32),
            cotangent[late_index, 0].astype(jnp.float32) * late_scale,
        )
        grad_inputs, mat_grads, gain_grads = block_back(
            inputs, segment_row, weights, gain_pair, grad_output
        )
        if mat_totals is None:
            mat_totals = mat_grads
            gain_total = gain_grads
        else:
            mat_totals = tuple((total + grad for total, grad in zip(mat_totals, mat_grads)))
            gain_total = gain_total + gain_grads
        if turn_index < batches:
            received = from_behind(grad_inputs.astype(jnp.bfloat16), "pipe", -1)
        if turn_index >= 1:
            returned.append(grad_inputs)
    result_rows = jnp.stack(
        [
            jnp.where(leading, returned[member], section_outputs[member + 1])
            for member in range(batches)
        ]
    )
    section_result = result_rows[None, :, None]
    group_size = lax.axis_size("dp")
    own_place = lax.axis_index("dp")
    summed = lax.psum(
        (mat_totals[0], mat_totals[1], mat_totals[2], mat_totals[3], gain_total), "dp"
    )
    shares = tuple(
        (
            lax.dynamic_slice_in_dim(
                summed[member],
                own_place * (summed[member].shape[0] // group_size),
                summed[member].shape[0] // group_size,
                0,
            )
            for member in range(4)
        )
    )
    gain_grad = summed[4]
    firsts = (first_in[0], first_out[0], first_up[0], first_down[0])
    seconds = (second_in[0], second_out[0], second_up[0], second_down[0])
    states = [
        moments(masters[member], shares[member], firsts[member], seconds[member])
        for member in range(4)
    ]
    update_parts = jnp.stack([jnp.sum(state[2] * state[2]) for state in states])
    update_sums = lax.psum(update_parts, "dp")
    weight_norms = jnp.sqrt(weight_sums)
    update_norms = jnp.sqrt(update_sums)
    trust = weight_norms / update_norms
    updated = [masters[member] - rate * trust[member] * states[member][2] for member in range(4)]
    gain_drift, gain_spread, gain_update = moments(
        gain_pair, gain_grad, gain_first[0], gain_second[0]
    )
    gain_weight = jnp.sqrt(jnp.sum(gain_pair * gain_pair, axis=-1))
    gain_step = jnp.sqrt(jnp.sum(gain_update * gain_update, axis=-1))
    gain_new = gain_pair - rate * (gain_weight / gain_step)[:, None] * gain_update
    norm_pairs = jnp.stack(
        [jnp.concatenate([weight_norms, gain_weight]), jnp.concatenate([update_norms, gain_step])],
        axis=-1,
    )
    return (
        section_result,
        states[0][0][None],
        states[1][0][None],
        states[2][0][None],
        states[3][0][None],
        states[0][1][None],
        states[1][1][None],
        states[2][1][None],
        states[3][1][None],
        updated[0][None],
        updated[1][None],
        updated[2][None],
        updated[3][None],
        updated[0].astype(jnp.bfloat16)[None],
        updated[1].astype(jnp.bfloat16)[None],
        updated[2].astype(jnp.bfloat16)[None],
        updated[3].astype(jnp.bfloat16)[None],
        gain_drift[None],
        gain_spread[None],
        gain_new[None],
        norm_pairs[None],
    )


def solution(mesh):
    in_specs = (
        P(None, "dp", None, None),
        P(None, "dp", None, None),
        P(None, "dp", None, None),
        P(None, "dp", None),
        P("pipe", "dp", None),
        P("pipe", "dp", None),
        P("pipe", "dp", None),
        P("pipe", "dp", None),
        P("pipe", "dp", None),
        P("pipe", "dp", None),
        P("pipe", "dp", None),
        P("pipe", "dp", None),
        P("pipe", "dp", None),
        P("pipe", "dp", None),
        P("pipe", "dp", None),
        P("pipe", "dp", None),
        P("pipe", None, None),
        P("pipe", None, None),
        P("pipe", None, None),
    )
    out_specs = (
        P("pipe", None, "dp", None, None),
        P("pipe", "dp", None),
        P("pipe", "dp", None),
        P("pipe", "dp", None),
        P("pipe", "dp", None),
        P("pipe", "dp", None),
        P("pipe", "dp", None),
        P("pipe", "dp", None),
        P("pipe", "dp", None),
        P("pipe", "dp", None),
        P("pipe", "dp", None),
        P("pipe", "dp", None),
        P("pipe", "dp", None),
        P("pipe", "dp", None),
        P("pipe", "dp", None),
        P("pipe", "dp", None),
        P("pipe", "dp", None),
        P("pipe", None, None),
        P("pipe", None, None),
        P("pipe", None, None),
        P("pipe", None, None),
    )
    return jax.shard_map(
        per_device, mesh=mesh, in_specs=in_specs, out_specs=out_specs, check_vma=False
    )
```

profile of v0, /device:TPU:0, one launch (start us, length us, event | category | flops | bytes accessed | tf_op | source)
XLA Modules:
  0.0 591.1 jit_solution(16157158710360353491)
XLA Ops:
  17.7 50.7 %all_gather.13 = bf16[384,1152]{1,0:T(8,128)(2,1)S(1)} all-gather(bf16[24,1152]{1,0:T(8,128)(2,1)S(1)} %bitcast_convert_fusion.5), channel_id=1, replica_groups=mesh['pipe'=2,'dp'=16] {'dp'}, dimensions={0}, use_global_device_ids=true | all-gather | bytes 940032 | tf_op jit(solution)/shard_map/all_gather | solution.py:208
  73.3 37.9 %all_gather.14 = bf16[384,384]{1,0:T(8,128)(2,1)S(1)} all-gather(bf16[24,384]{1,0:T(8,128)(2,1)} %bitcast_convert_fusion.6), channel_id=1, replica_groups=mesh['pipe'=2,'dp'=16] {'dp'}, dimensions={0}, use_global_device_ids=true | all-gather | bytes 313344 | tf_op jit(solution)/shard_map/all_gather | solution.py:209
  111.2 6.3 %fusion.275 = (f32[6,512]{1,0:T(8,128)S(1)}, f32[6,512,512]{1,2,0:T(8,128)}) fusion(pred[512,512]{0,1:T(8,128)(4,1)} %fusion.117, bf16[512,6,64]{0,2,1:T(8,128)(2,1)} %bitcast.463, bf16[512,6,64]{0,2,1:T(8,128)(2,1)} %bitcast.462), kind=kOutput, calls=%fused_computation.475 | convolution fusion | flops 207618560 | bytes 7352320 | tf_op jit(solution)/shard_map/sub | solution.py:67
  117.4 3.5 fusion.111
  121.5 9.6 %all-gather.3.cloned.1.call-done = bf16[1536,384]{1,0:T(8,128)(2,1)} async-done(((bf16[96,384]{1,0:T(8,128)(2,1)}), bf16[1536,384]{1,0:T(8,128)(2,1)}) %all-gather.3.cloned.1.call-update) | async-done | bytes 1179664 | tf_op jit(solution)/shard_map/all_gather | solution.py:211
  131.1 4.6 fusion.96
  144.2 6.3 %fusion.277 = (f32[6,512]{1,0:T(8,128)S(1)}, f32[6,512,512]{1,2,0:T(8,128)}) fusion(pred[512,512]{0,1:T(8,128)(4,1)} %get-tuple-element.220, bf16[512,6,64]{0,2,1:T(8,128)(2,1)} %bitcast.466, bf16[512,6,64]{0,2,1:T(8,128)(2,1)} %bitcast.465), kind=kOutput, calls=%fused_computation.477 | convolution fusion | flops 207618560 | bytes 7352320 | tf_op jit(solution)/shard_map/sub | solution.py:67
  150.5 3.4 fusion.110
  154.5 4.9 fusion.279
  159.4 3.1 collective-permute-start.2
  186.1 2.9 fusion.18
  234.0 2.8 fusion.249
  236.8 3.1 fusion.25
  244.1 4.0 multiply_reduce_fusion.1
  248.1 4.6 multiply_convert_fusion.1
  263.2 3.0 convolution_add_fusion.3
  269.4 2.9 fusion.32
  288.6 3.1 convolution_add_fusion.2
  299.3 7.1 %fusion.286 = (f32[6,512]{1,0:T(8,128)}, f32[6,512,512]{1,2,0:T(8,128)}) fusion(pred[512,512]{0,1:T(8,128)(4,1)} %fusion.112, bf16[512,6,64]{0,2,1:T(8,128)(2,1)} %bitcast.460, bf16[512,6,64]{0,2,1:T(8,128)(2,1)} %bitcast.459), kind=kOutput, calls=%fused_computation.486 | convolution fusion | flops 207618560 | bytes 7352320 | tf_op jit(solution)/shard_map/sub | solution.py:67
  306.4 3.6 fusion.109
  313.2 5.6 select_bitcast_fusion
  320.3 200.2 %all-reduce.4.cloned.1.call-done = (f32[384,1152]{1,0:T(8,128)}, f32[384,384]{1,0:T(8,128)}, f32[384,1536]{1,0:T(8,128)}, f32[1536,384]{1,0:T(8,128)}) async-done(((f32[384,1152]{1,0:T(8,128)}, f32[384,384]{1,0:T(8,128)}, f32[384,1536]{1,0:T(8,128)}, f32[1536,384]{1,0:T(8,128)}), (f32[384,1152]{1,0:T(8,128)}, f32[384,384]{1,0:T(8,128)}, f32[384,1536]{1,0:T(8,128)}, ...) | async-done | bytes 7077904 | tf_op jit(solution)/shard_map/psum | solution.py:275
  532.3 2.7 pad_maximum_fusion.9
  536.5 39.7 %all-reduce = (f32[4]{0:T(128)S(1)}, f32[4]{0:T(128)S(1)}, f32[2,384]{1,0:T(2,128)S(1)}) all-reduce(f32[4]{0:T(128)S(1)} %pad_maximum_fusion.10, f32[4]{0:T(128)S(1)} %pad_maximum_fusion.9, f32[2,384]{1,0:T(2,128)S(1)} %fusion.200), channel_id=1, replica_groups=mesh['pipe'=2,'dp'=16] {'dp'}, use_global_device_ids=true, to_apply=%region_64.65 | all-reduce | flops 776 | bytes 6208 | tf_op jit(solution)/shard_map/psum | solution.py:297
  (438 shorter events, 157.3 us)
Async XLA Ops:
  7.2 114.3 %all-gather.5.cloned.1.call-start = ((), (), s32[]{:S(2)}) async-start(), calls=%async_computation.1 | async-start | bytes 1253376 | tf_op jit(solution)/shard_map/all_gather | solution.py:210
  8.9 122.2 %all-gather.3.cloned.1.call-start = ((), (), s32[]{:S(2)}) async-start(), calls=%async_computation | async-start | bytes 1253376 | tf_op jit(solution)/shard_map/all_gather | solution.py:211
  10.5 510.0 %all-reduce.4.cloned.1.call-start = ((), (), s32[]{:S(2)}) async-start(), calls=%async_computation.2 | async-start | bytes 14155776 | tf_op jit(solution)/shard_map/psum | solution.py:275
  11.3 126.0 %copy-start.89 = (s32[1,1,512]{2,1,0:T(1,128)}, s32[1,1,512]{2,1,0:T(1,128)S(1)}, u32[]{:S(2)}) copy-start(s32[1,1,512]{2,1,0:T(1,128)S(1)} %get-tuple-element.167) | copy-start | bytes 6148
  16.9 104.0 %copy-start.17 = (bf16[1,1,512,384]{2,3,1,0:T(8,128)(2,1)}, bf16[1,1,512,384]{2,3,1,0:T(8,128)(2,1)S(1)}, u32[]{:S(2)}) copy-start(bf16[1,1,512,384]{2,3,1,0:T(8,128)(2,1)S(1)} %copy.154) | copy-start | bytes 1179652
  17.3 121.6 %copy-start.5 = (bf16[1,1,512,384]{2,3,1,0:T(8,128)(2,1)}, bf16[1,1,512,384]{2,3,1,0:T(8,128)(2,1)S(1)}, u32[]{:S(2)}) copy-start(bf16[1,1,512,384]{2,3,1,0:T(8,128)(2,1)S(1)} %copy.155) | copy-start | bytes 1179652
  135.7 3.3 collective-permute-start
  159.4 7.4 %collective-permute-start.2 = (bf16[512,384]{0,1:T(8,128)(2,1)}, bf16[512,384]{0,1:T(8,128)(2,1)}, u32[]{:S(2)}, u32[]{:S(2)}) collective-permute-start(bf16[512,384]{0,1:T(8,128)(2,1)} %get-tuple-element.188), channel_id=1, source_target_pairs={{0,16},{1,17},{2,18},{3,19},{4,20},{5,21},{6,22},{7,23},{8,24},{9,... | collective-permute-start | bytes 1179656 | tf_op jit(solution)/shard_map/ppermute | solution.py:24
  170.3 37.5 %copy-start = (f32[512,384]{0,1:T(8,128)}, f32[512,384]{0,1:T(8,128)S(1)}, u32[]{:S(2)}) copy-start(f32[512,384]{0,1:T(8,128)S(1)} %get-tuple-element.105) | copy-start | bytes 2359300
  226.1 10.6 %collective-permute-start.1 = (bf16[512,384]{0,1:T(8,128)(2,1)S(1)}, bf16[512,384]{0,1:T(8,128)(2,1)S(1)}, u32[]{:S(2)}, u32[]{:S(2)}) collective-permute-start(bf16[512,384]{0,1:T(8,128)(2,1)S(1)} %add_convert_fusion), channel_id=1, source_target_pairs={{16,0},{17,1},{18,2},{19,3},{20,4},{21,5},{22,6},{23,7},{24,8},{25... | collective-permute-start | bytes 1179656 | tf_op jit(solution)/shard_map/ppermute | solution.py:24
  261.6 6.9 %collective-permute-start.3 = (bf16[512,384]{0,1:T(8,128)(2,1)S(1)}, bf16[512,384]{0,1:T(8,128)(2,1)S(1)}, u32[]{:S(2)}, u32[]{:S(2)}) collective-permute-start(bf16[512,384]{0,1:T(8,128)(2,1)S(1)} %get-tuple-element.101), channel_id=1, source_target_pairs={{16,0},{17,1},{18,2},{19,3},{20,4},{21,5},{22,6},{23,7},{24,8},{25... | collective-permute-start | bytes 1179656 | tf_op jit(solution)/shard_map/ppermute | solution.py:24
  318.8 201.7 %copy-start.66 = (f32[1,24,1152]{2,1,0:T(8,128)S(1)}, f32[1,24,1152]{2,1,0:T(8,128)}, u32[]{:S(2)}) copy-start(f32[1,24,1152]{2,1,0:T(8,128)} %param.23) | copy-start | bytes 331780
  318.8 204.1 %copy-start.64 = (f32[1,24,1536]{2,1,0:T(8,128)S(1)}, f32[1,24,1536]{2,1,0:T(8,128)}, u32[]{:S(2)}) copy-start(f32[1,24,1536]{2,1,0:T(8,128)} %param.25) | copy-start | bytes 442372
  318.8 204.1 %copy-start.77 = (f32[1,24,1536]{2,1,0:T(8,128)S(1)}, f32[1,24,1536]{2,1,0:T(8,128)}, u32[]{:S(2)}) copy-start(f32[1,24,1536]{2,1,0:T(8,128)} %param.33) | copy-start | bytes 442372
  318.8 204.1 %copy-start.78 = (f32[1,24,1536]{2,1,0:T(8,128)S(1)}, f32[1,24,1536]{2,1,0:T(8,128)}, u32[]{:S(2)}) copy-start(f32[1,24,1536]{2,1,0:T(8,128)} %param.29) | copy-start | bytes 442372
  318.8 206.5 %copy-start.75 = (f32[1,24,384]{2,1,0:T(8,128)S(1)}, f32[1,24,384]{2,1,0:T(8,128)}, u32[]{:S(2)}) copy-start(f32[1,24,384]{2,1,0:T(8,128)} %param.24) | copy-start | bytes 110596
  318.8 206.5 %copy-start.83 = (f32[1,24,384]{2,1,0:T(8,128)S(1)}, f32[1,24,384]{2,1,0:T(8,128)}, u32[]{:S(2)}) copy-start(f32[1,24,384]{2,1,0:T(8,128)} %param.32) | copy-start | bytes 110596
  318.8 206.4 %copy-start.84 = (f32[1,24,384]{2,1,0:T(8,128)S(1)}, f32[1,24,384]{2,1,0:T(8,128)}, u32[]{:S(2)}) copy-start(f32[1,24,384]{2,1,0:T(8,128)} %param.28) | copy-start | bytes 110596
  318.8 208.5 %copy-start.63 = (f32[1,96,384]{2,1,0:T(8,128)S(1)}, f32[1,96,384]{2,1,0:T(8,128)}, u32[]{:S(2)}) copy-start(f32[1,96,384]{2,1,0:T(8,128)} %param.26) | copy-start | bytes 442372
  318.8 208.4 %copy-start.79 = (f32[1,96,384]{2,1,0:T(8,128)S(1)}, f32[1,96,384]{2,1,0:T(8,128)}, u32[]{:S(2)}) copy-start(f32[1,96,384]{2,1,0:T(8,128)} %param.34) | copy-start | bytes 442372
  318.8 208.4 %copy-start.80 = (f32[1,96,384]{2,1,0:T(8,128)S(1)}, f32[1,96,384]{2,1,0:T(8,128)}, u32[]{:S(2)}) copy-start(f32[1,96,384]{2,1,0:T(8,128)} %param.30) | copy-start | bytes 442372
  520.5 59.0 %copy-start.91 = (f32[1,2,384]{2,1,0:T(2,128)S(1)}, f32[1,2,384]{2,1,0:T(2,128)}, u32[]{:S(2)}) copy-start(f32[1,2,384]{2,1,0:T(2,128)} %param.35) | copy-start | bytes 9220
  520.5 59.0 %copy-start.106 = (f32[1,2,384]{2,1,0:T(2,128)S(1)}, f32[1,2,384]{2,1,0:T(2,128)}, u32[]{:S(2)}) copy-start(f32[1,2,384]{2,1,0:T(2,128)} %param.37) | copy-start | bytes 9220
  520.5 59.0 %copy-start.107 = (f32[1,2,384]{2,1,0:T(2,128)S(1)}, f32[1,2,384]{2,1,0:T(2,128)}, u32[]{:S(2)}) copy-start(f32[1,2,384]{2,1,0:T(2,128)} %param.36) | copy-start | bytes 9220
  (103 other events, 346.8 us)
Sparse Core Ops, SparseCore 0:
  11.4 61.4 all-gather.4
  76.3 54.7 all-gather.2
  291.8 228.6 all-reduce.3
where the time goes:
time: 599 us; the launch traced here: 591 us
  waiting for transfers between devices  210 us (35%)
  matrix products  133 us (22%)
  blocking collectives  128 us (21%)
  other arithmetic  50.9 us (8%)
  local copies, waits for them, and re-layouts  42.9 us (7%)
  between operations  18.3 us (3%)
  starting transfers between devices  7.55 us (1%)
    psum x1, waiting for transfers between devices, per_device(): lax.psum((mat_totals[0], mat_totals[1], mat_totals[2], mat_totals[3], gai...  200 us
    all_gather x1, blocking collectives, per_device(): lax.all_gather(masters[0].astype(jnp.bfloat16), 'dp', axis=0, tiled=True)  50.7 us
    psum x1, blocking collectives, per_device(): update_sums = lax.psum(update_parts, 'dp')  39.7 us
    all_gather x1, blocking collectives, per_device(): lax.all_gather(masters[1].astype(jnp.bfloat16), 'dp', axis=0, tiled=True)  37.9 us
    slice x24, local copies, waits for them, and re-layouts, split_heads(): packed[:, member * D:(member + 1) * D].reshape(length, HEADS, HEAD_DIM)  25.6 us
    sub x3, matrix products, attend(): lifted = jnp.exp(scores - largest)  19.6 us
    dot_general x3, matrix products, block_states(): jnp.dot(active, matrix_down, preferred_element_type=jnp.float32)  15.1 us
    dot_general x6, matrix products, attend(): jnp.einsum('hqk,khd->qhd', chances, value_rows, preferred_element_type=jn...  14.1 us
  transfers between devices with their start and end apart: 7, of which 2 were waited for; matrix products, arithmetic and copies ran while one was open for 12% of the time, Pallas kernels for 0%

commit v1 on v0

v1 whole, which is shorter than its diff:
```python
import jax
import jax.numpy as jnp
from jax import lax
from jax.experimental import pallas as pl
from jax.experimental.pallas import tpu as pltpu
from jax.sharding import PartitionSpec as P

D = 384
FF = 1536
HEADS = 6
HEAD_DIM = 64
STEP = 3
BF = jnp.bfloat16
F32 = jnp.float32

rate = 0.3
beta = 0.5
eps_adam = 1e-06
decay = 0.01
eps_norm = 1e-05
neg_large = -1e30

QB = 128
REACH = 256
ROWS = 64
CHUNK = 256
WIDE = 4 * D
VM = pl.BlockSpec(memory_space=pltpu.VMEM)
SM = pl.BlockSpec(memory_space=pltpu.SMEM)
ANY = pl.BlockSpec(memory_space=pl.ANY)
struct = jax.ShapeDtypeStruct


def dot(a, b, ca=1, cb=0):
    return lax.dot_general(a, b, (((ca,), (cb,)), ((), ())), preferred_element_type=F32)


def bands(length):
    out = []
    off = 0
    for b in range(length // QB):
        ks, ke = max(0, QB * b - REACH), QB * (b + 1)
        out.append((b, ks, ke, off))
        off += ke - ks
    return out, off


def unit_of(x):
    mean = jnp.sum(x, axis=-1, keepdims=True) * (1.0 / D)
    centered = x - mean
    variance = jnp.sum(centered * centered, axis=-1, keepdims=True) * (1.0 / D)
    inverse = lax.rsqrt(variance + eps_norm)
    return centered * inverse, inverse


def norm_into(x_ref, gain, n_ref):
    for r in range(0, x_ref.shape[0], ROWS):
        unit, _ = unit_of(x_ref[r : r + ROWS, :].astype(F32))
        n_ref[r : r + ROWS, :] = (unit * gain).astype(BF)


def norm_back(dn_ref, x_ref, dy_ref, gain, out_ref, low_ref):
    grad = jnp.zeros((1, D), F32)
    for r in range(0, x_ref.shape[0], ROWS):
        unit, inverse = unit_of(x_ref[r : r + ROWS, :].astype(F32))
        dn = dn_ref[r : r + ROWS, :]
        grad = grad + jnp.sum(dn * unit, axis=0, keepdims=True)
        e = dn * gain
        first = jnp.sum(e, axis=-1, keepdims=True) * (1.0 / D)
        cross = jnp.sum(e * unit, axis=-1, keepdims=True) * (1.0 / D)
        total = dy_ref[r : r + ROWS, :].astype(F32) + (e - first - unit * cross) * inverse
        if out_ref is not None:
            out_ref[r : r + ROWS, :] = total
        if low_ref is not None:
            low_ref[r : r + ROWS, :] = total.astype(BF)
    return grad


def make_bias(segc_ref, segr_ref, bias_ref, length):
    for b, ks, ke, off in bands(length)[0]:
        row = segr_ref[:, QB * b : QB * b + QB]
        for k in range(ks, ke, QB):
            allowed = segc_ref[k : k + QB, :] == row
            if k == QB * b:
                keys = lax.broadcasted_iota(jnp.int32, (QB, QB), 0)
                allowed = allowed & (keys <= lax.broadcasted_iota(jnp.int32, (QB, QB), 1))
            bias_ref[off + k - ks : off + k - ks + QB, :] = jnp.where(allowed, 0.0, neg_large)


def head_masked(pair_of, scale, dst_ref):
    lane = lax.broadcasted_iota(jnp.int32, (1, 2 * HEAD_DIM), 1)
    for p in range(HEADS // 2):
        pair = pair_of(p)
        for member in (0, 1):
            mask = jnp.where(lane // HEAD_DIM == member, scale, 0.0).astype(BF)
            dst_ref[2 * p + member] = pair * mask


class Weights:
    def __init__(self, wide, up, down):
        self.wide, self.up_ref, self.down = wide, up, down

    def cols(self, ref, lo, n):
        return ref[:, :, lo : lo + n].reshape(D, n)

    def inn(self, lo=0, n=3 * D):
        return self.cols(self.wide, lo, n)

    def out(self):
        return self.cols(self.wide, 3 * D, D)

    def up(self, lo=0, n=FF):
        return self.cols(self.up_ref, lo, n)


def forward(x_ref, segc, segr, w, ready, g_ref, k, out):
    length = x_ref.shape[0]
    norm_into(x_ref, g_ref[0:1, :], k["n1"])
    make_bias(segc, segr, k["bias"], length)
    ready(0)
    pk, pt = k["pk"], k["pt"]
    for c in range(0, 3 * D, D):
        pk[:, c : c + D] = dot(k["n1"][...], w.inn(c, D)).astype(BF)
    k["vT"][...] = pk[:, 2 * D :].T
    head_masked(lambda p: pk[:, 128 * p : 128 * p + 128], HEAD_DIM ** (-0.5), k["qm"])
    for b, ks, ke, off in bands(length)[0]:
        for h in range(HEADS):
            lo = D + 128 * (h // 2)
            st = dot(pk[ks:ke, lo : lo + 128], k["qm"][h, QB * b : QB * b + QB, :], 1, 1)
            st = st + k["bias"][off : off + ke - ks, :]
            lifted = jnp.exp(st - jnp.max(st, axis=0, keepdims=True))
            pb = (lifted * (1.0 / jnp.sum(lifted, axis=0, keepdims=True))).astype(BF)
            pt[h, off : off + ke - ks, :] = pb
            rows = slice(HEAD_DIM * h, HEAD_DIM * h + HEAD_DIM)
            k["attT"][rows, QB * b : QB * b + QB] = dot(k["vT"][rows, ks:ke], pb).astype(BF)
    mid = k["mid"]
    mid[...] = x_ref[...].astype(F32) + dot(k["attT"][...], w.out(), 0, 0)
    norm_into(mid, g_ref[1:2, :], k["n2"])
    ready(1)
    c0 = 0.7978845608028654
    c1 = 0.044715
    hs = k["hs"]
    for i, c in enumerate(range(0, FF, CHUNK)):
        hs[i % 2] = dot(k["n2"][...], w.up(c, CHUNK))
        for r in range(0, length, ROWS):
            v = hs[i % 2, r : r + ROWS, :]
            v2 = v * v
            th = jnp.tanh(v * (c0 + (c0 * c1) * v2))
            half = 0.5 * v
            k["act"][r : r + ROWS, c : c + CHUNK] = (half + half * th).astype(BF)
            slope = 0.5 + 0.5 * th + half * (1.0 - th * th) * (c0 + (3.0 * c0 * c1) * v2)
            k["gp"][r : r + ROWS, c : c + CHUNK] = slope.astype(BF)
    ready(2)
    out(mid[...] + dot(k["act"][...], w.down[...]))


def backward(x_ref, dy_ref, w, ready, g_ref, k, s, emit, dx, dx_low, gg):
    act, n2, pk, pt = k["act"], k["n2"], k["pk"], k["pt"]
    length = x_ref.shape[0]
    dyb = dy_ref
    emit.down(lambda lo, n: dot(act[:, lo : lo + n], dyb[...], 0, 0))
    ready(2)
    dh = s["dh"]
    for c in range(0, FF, CHUNK):
        grad = dot(dyb[...], w.down[c : c + CHUNK, :], 1, 1) * k["gp"][:, c : c + CHUNK].astype(F32)
        dh[:, c : c + CHUNK] = grad.astype(BF)
    emit.wide(1, lambda lo, n: dot(n2[...], dh[:, lo : lo + n], 0, 0), 0, FF)
    ready(1)
    s["dn"][...] = dot(dh[...], w.up(), 1, 1)
    dmb = s["dmb"]
    gg[1:2, :] = norm_back(s["dn"], k["mid"], dy_ref, g_ref[1:2, :], s["dmid"], dmb)
    emit.wide(0, lambda lo, n: dot(k["attT"][...], dmb[:, lo : lo + n]), 3 * D, D)
    ready(0)
    da = s["da"]
    da[...] = dot(dmb[...], w.out(), 1, 1).astype(BF)
    head_masked(lambda p: da[:, 128 * p : 128 * p + 128], 1.0, s["dam"])
    s["kT"][...] = pk[:, D : 2 * D].T
    dk, dv = s["dk"], s["dv"]
    for p in range(HEADS // 2):
        lo = 128 * p
        for b, ks, ke, off in bands(length)[0]:
            qs = slice(QB * b, QB * b + QB)
            gk = gv = None
            for h in (2 * p, 2 * p + 1):
                rows = slice(HEAD_DIM * h, HEAD_DIM * h + HEAD_DIM)
                dp = dot(pk[ks:ke, 2 * D + lo : 2 * D + lo + 128], s["dam"][h, qs, :], 1, 1)
                pb = pt[h, off : off + ke - ks, :]
                pf = pb.astype(F32)
                inner = jnp.sum(pf * dp, axis=0, keepdims=True)
                ds = (pf * (dp - inner)).astype(BF)
                s["dqT"][rows, qs] = dot(s["kT"][rows, ks:ke], ds) * HEAD_DIM ** (-0.5)
                one, two = dot(ds, k["qm"][h, qs, :]), dot(pb, s["dam"][h, qs, :])
                gk, gv = (one, two) if gk is None else (gk + one, gv + two)
            n = ke - ks - QB
            if n:
                dk[ks : ks + n, lo : lo + 128] += gk[:n]
                dv[ks : ks + n, lo : lo + 128] += gv[:n]
            dk[ks + n : ke, lo : lo + 128] = gk[n:]
            dv[ks + n : ke, lo : lo + 128] = gv[n:]
    dpk = s["dpk"]
    dpk[:, 0:D] = s["dqT"][...].T.astype(BF)
    dpk[:, D : 2 * D] = dk[...].astype(BF)
    dpk[:, 2 * D :] = dv[...].astype(BF)
    emit.wide(0, lambda lo, n: dot(k["n1"][...], dpk[:, lo : lo + n], 0, 0), 0, 3 * D)
    s["dn"][...] = dot(dpk[...], w.inn(), 1, 1)
    gg[0:1, :] = norm_back(s["dn"], x_ref, s["dmid"], g_ref[0:1, :], dx, dx_low)


def kept_shapes(L):
    nb = bands(L)[1]
    return dict(
        n1=((L, D), BF),
        pk=((L, 3 * D), BF),
        pt=((HEADS, nb, QB), BF),
        attT=((D, L), BF),
        mid=((L, D), F32),
        n2=((L, D), BF),
        act=((L, FF), BF),
        gp=((L, FF), BF),
        qm=((HEADS, L, 2 * HEAD_DIM), BF),
    )


def forward_scratch(L):
    nb = bands(L)[1]
    return dict(vT=((D, L), BF), bias=((nb, QB), F32), hs=((2, L, CHUNK), F32))


def backward_scratch(L):
    return dict(
        dh=((L, FF), BF),
        dn=((L, D), F32),
        dmid=((L, D), F32),
        dmb=((L, D), BF),
        dam=((HEADS, L, 2 * HEAD_DIM), BF),
        kT=((D, L), BF),
        dqT=((D, L), F32),
        dk=((L, D), F32),
        dv=((L, D), F32),
        dpk=((L, 3 * D), BF),
        da=((L, D), BF),
    )


def weight_scratch(plan):
    wide = (plan.slabs, D // plan.slabs, WIDE)
    return dict(wide=(wide, BF), up=(wide, BF), down=((FF, D), BF))


def vmem(shapes):
    return [pltpu.VMEM(shape, dtype) for shape, dtype in shapes.values()]


class Plan:
    def __init__(self, mesh):
        self.count = mesh.shape["dp"]
        self.bits = self.count.bit_length() - 1
        n = self.bits
        falling = list(reversed(range(n)))
        swapped = falling[:-2] + [falling[-1], falling[-2]]
        mixed = [0, n - 1] + list(range(1, n - 1))
        self.gather_orders = (falling, swapped, mixed)
        self.scatter_orders = tuple(tuple(reversed(o)) for o in self.gather_orders)
        self.slabs = self.count if (D // self.count) % 8 == 0 else 1

    def tables(self):
        me = lax.axis_index("dp")
        far = jnp.arange(self.count, dtype=jnp.int32) ^ me
        out = []
        for orders, rising in ((self.gather_orders, True), (self.scatter_orders, False)):
            for order in orders:
                place = jnp.zeros_like(far)
                for k, bit in enumerate(order):
                    shift = k if rising else self.bits - 1 - k
                    place = place | (((far >> bit) & 1) << shift)
                out.append(place)
        return out


def load_weights(plan, meta, own, got, dst, sems, block):
    core = meta[0]

    def start(src):
        for f in range(3):
            if plan.slabs == 1:
                pltpu.make_async_copy(src[f], dst[f], sems.at[f]).start()
                continue
            for s in range(plan.slabs):
                rows = FF // plan.slabs
                to = dst[f].at[s] if f < 2 else dst[f].at[rows * s : rows * s + rows, :]
                pltpu.make_async_copy(src[f].at[meta[1 + f * plan.count + s]], to, sems.at[f]).start()

    @pl.when(core == block)
    def _():
        start(own)

    @pl.when(core != block)
    def _():
        start(got)

    done = set()

    def ready(f):
        if f not in done:
            done.add(f)
            pltpu.make_async_copy(dst[f], dst[f], sems.at[f]).wait()

    return ready


class Emit:
    def __init__(self, plan, meta, wide, up, down):
        self.plan, self.meta, self.flows, self.down_ref = plan, meta, (wide, up), down

    def place(self, f, s):
        return self.meta[1 + (3 + f) * self.plan.count + s]

    def wide(self, f, make, base, width):
        ref, n, half = self.flows[f], self.plan.slabs, WIDE // 2
        step = D
        for lo in range(0, width, step):
            value = make(lo, step)
            if n == 1:
                ref[0, :, base + lo : base + lo + step] = value.astype(BF)
                continue
            value = value.reshape(n, D // n, step).astype(BF)
            h, at = (base + lo) // half, (base + lo) % half
            for s in range(n):
                ref[h ^ self.meta[0], self.place(f, s), :, at : at + step] = value[s]

    def down(self, make):
        ref, n = self.down_ref, self.plan.slabs
        step = D
        for lo in range(0, FF, step):
            value = make(lo, step)
            if n == 1:
                ref[0, lo : lo + step, :] = value.astype(BF)
                continue
            rows = FF // n // 2
            value = value.reshape(step // rows, rows, D).astype(BF)
            for i in range(step // rows):
                s, h = divmod(lo // rows + i, 2)
                ref[h ^ self.meta[0], self.place(2, s), :, :] = value[i]


def grad_shapes(plan):
    if plan.slabs == 1:
        return [struct((1, D, WIDE), BF), struct((1, D, WIDE), BF), struct((1, FF, D), BF)]
    n = plan.slabs
    wide = struct((2, n, D // n, WIDE // 2), BF)
    return [wide, wide, struct((2, n, FF // n // 2, D), BF)]


def params(mb=56):
    return pltpu.CompilerParams(vmem_limit_bytes=mb * 2**20)


def extractor_forward(plan, meta, x, segc, segr, prompts, gains, own, got):
    L = x.shape[0]
    kept, fs, ws = kept_shapes(L), forward_scratch(L), weight_scratch(plan)

    def kernel(meta, x, segc, segr, pr, g, *refs):
        own, got = refs[0:3], refs[3:6]
        x1 = refs[6]
        k = dict(zip(kept, refs[7:]))
        rest = refs[7 + len(kept) :]
        k.update(zip(fs, rest))
        dst, sems = rest[len(fs) : len(fs) + 3], rest[-1]
        ready = load_weights(plan, meta, own, got, dst, sems, 0)

        def out(value):
            x1[...] = value.astype(BF).astype(F32) + pr[...].astype(F32)

        forward(x, segc, segr, Weights(*dst), ready, g, k, out)

    outs = [struct((L, D), F32)] + [struct(*v) for v in kept.values()]
    res = pl.pallas_call(
        kernel,
        name="extractor_forward",
        out_shape=outs,
        in_specs=[SM] + [VM] * 5 + [ANY] * 6,
        out_specs=[VM] * len(outs),
        scratch_shapes=vmem(fs) + vmem(ws) + [pltpu.SemaphoreType.DMA((3,))],
        compiler_params=params(),
    )(meta, x, segc, segr, prompts, gains, *own, *got)
    return res[0], res[1:]


def generator_step(plan, meta, x, segc, segr, cot, gains, own, got):
    L = x.shape[0]
    kept, fs, bs, ws = kept_shapes(L), forward_scratch(L), backward_scratch(L), weight_scratch(plan)

    def kernel(meta, x, segc, segr, cot, g, *refs):
        own, got = refs[0:3], refs[3:6]
        y2, dx, gw, gu, gd, gg = refs[6:12]
        rest = refs[12:]
        k = dict(zip(kept, rest))
        rest = rest[len(kept) :]
        k.update(zip(fs, rest))
        rest = rest[len(fs) :]
        s = dict(zip(bs, rest))
        rest = rest[len(bs) :]
        dst, sems = rest[:3], rest[3]
        ready = load_weights(plan, meta, own, got, dst, sems, 1)

        def out(value):
            y2[...] = value

        w = Weights(*dst)
        forward(x, segc, segr, w, ready, g, k, out)
        backward(x, cot, w, ready, g, k, s, Emit(plan, meta, gw, gu, gd), None, dx, gg)

    return pl.pallas_call(
        kernel,
        name="generator_step",
        out_shape=[struct((L, D), F32), struct((L, D), BF)] + grad_shapes(plan) + [struct((2, D), F32)],
        in_specs=[SM] + [VM] * 5 + [ANY] * 6,
        out_specs=[VM] * 6,
        scratch_shapes=vmem(kept) + vmem(fs) + vmem(bs) + vmem(ws) + [pltpu.SemaphoreType.DMA((3,))],
        compiler_params=params(),
    )(meta, x, segc, segr, cot, gains, *own, *got)


def extractor_backward(plan, meta, x, dy, gains, own, got, kept_values):
    L = x.shape[0]
    kept, bs, ws = kept_shapes(L), backward_scratch(L), weight_scratch(plan)

    def kernel(meta, x, dy, g, *refs):
        own, got = refs[0:3], refs[3:6]
        k = dict(zip(kept, refs[6:]))
        rest = refs[6 + len(kept) :]
        dx, gw, gu, gd, gg = rest[:5]
        rest = rest[5:]
        s = dict(zip(bs, rest))
        rest = rest[len(bs) :]
        dst, sems = rest[:3], rest[3]
        ready = load_weights(plan, meta, own, got, dst, sems, 0)
        backward(x, dy, Weights(*dst), ready, g, k, s, Emit(plan, meta, gw, gu, gd), dx, None, gg)

    return pl.pallas_call(
        kernel,
        name="extractor_backward",
        out_shape=[struct((L, D), F32)] + grad_shapes(plan) + [struct((2, D), F32)],
        in_specs=[SM] + [VM] * 3 + [ANY] * 6 + [VM] * len(kept),
        out_specs=[VM] * 5,
        scratch_shapes=vmem(bs) + vmem(ws) + [pltpu.SemaphoreType.DMA((3,))],
        compiler_params=params(),
    )(meta, x, dy, gains, *own, *got, *kept_values)


def swap_cores(block):
    return lax.ppermute(block, "pipe", [(0, 1), (1, 0)])


def swap(block, bit):
    return lax.ppermute(block, "dp", [(i, i ^ (1 << bit)) for i in range(lax.axis_size("dp"))])


def gather(plan, shards):
    held = [shard[None] for shard in shards]
    for turn in range(plan.bits):
        came = [swap(held[f], plan.gather_orders[f][turn]) for f in range(3)]
        held = [jnp.concatenate([a, b], 0) for a, b in zip(held, came)]
    return held


def scatter(plan, grads):
    sums = [mine.astype(F32) + other.astype(F32) for mine, other in ((g[0], swap_cores(g[1])) for g in grads)]
    sums = [v.astype(BF) for v in sums]
    for turn in range(plan.bits):
        half = sums[0].shape[0] // 2
        came = [swap(sums[f][half:], plan.scatter_orders[f][turn]) for f in range(3)]
        sums = [(v[:half].astype(F32) + c.astype(F32)).astype(BF) for v, c in zip(sums, came)]
    return [v[0] for v in sums]


def placed_gather(plan, tables, flows):
    if plan.slabs > 1:
        return flows
    return [jnp.take(v, tables[f], axis=0).reshape((1, -1, v.shape[-1]) if f < 2 else (-1, v.shape[-1])) for f, v in enumerate(flows)]


def placed_scatter(plan, tables, core, grads):
    if plan.slabs > 1:
        return grads
    out = []
    for f, v in enumerate(grads):
        v = v.reshape(plan.count, -1, v.shape[-1])
        v = jnp.zeros_like(v).at[tables[3 + f]].set(v)
        axis = 2 if f < 2 else 1
        half = v.shape[axis] // 2
        out.append([lax.dynamic_slice_in_dim(v, c * half, half, axis) for c in (core, 1 - core)])
    return out


def moments(master, grad, first, second):
    drift = beta * first + (1.0 - beta) * grad
    spread = beta * second + (1.0 - beta) * grad * grad
    correction = 1.0 - beta**STEP
    update = drift / correction / (jnp.sqrt(spread / correction) + eps_adam) + decay * master
    return (drift, spread, update)


def solution(mesh):
    plan = Plan(mesh)

    def per_device(
        tokens,
        prompts,
        cotangent,
        segments,
        weight_in,
        weight_out,
        weight_up,
        weight_down,
        first_in,
        first_out,
        first_up,
        first_down,
        second_in,
        second_out,
        second_up,
        second_down,
        gains,
        gain_first,
        gain_second,
    ):
        core = lax.axis_index("pipe")
        leading = core == 0
        masters = (weight_in[0], weight_out[0], weight_up[0], weight_down[0])
        tables = plan.tables()
        meta = jnp.concatenate([core[None].astype(jnp.int32)] + tables)
        low = [m.astype(BF) for m in masters]
        flows = gather(plan, [jnp.concatenate(low[:2], 1), low[2], low[3]])
        flows = placed_gather(plan, tables, flows)
        got = [swap_cores(v) for v in flows]
        gains_got = swap_cores(gains[0])
        gains_zero = jnp.where(leading, gains[0], gains_got)
        gains_one = jnp.where(leading, gains_got, gains[0])

        def mine(v):
            return lax.dynamic_index_in_dim(v, core, 0, keepdims=False)[0]

        x, pr, cot, seg = mine(tokens), mine(prompts), mine(cotangent), mine(segments)
        segc, segr = seg[:, None], seg[None, :]
        x1, kept = extractor_forward(plan, meta, x, segc, segr, pr, gains_zero, flows, got)
        y2, dx1, *rest = generator_step(plan, meta, x1, segc, segr, cot, gains_one, flows, got)
        grads_one, gg_one = rest[:3], rest[3]
        half_one = scatter(plan, placed_scatter(plan, tables, core, grads_one))
        dx0, *rest = extractor_backward(plan, meta, x, dx1, gains_zero, flows, got, kept)
        grads_zero, gg_zero = rest[:3], rest[3]
        half_zero = scatter(plan, placed_scatter(plan, tables, core, grads_zero))

        result_got = swap_cores(jnp.where(leading, y2, dx0))
        result = jnp.where(leading, jnp.stack([dx0, result_got]), jnp.stack([result_got, y2]))
        section_result = result[None, :, None]
        gain_grad = jnp.where(leading, gg_zero, gg_one) + swap_cores(jnp.where(leading, gg_one, gg_zero))

        half_own = [jnp.where(leading, a, b) for a, b in zip(half_zero, half_one)]
        half_send = [jnp.where(leading, b, a) for a, b in zip(half_zero, half_one)]
        half_got = [swap_cores(v) for v in half_send]
        full = []
        for f, (a, b) in enumerate(zip(half_own, half_got)):
            axis = 1 if f < 2 else 0
            full.append(jnp.where(leading, jnp.concatenate([a, b], axis), jnp.concatenate([b, a], axis)).astype(F32))
        shares = (full[0][:, : 3 * D], full[0][:, 3 * D :], full[1], full[2])

        firsts = (first_in[0], first_out[0], first_up[0], first_down[0])
        seconds = (second_in[0], second_out[0], second_up[0], second_down[0])
        states = [moments(masters[m], shares[m], firsts[m], seconds[m]) for m in range(4)]
        squares = [jnp.sum(m * m) for m in masters] + [jnp.sum(st[2] * st[2]) for st in states]
        small = jnp.concatenate([jnp.pad(jnp.stack(squares), (0, D - 8))[None], gain_grad], 0)
        for bit in range(plan.bits):
            small = small + swap(small, bit)
        weight_norms = jnp.sqrt(small[0, 0:4])
        update_norms = jnp.sqrt(small[0, 4:8])
        trust = weight_norms / update_norms
        updated = [masters[m] - rate * trust[m] * states[m][2] for m in range(4)]
        gain_pair = gains[0]
        gain_drift, gain_spread, gain_update = moments(gain_pair, small[1:3], gain_first[0], gain_second[0])
        gain_weight = jnp.sqrt(jnp.sum(gain_pair * gain_pair, axis=-1))
        gain_step = jnp.sqrt(jnp.sum(gain_update * gain_update, axis=-1))
        gain_new = gain_pair - rate * (gain_weight / gain_step)[:, None] * gain_update
        norm_pairs = jnp.stack(
            [jnp.concatenate([weight_norms, gain_weight]), jnp.concatenate([update_norms, gain_step])],
            axis=-1,
        )
        return (
            section_result,
            *[st[0][None] for st in states],
            *[st[1][None] for st in states],
            *[u[None] for u in updated],
            *[u.astype(BF)[None] for u in updated],
            gain_drift[None],
            gain_spread[None],
            gain_new[None],
            norm_pairs[None],
        )

    rows = P(None, "dp", None, None)
    matrix = P("pipe", "dp", None)
    gain = P("pipe", None, None)
    in_specs = (rows, rows, rows, P(None, "dp", None)) + (matrix,) * 12 + (gain,) * 3
    out_specs = (P("pipe", None, "dp", None, None),) + (matrix,) * 16 + (gain,) * 4
    return jax.shard_map(
        per_device, mesh=mesh, in_specs=in_specs, out_specs=out_specs, check_vma=False
    )
```

time: 599 us -> 220 us (0.37)
  waiting for transfers between devices: 210 us -> 49.5 us
  matrix products: 133 us -> 0 us
  blocking collectives: 128 us -> 0 us
  Pallas kernels: 0 us -> 67.2 us
  starting transfers between devices: 7.55 us -> 56.1 us
  other arithmetic: 50.9 us -> 21.8 us
  local copies, waits for them, and re-layouts: 42.9 us -> 18.4 us
  between operations: 18.3 us -> 4.42 us
    psum x1 -> x0, waiting for transfers between devices: 200 us -> none  [per_device(): lax.psum((mat_totals[0], mat_totals[1], mat_totals[2], mat_totals[3], gai...]
    dot_general x63 -> x0, matrix products: 114 us -> none  [the longest x3 15.1 us: block_states(): jnp.dot(active, matrix_down, preferred_element_type=jnp.float32)]
    all_gather x2 -> x0, blocking collectives: 88.6 us -> none  [the longest x1 50.7 us: per_device(): lax.all_gather(masters[0].astype(jnp.bfloat16), 'dp', axis=0, tiled=True)]
    pallas_call x0 -> x3, Pallas kernels: none -> 67.2 us  [the longest x1 35.2 us: generator_step(): pl.pallas_call(kernel, name='generator_step', out_shape=[struct((L, D), F...]
    ppermute x4 -> x55, waiting for transfers between devices: 0.01 us -> 49.5 us  [the longest x40 48.3 us: swap(): lax.ppermute(block, 'dp', [(i, i ^ 1 << bit) for i in range(lax.axis_size...]
    ppermute x4 -> x55, starting transfers between devices: 7.43 us -> 56.1 us  [the longest x40 51.8 us: swap(): lax.ppermute(block, 'dp', [(i, i ^ 1 << bit) for i in range(lax.axis_size...]
    psum x1 -> x0, blocking collectives: 39.7 us -> none  [per_device(): update_sums = lax.psum(update_parts, 'dp')]
    slice x30 -> x25, local copies, waits for them, and re-layouts: 30.1 us -> 0.92 us  [the longest x1 0.61 us: per_device(): updated = [masters[m] - rate * trust[m] * states[m][2] for m in range(4)]]
  transfers between devices with their start and end apart: 7 -> 55, of which waited for: 2 -> 21; matrix products, arithmetic and copies ran while one was open for 12% -> 14% of each run, Pallas kernels for 0% -> 8%
where the time goes in v1:
time: 220 us; the launch traced here: 217 us
  Pallas kernels  67.2 us (31%)
  starting transfers between devices  56.1 us (26%)
  waiting for transfers between devices  49.5 us (22%)
  other arithmetic  21.8 us (10%)
  local copies, waits for them, and re-layouts  18.4 us (8%)
  between operations  4.42 us (2%)
    ppermute x40, starting transfers between devices, swap(): lax.ppermute(block, 'dp', [(i, i ^ 1 << bit) for i in range(lax.axis_size...  51.8 us
    ppermute x40, waiting for transfers between devices, swap(): lax.ppermute(block, 'dp', [(i, i ^ 1 << bit) for i in range(lax.axis_size...  48.3 us
    pallas_call x1, Pallas kernels, generator_step(): pl.pallas_call(kernel, name='generator_step', out_shape=[struct((L, D), F...  35.2 us
    pallas_call x1, Pallas kernels, extractor_backward(): pl.pallas_call(kernel, name='extractor_backward', out_shape=[struct((L, D...  17.3 us
    pallas_call x1, Pallas kernels, extractor_forward(): pl.pallas_call(kernel, name='extractor_forward', out_shape=outs, in_specs...  14.7 us
    another operation x1, local copies, waits for them, and re-layouts, per_device(): jnp.stack(squares)  5.26 us
  transfers between devices with their start and end apart: 55, of which 21 were waited for; matrix products, arithmetic and copies ran while one was open for 14% of the time, Pallas kernels for 8%

profile of v1, /device:TPU:0, one launch (start us, length us, event | category | flops | bytes accessed | tf_op | source)
XLA Modules:
  0.0 217.5 jit_solution(2638795637383477137)
XLA Ops:
  2.4 4.1 %collective-permute-start.1 = (bf16[1,24,1536]{2,1,0:T(8,128)(2,1)S(1)}, bf16[1,24,1536]{2,1,0:T(8,128)(2,1)S(1)}, u32[]{:S(2)}, u32[]{:S(2)}) collective-permute-start(bf16[1,24,1536]{2,1,0:T(8,128)(2,1)S(1)} %maximum_bitcast_fusion), channel_id=1, source_target_pairs={{0,8},{1,9},{2,10},{3,11},{4,12},{5,13},{6,14},{7,15},{8,0},{9,1},... | collective-permute-start | bytes 221192 | tf_op jit(solution)/shard_map/ppermute | solution.py:456
  12.7 2.7 %collective-permute-start.10 = (bf16[2,96,384]{2,1,0:T(8,128)(2,1)S(1)}, bf16[2,96,384]{2,1,0:T(8,128)(2,1)S(1)}, u32[]{:S(2)}, u32[]{:S(2)}) collective-permute-start(bf16[2,96,384]{2,1,0:T(8,128)(2,1)S(1)} %pad_maximum_fusion.8), channel_id=1, source_target_pairs={{0,8},{1,9},{2,10},{3,11},{4,12},{5,13},{6,14},{7,15},{8,0},{9,1},... | collective-permute-start | bytes 442376 | tf_op jit(solution)/shard_map/ppermute | solution.py:456
  18.3 3.4 %collective-permute-done.2 = bf16[2,24,1536]{2,1,0:T(8,128)(2,1)S(1)} collective-permute-done((bf16[2,24,1536]{2,1,0:T(8,128)(2,1)S(1)}, bf16[2,24,1536]{2,1,0:T(8,128)(2,1)S(1)}, u32[]{:S(2)}, u32[]{:S(2)}) %collective-permute-start.2) | collective-permute-done | bytes 147488 | tf_op jit(solution)/shard_map/ppermute | solution.py:456
  25.2 4.2 %collective-permute-done.3 = bf16[4,24,1536]{2,1,0:T(8,128)(2,1)S(1)} collective-permute-done((bf16[4,24,1536]{2,1,0:T(8,128)(2,1)S(1)}, bf16[4,24,1536]{2,1,0:T(8,128)(2,1)S(1)}, u32[]{:S(2)}, u32[]{:S(2)}) %collective-permute-start.3) | collective-permute-done | bytes 294944 | tf_op jit(solution)/shard_map/ppermute | solution.py:456
  29.5 3.5 %collective-permute-done.11 = bf16[4,96,384]{2,1,0:T(8,128)(2,1)S(1)} collective-permute-done((bf16[4,96,384]{2,1,0:T(8,128)(2,1)S(1)}, bf16[4,96,384]{2,1,0:T(8,128)(2,1)S(1)}, u32[]{:S(2)}, u32[]{:S(2)}) %collective-permute-start.11) | collective-permute-done | bytes 294944 | tf_op jit(solution)/shard_map/ppermute | solution.py:456
  36.5 7.7 %collective-permute-done.4 = bf16[8,24,1536]{2,1,0:T(8,128)(2,1)S(1)} collective-permute-done((bf16[8,24,1536]{2,1,0:T(8,128)(2,1)S(1)}, bf16[8,24,1536]{2,1,0:T(8,128)(2,1)S(1)}, u32[]{:S(2)}, u32[]{:S(2)}) %collective-permute-start.4) | collective-permute-done | bytes 589856 | tf_op jit(solution)/shard_map/ppermute | solution.py:456
  49.2 2.0 dynamic-slice_bitcast_fusion
  53.9 14.7 %extractor_forward.1 = (f32[512,384]{1,0:T(8,128)}, bf16[512,384]{1,0:T(8,128)(2,1)}, bf16[512,1152]{1,0:T(8,128)(2,1)}, bf16[6,1152,128]{2,1,0:T(8,128)(2,1)}, ...) custom-call(s32[97]{0:T(128)} %concatenate.156.meta, ...), custom_call_target="tpu_custom_call" | custom-call | tf_op jit(solution)/shard_map/extractor_forward/pallas_call | solution.py:377
  68.6 35.2 %generator_step.1 = (f32[512,384]{1,0:T(8,128)}, bf16[512,384]{1,0:T(8,128)(2,1)}, bf16[2,16,24,768]{3,2,1,0:T(8,128)(2,1)}, bf16[2,16,24,768]{3,2,1,0:T(8,128)(...) custom-call(s32[97]{0:T(128)} %concatenate.156.meta, f32[512,384]{1,0:T(8,128)} %get-tuple-element.42.x, ...), custom_call_target="tpu_custom_call" | custom-call | tf_op jit(solution)/shard_map/generator_step/pallas_call | solution.py:413
  105.1 17.3 %extractor_backward.1 = (f32[512,384]{1,0:T(8,128)}, bf16[2,16,24,768]{3,2,1,0:T(8,128)(2,1)}, bf16[2,16,24,768]{3,2,1,0:T(8,128)(2,1)}, bf16[2,16,48,384]{3,2,1,0:T(8,128)(2,1)}, f32[2,384]{1,0:T(2,128)}) custom-call(s32[97]{0:T(128)} %concatenate.156.meta, bf16[512,384]{1,0:T(8,128)(2,1)} %dynamic-slice_bitcast_fusion.2.x, ...), custom_call_target="tpu_custom_call" | custom-call | tf_op jit(solution)/shard_map/extractor_backward/pallas_call | solution.py:440
  134.7 4.8 %collective-permute-done.45 = bf16[8,48,384]{2,1,0:T(8,128)(2,1)S(1)} collective-permute-done((bf16[8,48,384]{2,1,0:T(8,128)(2,1)S(1)}, bf16[8,48,384]{2,1,0:T(8,128)(2,1)S(1)}, u32[]{:S(2)}, u32[]{:S(2)}) %collective-permute-start.45) | collective-permute-done | bytes 294944 | tf_op jit(solution)/shard_map/ppermute | solution.py:456
  140.5 4.7 %collective-permute-done.40 = bf16[8,48,384]{2,1,0:T(8,128)(2,1)S(1)} collective-permute-done((bf16[8,48,384]{2,1,0:T(8,128)(2,1)S(1)}, bf16[8,48,384]{2,1,0:T(8,128)(2,1)S(1)}, u32[]{:S(2)}, u32[]{:S(2)}) %collective-permute-start.40) | collective-permute-done | bytes 294944 | tf_op jit(solution)/shard_map/ppermute | solution.py:456
  149.9 5.2 %collective-permute-done.18 = bf16[8,24,768]{2,1,0:T(8,128)(2,1)S(1)} collective-permute-done((bf16[8,24,768]{2,1,0:T(8,128)(2,1)S(1)}, bf16[8,24,768]{2,1,0:T(8,128)(2,1)S(1)}, u32[]{:S(2)}, u32[]{:S(2)}) %collective-permute-start.18) | collective-permute-done | bytes 294944 | tf_op jit(solution)/shard_map/ppermute | solution.py:456
  158.4 4.6 %collective-permute-start.47 = (bf16[2,48,384]{2,1,0:T(8,128)(2,1)S(1)}, bf16[2,48,384]{2,1,0:T(8,128)(2,1)S(1)}, u32[]{:S(2)}, u32[]{:S(2)}) collective-permute-start(bf16[2,48,384]{2,1,0:T(8,128)(2,1)S(1)} %slice.323), channel_id=1, source_target_pairs={{0,8},{1,9},{2,10},{3,11},{4,12},{5,13},{6,14},{7,15},{8,0},{9,1},... | collective-permute-start | bytes 221192 | tf_op jit(solution)/shard_map/ppermute | solution.py:456
  163.1 1.7 collective-permute-start.42
  173.8 2.3 %collective-permute-start.32 = (bf16[1,24,768]{2,1,0:T(8,128)(2,1)S(1)}, bf16[1,24,768]{2,1,0:T(8,128)(2,1)S(1)}, u32[]{:S(2)}, u32[]{:S(2)}) collective-permute-start(bf16[1,24,768]{2,1,0:T(8,128)(2,1)S(1)} %slice.301), channel_id=1, source_target_pairs={{0,8},{1,9},{2,10},{3,11},{4,12},{5,13},{6,14},{7,15},{8,0},{9,1},... | collective-permute-start | bytes 110600 | tf_op jit(solution)/shard_map/ppermute | solution.py:456
  176.9 2.3 %collective-permute-start.21 = (bf16[1,24,768]{2,1,0:T(8,128)(2,1)S(1)}, bf16[1,24,768]{2,1,0:T(8,128)(2,1)S(1)}, u32[]{:S(2)}, u32[]{:S(2)}) collective-permute-start(bf16[1,24,768]{2,1,0:T(8,128)(2,1)S(1)} %slice.283), channel_id=1, source_target_pairs={{0,8},{1,9},{2,10},{3,11},{4,12},{5,13},{6,14},{7,15},{8,0},{9,1},... | collective-permute-start | bytes 110600 | tf_op jit(solution)/shard_map/ppermute | solution.py:456
  179.3 2.3 %collective-permute-done.26 = bf16[1,24,768]{2,1,0:T(8,128)(2,1)S(1)} collective-permute-done((bf16[1,24,768]{2,1,0:T(8,128)(2,1)S(1)}, bf16[1,24,768]{2,1,0:T(8,128)(2,1)S(1)}, u32[]{:S(2)}, u32[]{:S(2)}) %collective-permute-start.26) | collective-permute-done | bytes 36896 | tf_op jit(solution)/shard_map/ppermute | solution.py:456
  187.5 5.3 %stack.65 = f32[8]{0:T(128)S(1)} concatenate(f32[1]{0:T(128)} %bitcast.39, f32[1]{0:T(128)} %bitcast.40, f32[1]{0:T(128)} %bitcast.41, f32[1]{0:T(128)} %bitcast.42, f32[1]{0:T(128)} %bitcast.43, f32[1]{0:T(128)} %bitcast.44, f32[1]{0:T(128)} %bitcast.49, f32[1]{0:T(128)} %bitcast.54), dimensions={0} | concatenate | bytes 64 | tf_op jit(solution)/shard_map/stack | solution.py:572
  194.4 2.0 collective-permute-done.51
  198.0 2.1 collective-permute-done.52
  201.6 2.2 %collective-permute-done.53 = f32[3,384]{1,0:T(4,128)S(1)} collective-permute-done((f32[3,384]{1,0:T(4,128)S(1)}, f32[3,384]{1,0:T(4,128)S(1)}, u32[]{:S(2)}, u32[]{:S(2)}) %collective-permute-start.53) | collective-permute-done | bytes 4640 | tf_op jit(solution)/shard_map/ppermute | solution.py:456
  203.8 2.1 collective-permute-start.54
  206.0 2.7 %maximum_select_fusion = f32[1,2,1,512,384]{4,3,2,1,0:T(8,128)} fusion(f32[1,1,1,512,384]{4,3,2,1,0:T(8,128)} %bitcast.11, f32[1,1,1,512,384]{4,3,2,1,0:T(8,128)S(1)} %bitcast.210, f32[1,1,1,512,384]{4,3,2,1,0:T(8,128)S(1)} %bitcast.209, pred[]{:T(512)S(6)} %eq.3), kind=kLoop, calls=%fused_computation | loop fusion | flops 1179648 | bytes 3932161 | tf_op jit(solution)/shard_map/jit(_where)/select_n | solution.py:555
  (288 shorter events, 73.8 us)
Async XLA Ops:
  2.4 8.6 %collective-permute-start.1 = (bf16[1,24,1536]{2,1,0:T(8,128)(2,1)S(1)}, bf16[1,24,1536]{2,1,0:T(8,128)(2,1)S(1)}, u32[]{:S(2)}, u32[]{:S(2)}) collective-permute-start(bf16[1,24,1536]{2,1,0:T(8,128)(2,1)S(1)} %maximum_bitcast_fusion), channel_id=1, source_target_pairs={{0,8},{1,9},{2,10},{3,11},{4,12},{5,13},{6,14},{7,15},{8,0},{9,1},... | collective-permute-start | bytes 221192 | tf_op jit(solution)/shard_map/ppermute | solution.py:456
  11.0 10.8 %collective-permute-start.2 = (bf16[2,24,1536]{2,1,0:T(8,128)(2,1)S(1)}, bf16[2,24,1536]{2,1,0:T(8,128)(2,1)S(1)}, u32[]{:S(2)}, u32[]{:S(2)}) collective-permute-start(bf16[2,24,1536]{2,1,0:T(8,128)(2,1)S(1)} %pad_maximum_fusion.6), channel_id=1, source_target_pairs={{0,4},{1,5},{2,6},{3,7},{4,0},{5,1},{6,2},{7,3},{8,12},{9,13},{10,... | collective-permute-start | bytes 442376 | tf_op jit(solution)/shard_map/ppermute | solution.py:456
  12.7 10.7 %collective-permute-start.10 = (bf16[2,96,384]{2,1,0:T(8,128)(2,1)S(1)}, bf16[2,96,384]{2,1,0:T(8,128)(2,1)S(1)}, u32[]{:S(2)}, u32[]{:S(2)}) collective-permute-start(bf16[2,96,384]{2,1,0:T(8,128)(2,1)S(1)} %pad_maximum_fusion.8), channel_id=1, source_target_pairs={{0,8},{1,9},{2,10},{3,11},{4,12},{5,13},{6,14},{7,15},{8,0},{9,1},... | collective-permute-start | bytes 442376 | tf_op jit(solution)/shard_map/ppermute | solution.py:456
  23.5 9.5 %collective-permute-start.11 = (bf16[4,96,384]{2,1,0:T(8,128)(2,1)S(1)}, bf16[4,96,384]{2,1,0:T(8,128)(2,1)S(1)}, u32[]{:S(2)}, u32[]{:S(2)}) collective-permute-start(bf16[4,96,384]{2,1,0:T(8,128)(2,1)S(1)} %pad_maximum_fusion.5), channel_id=1, source_target_pairs={{0,2},{1,3},{2,0},{3,1},{4,6},{5,7},{6,4},{7,5},{8,10},{9,11},{10,... | collective-permute-start | bytes 884744 | tf_op jit(solution)/shard_map/ppermute | solution.py:456
  24.1 10.0 %collective-permute-start.7 = (bf16[4,24,1536]{2,1,0:T(8,128)(2,1)S(1)}, bf16[4,24,1536]{2,1,0:T(8,128)(2,1)S(1)}, u32[]{:S(2)}, u32[]{:S(2)}) collective-permute-start(bf16[4,24,1536]{2,1,0:T(8,128)(2,1)S(1)} %pad_maximum_fusion.4), channel_id=1, source_target_pairs={{0,1},{1,0},{2,3},{3,2},{4,5},{5,4},{6,7},{7,6},{8,9},{9,8},{10,11... | collective-permute-start | bytes 884744 | tf_op jit(solution)/shard_map/ppermute | solution.py:456
  29.4 14.9 %collective-permute-start.4 = (bf16[8,24,1536]{2,1,0:T(8,128)(2,1)S(1)}, bf16[8,24,1536]{2,1,0:T(8,128)(2,1)S(1)}, u32[]{:S(2)}, u32[]{:S(2)}) collective-permute-start(bf16[8,24,1536]{2,1,0:T(8,128)(2,1)S(1)} %pad_maximum_fusion), channel_id=1, source_target_pairs={{0,1},{1,0},{2,3},{3,2},{4,5},{5,4},{6,7},{7,6},{8,9},{9,8},{10,11... | collective-permute-start | bytes 1769480 | tf_op jit(solution)/shard_map/ppermute | solution.py:456
  33.0 12.2 %collective-permute-start.12 = (bf16[8,96,384]{2,1,0:T(8,128)(2,1)S(1)}, bf16[8,96,384]{2,1,0:T(8,128)(2,1)S(1)}, u32[]{:S(2)}, u32[]{:S(2)}) collective-permute-start(bf16[8,96,384]{2,1,0:T(8,128)(2,1)S(1)} %pad_maximum_fusion.2), channel_id=1, source_target_pairs={{0,4},{1,5},{2,6},{3,7},{4,0},{5,1},{6,2},{7,3},{8,12},{9,13},{10,... | collective-permute-start | bytes 1769480 | tf_op jit(solution)/shard_map/ppermute | solution.py:456
  34.1 11.7 %collective-permute-start.8 = (bf16[8,24,1536]{2,1,0:T(8,128)(2,1)S(1)}, bf16[8,24,1536]{2,1,0:T(8,128)(2,1)S(1)}, u32[]{:S(2)}, u32[]{:S(2)}) collective-permute-start(bf16[8,24,1536]{2,1,0:T(8,128)(2,1)S(1)} %pad_maximum_fusion.1), channel_id=1, source_target_pairs={{0,2},{1,3},{2,0},{3,1},{4,6},{5,7},{6,4},{7,5},{8,10},{9,11},{10,... | collective-permute-start | bytes 1769480 | tf_op jit(solution)/shard_map/ppermute | solution.py:456
  45.1 8.8 %collective-permute-start.13 = (bf16[16,24,1536]{2,1,0:T(8,128)(2,1)}, bf16[16,24,1536]{2,1,0:T(8,128)(2,1)}, u32[]{:S(2)}, u32[]{:S(2)}) collective-permute-start(bf16[16,24,1536]{2,1,0:T(8,128)(2,1)} %constant_dynamic-update-slice_fusion.refs_0_), channel_id=1, source_target_pairs={{0,16},{16,0},{1,17},{17,1},{2,18},{18,2},{3,19},{19,3},{4,20},{20... | collective-permute-start | bytes 3538952 | tf_op jit(solution)/shard_map/ppermute | solution.py:452
  45.3 8.6 %collective-permute-start.15 = (bf16[16,96,384]{2,1,0:T(8,128)(2,1)S(1)}, bf16[16,96,384]{2,1,0:T(8,128)(2,1)}, u32[]{:S(2)}, u32[]{:S(2)}) collective-permute-start(bf16[16,96,384]{2,1,0:T(8,128)(2,1)S(1)} %constant_dynamic-update-slice_fusion.10.refs_2_), channel_id=1, source_target_pairs={{0,16},{16,0},{1,17},{17,1},{2,18},{18,2},{3,19},{19,3},{4,20},{20... | collective-permute-start | bytes 3538952 | tf_op jit(solution)/shard_map/ppermute | solution.py:452
  104.9 23.7 %collective-permute-start.44 = (bf16[16,48,384]{2,1,0:T(8,128)(2,1)S(1)}, bf16[16,48,384]{2,1,0:T(8,128)(2,1)S(1)}, u32[]{:S(2)}, u32[]{:S(2)}) collective-permute-start(bf16[16,48,384]{2,1,0:T(8,128)(2,1)S(1)} %slice_bitcast_fusion), channel_id=1, source_target_pairs={{0,16},{16,0},{1,17},{17,1},{2,18},{18,2},{3,19},{19,3},{4,20},{20... | collective-permute-start | bytes 1769480 | tf_op jit(solution)/shard_map/ppermute | solution.py:452
  129.1 76.8 %collective-permute-start.16 = (f32[512,384]{1,0:T(8,128)}, f32[512,384]{1,0:T(8,128)}, u32[]{:S(2)}, u32[]{:S(2)}) collective-permute-start(f32[512,384]{1,0:T(8,128)} %broadcast_select_fusion), channel_id=1, source_target_pairs={{0,16},{16,0},{1,17},{17,1},{2,18},{18,2},{3,19},{19,3},{4,20},{20... | collective-permute-start | bytes 2359304 | tf_op jit(solution)/shard_map/ppermute | solution.py:452
  129.6 9.9 %collective-permute-start.45 = (bf16[8,48,384]{2,1,0:T(8,128)(2,1)S(1)}, bf16[8,48,384]{2,1,0:T(8,128)(2,1)S(1)}, u32[]{:S(2)}, u32[]{:S(2)}) collective-permute-start(bf16[8,48,384]{2,1,0:T(8,128)(2,1)S(1)} %slice.319), channel_id=1, source_target_pairs={{0,4},{1,5},{2,6},{3,7},{4,0},{5,1},{6,2},{7,3},{8,12},{9,13},{10,... | collective-permute-start | bytes 884744 | tf_op jit(solution)/shard_map/ppermute | solution.py:456
  130.4 14.8 %collective-permute-start.40 = (bf16[8,48,384]{2,1,0:T(8,128)(2,1)S(1)}, bf16[8,48,384]{2,1,0:T(8,128)(2,1)S(1)}, u32[]{:S(2)}, u32[]{:S(2)}) collective-permute-start(bf16[8,48,384]{2,1,0:T(8,128)(2,1)S(1)} %slice.311), channel_id=1, source_target_pairs={{0,4},{1,5},{2,6},{3,7},{4,0},{5,1},{6,2},{7,3},{8,12},{9,13},{10,... | collective-permute-start | bytes 884744 | tf_op jit(solution)/shard_map/ppermute | solution.py:456
  132.2 14.0 %collective-permute-start.34 = (bf16[8,24,768]{2,1,0:T(8,128)(2,1)S(1)}, bf16[8,24,768]{2,1,0:T(8,128)(2,1)S(1)}, u32[]{:S(2)}, u32[]{:S(2)}) collective-permute-start(bf16[8,24,768]{2,1,0:T(8,128)(2,1)S(1)} %slice.303), channel_id=1, source_target_pairs={{0,2},{1,3},{2,0},{3,1},{4,6},{5,7},{6,4},{7,5},{8,10},{9,11},{10,... | collective-permute-start | bytes 884744 | tf_op jit(solution)/shard_map/ppermute | solution.py:456
  133.9 13.9 %collective-permute-start.29 = (bf16[8,24,768]{2,1,0:T(8,128)(2,1)S(1)}, bf16[8,24,768]{2,1,0:T(8,128)(2,1)S(1)}, u32[]{:S(2)}, u32[]{:S(2)}) collective-permute-start(bf16[8,24,768]{2,1,0:T(8,128)(2,1)S(1)} %slice.295), channel_id=1, source_target_pairs={{0,2},{1,3},{2,0},{3,1},{4,6},{5,7},{6,4},{7,5},{8,10},{9,11},{10,... | collective-permute-start | bytes 884744 | tf_op jit(solution)/shard_map/ppermute | solution.py:456
  139.5 9.3 %collective-permute-start.23 = (bf16[8,24,768]{2,1,0:T(8,128)(2,1)S(1)}, bf16[8,24,768]{2,1,0:T(8,128)(2,1)S(1)}, u32[]{:S(2)}, u32[]{:S(2)}) collective-permute-start(bf16[8,24,768]{2,1,0:T(8,128)(2,1)S(1)} %slice.285), channel_id=1, source_target_pairs={{0,1},{1,0},{2,3},{3,2},{4,5},{5,4},{6,7},{7,6},{8,9},{9,8},{10,11... | collective-permute-start | bytes 884744 | tf_op jit(solution)/shard_map/ppermute | solution.py:456
  145.2 9.9 %collective-permute-start.18 = (bf16[8,24,768]{2,1,0:T(8,128)(2,1)S(1)}, bf16[8,24,768]{2,1,0:T(8,128)(2,1)S(1)}, u32[]{:S(2)}, u32[]{:S(2)}) collective-permute-start(bf16[8,24,768]{2,1,0:T(8,128)(2,1)S(1)} %slice.277), channel_id=1, source_target_pairs={{0,1},{1,0},{2,3},{3,2},{4,5},{5,4},{6,7},{7,6},{8,9},{9,8},{10,11... | collective-permute-start | bytes 884744 | tf_op jit(solution)/shard_map/ppermute | solution.py:456
  146.2 9.9 %collective-permute-start.46 = (bf16[4,48,384]{2,1,0:T(8,128)(2,1)S(1)}, bf16[4,48,384]{2,1,0:T(8,128)(2,1)S(1)}, u32[]{:S(2)}, u32[]{:S(2)}) collective-permute-start(bf16[4,48,384]{2,1,0:T(8,128)(2,1)S(1)} %slice.321), channel_id=1, source_target_pairs={{0,2},{1,3},{2,0},{3,1},{4,6},{5,7},{6,4},{7,5},{8,10},{9,11},{10,... | collective-permute-start | bytes 442376 | tf_op jit(solution)/shard_map/ppermute | solution.py:456
  147.9 9.9 %collective-permute-start.41 = (bf16[4,48,384]{2,1,0:T(8,128)(2,1)S(1)}, bf16[4,48,384]{2,1,0:T(8,128)(2,1)S(1)}, u32[]{:S(2)}, u32[]{:S(2)}) collective-permute-start(bf16[4,48,384]{2,1,0:T(8,128)(2,1)S(1)} %slice.313), channel_id=1, source_target_pairs={{0,2},{1,3},{2,0},{3,1},{4,6},{5,7},{6,4},{7,5},{8,10},{9,11},{10,... | collective-permute-start | bytes 442376 | tf_op jit(solution)/shard_map/ppermute | solution.py:456
  148.8 9.6 %collective-permute-start.35 = (bf16[4,24,768]{2,1,0:T(8,128)(2,1)S(1)}, bf16[4,24,768]{2,1,0:T(8,128)(2,1)S(1)}, u32[]{:S(2)}, u32[]{:S(2)}) collective-permute-start(bf16[4,24,768]{2,1,0:T(8,128)(2,1)S(1)} %slice.305), channel_id=1, source_target_pairs={{0,1},{1,0},{2,3},{3,2},{4,5},{5,4},{6,7},{7,6},{8,9},{9,8},{10,11... | collective-permute-start | bytes 442376 | tf_op jit(solution)/shard_map/ppermute | solution.py:456
  156.1 8.7 %collective-permute-start.24 = (bf16[4,24,768]{2,1,0:T(8,128)(2,1)S(1)}, bf16[4,24,768]{2,1,0:T(8,128)(2,1)S(1)}, u32[]{:S(2)}, u32[]{:S(2)}) collective-permute-start(bf16[4,24,768]{2,1,0:T(8,128)(2,1)S(1)} %slice.287), channel_id=1, source_target_pairs={{0,2},{1,3},{2,0},{3,1},{4,6},{5,7},{6,4},{7,5},{8,10},{9,11},{10,... | collective-permute-start | bytes 442376 | tf_op jit(solution)/shard_map/ppermute | solution.py:456
  158.4 8.7 %collective-permute-start.47 = (bf16[2,48,384]{2,1,0:T(8,128)(2,1)S(1)}, bf16[2,48,384]{2,1,0:T(8,128)(2,1)S(1)}, u32[]{:S(2)}, u32[]{:S(2)}) collective-permute-start(bf16[2,48,384]{2,1,0:T(8,128)(2,1)S(1)} %slice.323), channel_id=1, source_target_pairs={{0,8},{1,9},{2,10},{3,11},{4,12},{5,13},{6,14},{7,15},{8,0},{9,1},... | collective-permute-start | bytes 221192 | tf_op jit(solution)/shard_map/ppermute | solution.py:456
  173.0 9.1 %collective-permute-start.37 = (bf16[1,24,768]{2,1,0:T(8,128)(2,1)S(1)}, bf16[1,24,768]{2,1,0:T(8,128)(2,1)S(1)}, u32[]{:S(2)}, u32[]{:S(2)}) collective-permute-start(bf16[1,24,768]{2,1,0:T(8,128)(2,1)S(1)} %slice.309), channel_id=1, source_target_pairs={{0,8},{1,9},{2,10},{3,11},{4,12},{5,13},{6,14},{7,15},{8,0},{9,1},... | collective-permute-start | bytes 110600 | tf_op jit(solution)/shard_map/ppermute | solution.py:456
  (68 other events, 427.6 us)

commit v2 on v1

v2 whole, which is shorter than its diff:
```python
import math

import jax
import jax.numpy as jnp
from jax import lax
from jax.experimental import pallas as pl
from jax.experimental.pallas import tpu as pltpu
from jax.sharding import PartitionSpec as P

D = 384
FF = 1536
HEADS = 6
HEAD_DIM = 64
STEP = 3
BF = jnp.bfloat16
F32 = jnp.float32

rate = 0.3
beta = 0.5
eps_adam = 1e-06
decay = 0.01
eps_norm = 1e-05
neg_large = -1e30

QB = 128
REACH = 256
ROWS = 64
CHUNK = 384
WIDE = 4 * D
HALF = WIDE // 2
PAIRS = HEADS // 2
PAIR = 2 * HEAD_DIM
VM = pl.BlockSpec(memory_space=pltpu.VMEM)
SM = pl.BlockSpec(memory_space=pltpu.SMEM)
ANY = pl.BlockSpec(memory_space=pl.ANY)
struct = jax.ShapeDtypeStruct


def dot(a, b, ca=1, cb=0):
    return lax.dot_general(a, b, (((ca,), (cb,)), ((), ())), preferred_element_type=F32)


def bands(length):
    out = []
    off = 0
    for b in range(length // QB):
        ks, ke = max(0, QB * b - REACH), QB * (b + 1)
        out.append((b, ks, ke, off))
        off += ke - ks
    return out, off


def unit_of(x):
    mean = jnp.sum(x, axis=-1, keepdims=True) * (1.0 / D)
    centered = x - mean
    variance = jnp.sum(centered * centered, axis=-1, keepdims=True) * (1.0 / D)
    inverse = lax.rsqrt(variance + eps_norm)
    return centered * inverse, inverse


def norm_into(x_ref, gain, n_ref):
    for r in range(0, x_ref.shape[0], ROWS):
        unit, _ = unit_of(x_ref[r : r + ROWS, :].astype(F32))
        n_ref[r : r + ROWS, :] = (unit * gain).astype(BF)


def norm_back(dn_ref, x_ref, dy_ref, gain, out_ref, low_ref):
    grad = jnp.zeros((1, D), F32)
    for r in range(0, x_ref.shape[0], ROWS):
        unit, inverse = unit_of(x_ref[r : r + ROWS, :].astype(F32))
        dn = dn_ref[r : r + ROWS, :]
        grad = grad + jnp.sum(dn * unit, axis=0, keepdims=True)
        e = dn * gain
        first = jnp.sum(e, axis=-1, keepdims=True) * (1.0 / D)
        cross = jnp.sum(e * unit, axis=-1, keepdims=True) * (1.0 / D)
        total = dy_ref[r : r + ROWS, :].astype(F32) + (e - first - unit * cross) * inverse
        if out_ref is not None:
            out_ref[r : r + ROWS, :] = total
        if low_ref is not None:
            low_ref[r : r + ROWS, :] = total.astype(BF)
    return grad


def make_bias(seg_ref, bias_ref, length):
    columns = []
    for b in range(length // QB):
        row = seg_ref[:, QB * b : QB * b + QB].astype(F32)
        columns.append(jnp.broadcast_to(row, (QB, QB)).T)
    for b, ks, ke, off in bands(length)[0]:
        row = seg_ref[:, QB * b : QB * b + QB].astype(F32)
        for k in range(ks, ke, QB):
            allowed = columns[k // QB] == row
            if k == QB * b:
                keys = lax.broadcasted_iota(jnp.int32, (QB, QB), 0)
                allowed = allowed & (keys <= lax.broadcasted_iota(jnp.int32, (QB, QB), 1))
            bias_ref[off + k - ks : off + k - ks + QB, :] = jnp.where(allowed, 0.0, neg_large)


def head_masked(pair_of, scale, dst_ref):
    lane = lax.broadcasted_iota(jnp.int32, (1, PAIR), 1)
    for p in range(PAIRS):
        for b in range(dst_ref.shape[1]):
            pair = pair_of(p, b)
            for member in (0, 1):
                mask = jnp.where(lane // HEAD_DIM == member, scale, 0.0).astype(BF)
                dst_ref[p, b, QB * member : QB * member + QB, :] = pair * mask


def attend(pk, k, length):
    q2, vT, bias, ss, pt, attT = k["q2"], k["vT"], k["bias"], k["ss"], k["pt"], k["attT"]
    vT[...] = pk[:, 2 * D :].T
    head_masked(lambda p, b: pk[QB * b : QB * b + QB, PAIR * p : PAIR * p + PAIR], HEAD_DIM ** (-0.5), q2)
    places = bands(length)[0]
    for p in range(PAIRS):
        lo = D + PAIR * p
        for b, ks, ke, off in places:
            seen = bias[off : off + ke - ks, :]
            products = dot(pk[ks:ke, lo : lo + PAIR], q2[p, b], 1, 1)
            ss[p, off : off + ke - ks, :] = products + jnp.concatenate([seen, seen], 1)
    for p in range(PAIRS):
        for b, ks, ke, off in places:
            for m in (0, 1):
                cols = slice(QB * m, QB * m + QB)
                scores = ss[p, off : off + ke - ks, cols]
                lifted = jnp.exp(scores - jnp.max(scores, axis=0, keepdims=True))
                share = 1.0 / jnp.sum(lifted, axis=0, keepdims=True)
                pt[p, off : off + ke - ks, cols] = (lifted * share).astype(BF)
    for p in range(PAIRS):
        for b, ks, ke, off in places:
            both = dot(vT[PAIR * p : PAIR * p + PAIR, ks:ke], pt[p, off : off + ke - ks, :])
            for m in (0, 1):
                lo = HEAD_DIM * m
                part = both[lo : lo + HEAD_DIM, QB * m : QB * m + QB].astype(BF)
                attT[PAIR * p + lo : PAIR * p + lo + HEAD_DIM, QB * b : QB * b + QB] = part


def attend_back(pk, pt, da, k, length):
    d2, q2, kT, ss, ds, dqT, dk, dv, dpk = (k[n] for n in ("d2", "q2", "kT", "ss", "ds", "dqT", "dk", "dv", "dpk"))
    head_masked(lambda p, b: pk[QB * b : QB * b + QB, PAIR * p : PAIR * p + PAIR], HEAD_DIM ** (-0.5), q2)
    head_masked(lambda p, b: da[QB * b : QB * b + QB, PAIR * p : PAIR * p + PAIR], 1.0, d2)
    kT[...] = pk[:, D : 2 * D].T
    places = bands(length)[0]
    for p in range(PAIRS):
        lo = 2 * D + PAIR * p
        for b, ks, ke, off in places:
            ss[p, off : off + ke - ks, :] = dot(pk[ks:ke, lo : lo + PAIR], d2[p, b], 1, 1)
    for p in range(PAIRS):
        for b, ks, ke, off in places:
            for m in (0, 1):
                cols = slice(QB * m, QB * m + QB)
                chances = pt[p, off : off + ke - ks, cols].astype(F32)
                grad = ss[p, off : off + ke - ks, cols]
                inner = jnp.sum(chances * grad, axis=0, keepdims=True)
                ds[p, off : off + ke - ks, cols] = (chances * (grad - inner)).astype(BF)
    for p in range(PAIRS):
        lo = PAIR * p
        for b, ks, ke, off in places:
            grad = ds[p, off : off + ke - ks, :]
            both = dot(kT[lo : lo + PAIR, ks:ke], grad)
            for m in (0, 1):
                rows = slice(HEAD_DIM * m, HEAD_DIM * m + HEAD_DIM)
                part = both[rows, QB * m : QB * m + QB] * HEAD_DIM ** (-0.5)
                dqT[lo + HEAD_DIM * m : lo + HEAD_DIM * m + HEAD_DIM, QB * b : QB * b + QB] = part
            gk, gv = dot(grad, q2[p, b]), dot(pt[p, off : off + ke - ks, :], d2[p, b])
            n = ke - ks - QB
            if n:
                dk[ks : ks + n, lo : lo + PAIR] += gk[:n]
                dv[ks : ks + n, lo : lo + PAIR] += gv[:n]
            dk[ks + n : ke, lo : lo + PAIR] = gk[n:]
            dv[ks + n : ke, lo : lo + PAIR] = gv[n:]
    dpk[:, 0:D] = dqT[...].T.astype(BF)
    dpk[:, D : 2 * D] = dk[...].astype(BF)
    dpk[:, 2 * D :] = dv[...].astype(BF)


def attention_half(x, k, wide, gain, length):
    norm_into(x, gain[0:1, :], k["n1"])
    make_bias(k["seg"], k["bias"], length)
    pk = k["pk"]
    for c in range(0, 3 * D, D):
        pk[:, c : c + D] = dot(k["n1"][...], wide[:, c : c + D]).astype(BF)
    attend(pk, k, length)
    mid = k["mid"]
    mid[...] = x[...].astype(F32) + dot(k["attT"][...], wide[:, 3 * D :], 0, 0)
    norm_into(mid, gain[1:2, :], k["n2"])


def feed_forward(k, up, down, length, out):
    c0 = 0.7978845608028654
    c1 = 0.044715
    hs, act, gp, n2 = k["hs"], k["act"], k["gp"], k["n2"]
    for i, c in enumerate(range(0, FF, CHUNK)):
        hs[i % 2] = dot(n2[...], up[:, c : c + CHUNK])
        for r in range(0, length, ROWS):
            v = hs[i % 2, r : r + ROWS, :]
            v2 = v * v
            th = jnp.tanh(v * (c0 + (c0 * c1) * v2))
            half = 0.5 * v
            act[r : r + ROWS, c : c + CHUNK] = (half + half * th).astype(BF)
            slope = 0.5 + 0.5 * th + half * (1.0 - th * th) * (c0 + (3.0 * c0 * c1) * v2)
            gp[r : r + ROWS, c : c + CHUNK] = slope.astype(BF)
    out(k["mid"][...] + dot(act[...], down[...]))


def feed_back(dy, k, up, down, gain, emit):
    act, n2, dh, dn = k["act"], k["n2"], k["dh"], k["dn"]
    emit.down(lambda lo, n: dot(act[:, lo : lo + n], dy[...], 0, 0))
    for c in range(0, FF, CHUNK):
        grad = dot(dy[...], down[c : c + CHUNK, :], 1, 1) * k["gp"][:, c : c + CHUNK].astype(F32)
        dh[:, c : c + CHUNK] = grad.astype(BF)
    emit.up(lambda lo, n: dot(n2[...], dh[:, lo : lo + n], 0, 0))
    dn[...] = dot(dh[...], up[...], 1, 1)
    grad = norm_back(dn, k["mid"], dy, gain[1:2, :], k["dmid"], k["dmb"])
    return grad


def attention_back(k, wide, emit, length):
    dmb, da, dpk = k["dmb"], k["da"], k["dpk"]
    da[...] = dot(dmb[...], wide[:, 3 * D :], 1, 1).astype(BF)
    attend_back(k["pk"], k["pt"], da, k, length)

    def grad(lo):
        if lo < 3 * D:
            return dot(k["n1"][...], dpk[:, lo : lo + D], 0, 0)
        return dot(k["attT"][...], dmb[...])

    for at in range(0, HALF, D):
        emit.wide(grad, at)


def input_back(x, k, wide, gain, out, low):
    k["dn"][...] = dot(k["dpk"][...], wide[:, : 3 * D], 1, 1)
    return norm_back(k["dn"], x, k["dmid"], gain[0:1, :], out, low)


def spread_bits(index, order):
    out = 0
    for k, bit in enumerate(order):
        out = out | (((index >> k) & 1) << bit)
    return out


def gather_bits(index, order):
    out = 0
    for k, bit in enumerate(order):
        out = out | (((index >> bit) & 1) << k)
    return out


class Plan:
    def __init__(self, mesh):
        self.count = mesh.shape["dp"]
        self.bits = self.count.bit_length() - 1
        rest = tuple(range(4, self.bits))
        x, y, near, far = 0, 1, 2, 3
        gathers = (
            ((far, near, y, x), (far, x, near, y)),
            ((y, far, near, x), (near, far, x, y)),
            ((far, y, x, near), (far, x, y, near)),
        )
        scatters = (((y, x, far, near), (x, y, near, far)), ((x, far, near, y), (y, near, far, x)))
        self.gather_orders = tuple(tuple(rest + o for o in pair) for pair in gathers)
        self.scatter_orders = tuple(tuple(o + rest for o in pair) for pair in scatters)
        self.thin = (D // self.count) % 8 != 0
        self.slabs = 1 if self.thin else self.count
        self.rows = D // self.slabs

    def source(self, flow, block, place, me):
        return spread_bits(place, self.gather_orders[flow][block]) ^ me

    def place(self, block, half, device, me):
        order = tuple(reversed(self.scatter_orders[block][half]))
        return gather_bits(device, order) ^ gather_bits(me, order)

    def weight_shape(self, flow):
        return (D, WIDE) if flow < 2 else (FF, D)

    def grad_shapes(self):
        if self.thin:
            return {"gp_": [((D, WIDE), BF)], "gq_": [((D, WIDE), BF), ((FF, D), BF)]}
        n, r = self.slabs, self.rows
        return {"gp_": [((n, r, HALF), BF)] * 2, "gq_": [((n, 2, r, HALF), BF)] * 2}


class Emit:
    def __init__(self, plan, block, first, second):
        self.plan, self.first, self.second = plan, first, second
        self.core, me = lax.axis_index("pipe"), lax.axis_index("dp")
        if plan.thin:
            return
        leading = self.core == 0
        places = [[plan.place(block, half, s, me) for s in range(plan.slabs)] for half in (0, 1)]
        self.places = [
            [jnp.where(leading, places[which][s], places[1 - which][s]) for s in range(plan.slabs)] for which in (0, 1)
        ]

    def halves(self, zero, one, put, first=0):
        leading = self.core == 0
        for which, value in ((0, jnp.where(leading, zero, one)), (1, jnp.where(leading, one, zero))):
            value = value.astype(BF)
            for s in range(value.shape[0]):
                put(which, self.places[which][first + s], value[s])

    def wide(self, make, at):
        plan = self.plan
        zero, one = make(at), make(HALF + at)
        if plan.thin:
            self.first[0][:, at : at + D] = zero.astype(BF)
            self.first[0][:, HALF + at : HALF + at + D] = one.astype(BF)
            return
        shape = (plan.slabs, plan.rows, D)

        def put(which, place, value):
            self.first[which][place, :, at : at + D] = value

        self.halves(zero.reshape(shape), one.reshape(shape), put)

    def up(self, make):
        plan = self.plan
        if plan.thin:
            for lo in range(0, FF, D):
                self.second[0][:, lo : lo + D] = make(lo, D).astype(BF)
            return
        shape = (plan.slabs, plan.rows, D)
        for lo in range(0, HALF, D):

            def put(which, place, value, lo=lo):
                self.second[which][place, 0, :, lo : lo + D] = value

            self.halves(make(lo, D).reshape(shape), make(HALF + lo, D).reshape(shape), put)

    def down(self, make):
        plan = self.plan
        for lo in range(0, FF, D):
            value = make(lo, D)
            if plan.thin:
                self.second[1][lo : lo + D, :] = value.astype(BF)
                continue
            value = value.reshape(D // (4 * plan.rows), 2, 2 * plan.rows, D)

            def put(which, place, value, r=plan.rows):
                self.second[which][place, 1, :, 0:D] = value[:r]
                self.second[which][place, 1, :, D : 2 * D] = value[r:]

            self.halves(value[:, 0], value[:, 1], put, lo // (4 * plan.rows))


def limit(size):
    return pltpu.CompilerParams(vmem_limit_bytes=int(size) + 6 * 2**20)


def run_kernel(name, body, block, inputs, outs, scratch, cost, after=()):
    arrays = {n: v if isinstance(v, tuple) else (v, ()) for n, v in inputs.items()}
    size = sum(math.prod(shape) * jnp.dtype(dtype).itemsize for shape, dtype in scratch.values())

    def kernel(*refs):
        names = list(arrays) + [None] * len(after) + list(outs) + list(scratch)
        k = dict(zip(names, refs))
        core = lax.axis_index("pipe")
        for n, (_, index) in arrays.items():
            if index:
                k[n] = k[n].at[tuple(core if i == "core" else i for i in index)]
        gain = None
        if "gains" in arrays:
            gain = jnp.where(core == block, k["gains"][...], k["gains_got"][...])
        body(k, gain)

    result = pl.pallas_call(
        kernel,
        name=name,
        out_shape=[struct(*v) for v in outs.values()],
        in_specs=[VM] * len(arrays) + [ANY] * len(after),
        out_specs=[VM] * len(outs),
        scratch_shapes=[pltpu.VMEM(*v) for v in scratch.values()],
        compiler_params=limit(size),
        cost_estimate=pl.CostEstimate(flops=int(cost * 1e10), bytes_accessed=int(cost * 1e6), transcendentals=0),
    )(*[v for v, _ in arrays.values()], *after)
    return dict(zip(outs, result))


def small_kernel(name, kernel, outs, *inputs, after=()):
    def run(*refs):
        kernel(*refs[: len(inputs)], *refs[len(inputs) + len(after) :])

    return pl.pallas_call(
        run,
        name=name,
        out_shape=outs,
        in_specs=[VM] * len(inputs) + [ANY] * len(after),
        out_specs=[VM] * len(outs),
        compiler_params=limit(0),
    )(*inputs, *after)


def arrange(plan, flow, own, got):
    n, each = plan.slabs, plan.slabs // 2

    def kernel(a0, b0, a1, b1, zero, one):
        core, me = lax.axis_index("pipe"), lax.axis_index("dp")

        def move(first, second, dst, block):
            for place in range(n):
                src = first if place < each else second
                dst[plan.source(flow, block, place, me)] = src[place % each]

        @pl.when(core == 0)
        def _():
            move(a0, b0, zero, 0)
            move(a1, b1, one, 1)

        @pl.when(core != 0)
        def _():
            move(a0, b0, one, 1)
            move(a1, b1, zero, 0)

    like = struct((n, *own[0].shape[1:]), BF)
    out = small_kernel("arrange", kernel, [like, like], *own, *got)
    return [v.reshape(plan.weight_shape(flow)) for v in out]


def shapes(L):
    nb = bands(L)[1]
    return dict(
        n1=((L, D), BF),
        pk=((L, 3 * D), BF),
        pt=((PAIRS, nb, 2 * QB), BF),
        attT=((D, L), BF),
        mid=((L, D), F32),
        n2=((L, D), BF),
        act=((L, FF), BF),
        gp=((L, FF), BF),
        q2=((PAIRS, L // QB, 2 * QB, PAIR), BF),
        d2=((PAIRS, L // QB, 2 * QB, PAIR), BF),
        vT=((D, L), BF),
        bias=((nb, QB), F32),
        ss=((PAIRS, nb, 2 * QB), F32),
        ds=((PAIRS, nb, 2 * QB), BF),
        hs=((2, L, CHUNK), F32),
        dh=((L, FF), BF),
        dn=((L, D), F32),
        dmid=((L, D), F32),
        dmb=((L, D), BF),
        kT=((D, L), BF),
        dqT=((D, L), F32),
        dk=((L, D), F32),
        dv=((L, D), F32),
        dpk=((L, 3 * D), BF),
        da=((L, D), BF),
        x1=((L, D), F32),
        y2=((L, D), F32),
        dx=((L, D), F32),
        dxb=((L, D), BF),
        dg=((1, D), F32),
    )


def swap_cores(block):
    return lax.ppermute(block, "pipe", [(0, 1), (1, 0)])


def swap(block, bits):
    n = lax.axis_size("dp")
    route = [(c * n + i, c * n + (i ^ (1 << bits[c]))) for c in range(2) for i in range(n)]
    return lax.ppermute(block, ("pipe", "dp"), route)


def join(a, b, after):
    def kernel(a, b, out):
        n = a.shape[0]
        out[:n] = a[...]
        out[n:] = b[...]

    return small_kernel("join", kernel, [struct((2 * a.shape[0], *a.shape[1:]), a.dtype)], a, b, after=after)[0]


def gather(plan, shards):
    held = [shard[None] for shard in shards]
    last = ()
    for turn in range(plan.bits):
        came = [swap(held[f], (orders[0][turn], orders[1][turn])) for f, orders in enumerate(plan.gather_orders)]
        if turn < plan.bits - 1:
            for f in range(3):
                held[f] = join(held[f], came[f], last)
                last = (held[f],)
    return [(a, b) for a, b in zip(held, came)]


def added(a, b):
    return (a.astype(F32) + b.astype(F32)).astype(BF)


def add_first(first, second, after=()):
    def kernel(a, b, c, d, *outs):
        n = outs[0].shape[0]
        for i, out in enumerate(outs):
            for j in range(n):
                out[j, 0] = added(a[n * i + j], b[n * i + j])
                out[j, 1:3] = added(c[n * i + j], d[n * i + j])

    n, r, width = first[0].shape
    return small_kernel("add_first", kernel, [struct((n // 2, 3, r, width), BF)] * 2, *first, *second, after=after)


def add_split(a, b, after=()):
    def kernel(a, b, *outs):
        n = outs[0].shape[0]
        for i, out in enumerate(outs):
            for j in range(n):
                out[j] = added(a[n * i + j], b[n * i + j])

    return small_kernel("add_split", kernel, [struct((a.shape[0] // 2, *a.shape[1:]), BF)] * 2, a, b, after=after)


def behind(value, *others):
    return lax.optimization_barrier((value, *others))[0]


class Scatter:
    def __init__(self, plan, block, first, second):
        self.orders, self.turn = plan.scatter_orders[block], 0
        self.keep, self.send = add_first(first, second)

    def came(self, *after):
        send = behind(self.send, *after) if after else self.send
        value = swap(send, (self.orders[0][self.turn], self.orders[1][self.turn]))
        self.turn += 1
        return value

    def step(self, start_after=(), end_after=()):
        self.keep, self.send = add_split(self.keep, self.came(*start_after), end_after)


def owners(zero, one):
    def kernel(a, b, c, d, own, send):
        leading = lax.axis_index("pipe") == 0
        zero, one = a[0].astype(F32) + b[0].astype(F32), c[0].astype(F32) + d[0].astype(F32)
        own[...] = jnp.where(leading, zero, one).astype(BF)
        send[...] = jnp.where(leading, one, zero).astype(BF)

    like = struct(zero[0].shape[1:], BF)
    return small_kernel("owners", kernel, [like, like], *zero, *one)


def thin_arrange(plan, flow, own, got):
    core, me = lax.axis_index("pipe"), lax.axis_index("dp")
    index = jnp.arange(plan.count, dtype=jnp.int32)
    out = []
    for block in (0, 1):
        held = jnp.where(core == block, jnp.concatenate(own, 0), jnp.concatenate(got, 0))
        held = jnp.zeros_like(held).at[plan.source(flow, block, index, me)].set(held)
        out.append(held.reshape(plan.weight_shape(flow)))
    return out


def thin_halves(plan, block, grads, bundle):
    core, me = lax.axis_index("pipe"), lax.axis_index("dp")
    n, r = plan.count, D // plan.count
    parts = grads[0].reshape(n, r, 2, HALF).transpose(2, 0, 1, 3)
    if bundle:
        down = grads[1].reshape(n, 2, 2, r, D).transpose(1, 0, 3, 2, 4).reshape(2, n, r, HALF)
        parts = jnp.stack([parts, down], 2)
    index = jnp.arange(n, dtype=jnp.int32)
    halves = [jnp.zeros_like(parts[h]).at[plan.place(block, h, index, me)].set(parts[h]) for h in (0, 1)]
    return [jnp.where(core == 0, halves[i], halves[1 - i]) for i in (0, 1)]


def lanes(values):
    lane = lax.broadcasted_iota(jnp.int32, (1, D), 1)
    row = jnp.zeros((1, D), F32)
    for place, value in values:
        row = row + jnp.where(lane == place, value, 0.0)
    return row


def square_sum(v):
    return jnp.sum(jnp.sum(v * v, axis=1, keepdims=True), axis=0, keepdims=True)


def moments(master, grad, first, second):
    drift = beta * first + (1.0 - beta) * grad
    spread = beta * second + (1.0 - beta) * grad * grad
    correction = 1.0 - beta**STEP
    update = drift / correction / (jnp.sqrt(spread / correction) + eps_adam) + decay * master
    return (drift, spread, update)


def prepare(plan, masters):
    r = D // plan.count

    def kernel(wi, wo, wu, wd, wide, up, down, row):
        wide[:, : 3 * D] = wi[...].astype(BF)
        wide[:, 3 * D :] = wo[...].astype(BF)
        up[...] = wu[...].astype(BF)
        for q in range(4):
            down[q] = wd[r * q : r * q + r, :].astype(BF)
        row[...] = lanes([(i, square_sum(m[...])) for i, m in enumerate((wi, wo, wu, wd))])

    outs = [struct((r, WIDE), BF), struct((r, WIDE), BF), struct((4, r, D), BF), struct((1, D), F32)]
    return small_kernel("prepare", kernel, outs, *masters)


def update_moments(plan, own, got, masters, firsts, seconds, weight_row, gain_own, gain_got):
    r = D // plan.count

    def kernel(own, got, *refs):
        masters, firsts, seconds, (weight_row, gain_own, gain_got) = refs[0:4], refs[4:8], refs[8:12], refs[12:15]
        drifts, spreads, updates, small = refs[15:19], refs[19:23], refs[23:27], refs[27]
        leading = lax.axis_index("pipe") == 0
        a, b = own[...].astype(F32), got[...].astype(F32)
        h = (jnp.where(leading, a, b), jnp.where(leading, b, a))
        whole, tail = slice(None), 3 * D - HALF
        grads = [
            [((whole, slice(0, HALF)), h[0][0]), ((whole, slice(HALF, 3 * D)), h[1][0][:, :tail])],
            [((whole, slice(0, D)), h[1][0][:, tail:])],
            [((whole, slice(HALF * i, HALF * i + HALF)), h[i][1]) for i in (0, 1)],
            [
                ((slice(r * (2 * i + q), r * (2 * i + q) + r), whole), h[i][2][:, D * q : D * q + D])
                for i in (0, 1)
                for q in (0, 1)
            ],
        ]
        sums = []
        for m in range(4):
            total = jnp.zeros((1, 1), F32)
            for at, grad in grads[m]:
                drift, spread, update = moments(masters[m][at], grad, firsts[m][at], seconds[m][at])
                drifts[m][at], spreads[m][at], updates[m][at] = drift, spread, update
                total = total + square_sum(update)
            sums.append((4 + m, total))
        row = lanes(sums) + weight_row[...]
        gain = gain_own[...] + gain_got[...]
        for i in range(plan.count):
            small[i, 0:1, :] = row
            small[i, 1:3, :] = gain

    like = [struct(m.shape, F32) for m in masters]
    outs = like * 3 + [struct((plan.count, 3, D), F32)]
    res = small_kernel("moments", kernel, outs, own, got, *masters, *firsts, *seconds, weight_row, gain_own, gain_got)
    return res[0:4], res[4:8], res[8:12], res[12]


def finish(small, masters, updates, gains, gain_first, gain_second):
    def kernel(parts, m0, m1, m2, m3, u0, u1, u2, u3, gains, gf, gs, *outs):
        new, low, (gain_drift, gain_spread, gain_new, pairs) = outs[0:4], outs[4:8], outs[8:12]
        small = jnp.sum(parts[...], axis=0)
        weight = [jnp.sqrt(small[0:1, i : i + 1]) for i in range(4)]
        step = [jnp.sqrt(small[0:1, 4 + i : 5 + i]) for i in range(4)]
        for i, (m, u) in enumerate(zip((m0, m1, m2, m3), (u0, u1, u2, u3))):
            value = m[...] - rate * (weight[i] / step[i]) * u[...]
            new[i][...] = value
            low[i][...] = value.astype(BF)
        drift, spread, update = moments(gains[...], small[1:3, :], gf[...], gs[...])
        gain_drift[...] = drift
        gain_spread[...] = spread
        gain_weight = jnp.sqrt(jnp.sum(gains[...] * gains[...], axis=1, keepdims=True))
        gain_step = jnp.sqrt(jnp.sum(update * update, axis=1, keepdims=True))
        gain_new[...] = gains[...] - rate * (gain_weight / gain_step) * update
        for i in range(4):
            pairs[i : i + 1, 0:1] = weight[i]
            pairs[i : i + 1, 1:2] = step[i]
        pairs[4:6, 0:1] = gain_weight
        pairs[4:6, 1:2] = gain_step

    outs = [struct(m.shape, F32) for m in masters] + [struct(m.shape, BF) for m in masters]
    outs += [struct((2, D), F32)] * 3 + [struct((6, 2), F32)]
    return small_kernel("finish", kernel, outs, small, *masters, *updates, gains, gain_first, gain_second)


def lay_results(own, got):
    def kernel(own, got, out):
        core = lax.axis_index("pipe")
        out[core] = own[...]
        out[1 - core] = got[...]

    return small_kernel("lay_results", kernel, [struct((2, *own.shape), F32)], own, got)[0]


def solution(mesh):
    plan = Plan(mesh)

    def per_device(
        tokens,
        prompts,
        cotangent,
        segments,
        weight_in,
        weight_out,
        weight_up,
        weight_down,
        first_in,
        first_out,
        first_up,
        first_down,
        second_in,
        second_out,
        second_up,
        second_down,
        gains,
        gain_first,
        gain_second,
    ):
        L = tokens.shape[2]
        sh = shapes(L)
        masters = (weight_in[0], weight_out[0], weight_up[0], weight_down[0])
        firsts = (first_in[0], first_out[0], first_up[0], first_down[0])
        seconds = (second_in[0], second_out[0], second_up[0], second_down[0])

        wide, up, down, weight_row = prepare(plan, masters)
        flows = gather(plan, (wide, up, down))
        got = [tuple(swap_cores(v) for v in pieces) for pieces in flows]
        gains_got = swap_cores(gains[0])
        put = thin_arrange if plan.thin else arrange
        both = [put(plan, f, flows[f], got[f]) for f in range(3)]

        def weights(block, *which):
            return {n: both[f][block] for f, n in enumerate(("wide", "up", "down")) if n in which}

        def pick(*names):
            return {n: sh[n] for n in names}

        def there(source, *names):
            return {n: source[n] for n in names}

        gain_refs = {"gains": gains[0], "gains_got": gains_got}
        grads = plan.grad_shapes()
        g_first = {f"p{i}": v for i, v in enumerate(grads["gp_"])}
        g_second = {f"q{i}": v for i, v in enumerate(grads["gq_"])}
        x0 = {"x": (tokens, ("core", 0))}
        seg = {"seg": (segments[:, :, None], ("core", 0))}

        def refs_of(k, table):
            return [k[n] for n in table]

        def traded(source, table, block, bundle):
            values = [source[n] for n in table]
            if plan.thin:
                values = thin_halves(plan, block, values, bundle)
            return values[0], swap_cores(values[1])

        def body(k, gain):
            attention_half(k["x"], k, k["wide"], gain, L)

        attention_scratch = pick("q2", "vT", "bias", "ss")
        one = run_kernel(
            "extractor_attention", body, 0, {**gain_refs, **x0, **seg, **weights(0, "wide")},
            pick("n1", "pk", "pt", "attT", "mid", "n2"), attention_scratch, 6,
        )

        def body(k, gain):
            def out(value):
                k["x1"][...] = value.astype(BF).astype(F32) + k["pr"][...].astype(F32)

            feed_forward(k, k["up"], k["down"], L, out)

        two = run_kernel(
            "extractor_feed", body, 0,
            {**there(one, "n2", "mid"), "pr": (prompts, ("core", 0)), **weights(0, "up", "down")},
            pick("act", "gp", "x1"), pick("hs"), 4,
        )

        def body(k, gain):
            attention_half(k["x1"], k, k["wide"], gain, L)

        three = run_kernel(
            "generator_attention", body, 1, {**gain_refs, **there(two, "x1"), **seg, **weights(1, "wide")},
            pick("n1", "pk", "pt", "attT", "mid", "n2"), attention_scratch, 6,
        )

        def body(k, gain):
            def out(value):
                k["y2"][...] = value

            feed_forward(k, k["up"], k["down"], L, out)
            emit = Emit(plan, 1, None, refs_of(k, g_second))
            k["dg"][...] = feed_back(k["dy"], k, k["up"], k["down"], gain, emit)

        cot = {"dy": (cotangent, ("core", 0))}
        four = run_kernel(
            "generator_feed", body, 1,
            {**gain_refs, **there(three, "mid", "n2"), **cot, **weights(1, "up", "down")},
            {**pick("y2", "dmid", "dmb", "dg"), **g_second}, pick("act", "gp", "hs", "dh", "dn"), 10,
        )

        back_scratch = pick("q2", "d2", "kT", "ss", "ds", "dqT", "dk", "dv", "da")

        def body(k, gain):
            emit = Emit(plan, 1, refs_of(k, g_first), None)
            attention_back(k, k["wide"], emit, L)

        five = run_kernel(
            "generator_attention_back", body, 1,
            {**there(four, "dmb"), **there(three, "attT", "pk", "pt", "n1"), **weights(1, "wide")},
            {**g_first, **pick("dpk")}, back_scratch, 6,
        )

        second_one = traded(four, g_second, 1, 1)

        def body(k, gain):
            k["dg"][...] = input_back(k["x1"], k, k["wide"], gain, None, k["dxb"])

        six = run_kernel(
            "generator_input_back", body, 1,
            {**gain_refs, **there(five, "dpk"), **there(four, "dmid"), **there(two, "x1"), **weights(1, "wide")},
            pick("dg", "dxb"), pick("dn"), 3,
        )
        sum_one = Scatter(plan, 1, traded(five, g_first, 1, 0), second_one)

        def body(k, gain):
            emit = Emit(plan, 0, None, refs_of(k, g_second))
            k["dg"][...] = feed_back(k["dxb"], k, k["up"], k["down"], gain, emit)

        seven = run_kernel(
            "extractor_feed_back", body, 0,
            {**gain_refs, **there(six, "dxb"), **there(two, "act", "gp"), **there(one, "n2", "mid"), **weights(0, "up", "down")},
            {**g_second, **pick("dmid", "dmb", "dg")}, pick("dh", "dn"), 7, after=[sum_one.send],
        )
        second_zero = traded(seven, g_second, 0, 1)

        def body(k, gain):
            emit = Emit(plan, 0, refs_of(k, g_first), None)
            attention_back(k, k["wide"], emit, L)

        eight = run_kernel(
            "extractor_attention_back", body, 0,
            {**there(seven, "dmb"), **there(one, "attT", "pk", "pt", "n1"), **weights(0, "wide")},
            {**g_first, **pick("dpk")}, back_scratch, 6,
        )
        sum_one.step(end_after=[eight["dpk"]])
        sum_zero = Scatter(plan, 0, traded(eight, g_first, 0, 0), second_zero)

        def body(k, gain):
            dg = input_back(k["x"], k, k["wide"], gain, k["dx"], None)
            leading = lax.axis_index("pipe") == 0
            k["own"][...] = jnp.where(leading, k["dx"][...], k["y2"][...])
            k["send"][...] = jnp.where(leading, k["y2"][...], k["dx"][...])
            for i, (zero, one) in enumerate(((dg, k["g10"][...]), (k["g01"][...], k["g11"][...]))):
                k["gain_own"][i : i + 1, :] = jnp.where(leading, zero, one)
                k["gain_send"][i : i + 1, :] = jnp.where(leading, one, zero)

        nine = run_kernel(
            "extractor_input_back", body, 0,
            {**gain_refs, **there(eight, "dpk"), **there(seven, "dmid"), **x0, **weights(0, "wide"), **there(four, "y2"),
             "g01": seven["dg"], "g10": six["dg"], "g11": four["dg"]},
            {"own": sh["dx"], "send": sh["dx"], "gain_own": ((2, D), F32), "gain_send": ((2, D), F32)},
            pick("dn", "dx"), 3, after=[sum_zero.send, sum_one.send],
        )
        token = [nine["gain_own"]]
        sum_one.step(end_after=token)
        sum_zero.step(end_after=token)
        for turn in range(plan.bits - 3):
            sum_one.step()
            sum_zero.step()
        sum_zero.step()
        zero = sum_zero.keep, sum_zero.came()
        one = sum_one.keep, sum_one.came()
        own, send = owners(zero, one)
        grad_got = swap_cores(send)

        result = lay_results(nine["own"], swap_cores(nine["send"]))
        section_result = result[None, :, None]
        drifts, spreads, updates, small = update_moments(
            plan, own, grad_got, masters, firsts, seconds, weight_row, nine["gain_own"], swap_cores(nine["gain_send"])
        )
        small = lax.all_to_all(small, "dp", 0, 0)
        done = finish(small, masters, updates, gains[0], gain_first[0], gain_second[0])
        return (
            section_result,
            *[v[None] for v in (*drifts, *spreads)],
            *[v[None] for v in done],
        )

    rows = P(None, "dp", None, None)
    matrix = P("pipe", "dp", None)
    gain = P("pipe", None, None)
    in_specs = (rows, rows, rows, P(None, "dp", None)) + (matrix,) * 12 + (gain,) * 3
    out_specs = (P("pipe", None, "dp", None, None),) + (matrix,) * 16 + (gain,) * 4
    return jax.shard_map(
        per_device, mesh=mesh, in_specs=in_specs, out_specs=out_specs, check_vma=False
    )
```

time: 220 us -> 150 us (0.68)
  Pallas kernels: 67.2 us -> 37.2 us
  other arithmetic: 21.8 us -> 0 us
  local copies, waits for them, and re-layouts: 18.4 us -> 4.6 us
  waiting for transfers between devices: 49.5 us -> 62.7 us
  starting transfers between devices: 56.1 us -> 43.4 us
  between operations: 4.42 us -> 1.31 us
    pallas_call x3 -> x34, Pallas kernels: 67.2 us -> 37.2 us  [the longest x9 30.9 us: run_kernel(): pl.pallas_call(kernel, name=name, out_shape=[struct(*v) for v in outs.val...]
    ppermute x40 -> x20, starting transfers between devices: 51.8 us -> 34.3 us  [swap(): return lax.ppermute(block, ('pipe', 'dp'), route)]
    squeeze x9 -> x0, local copies, waits for them, and re-layouts: 7.05 us -> none  [the longest x6 3.7 us: scatter(): g[1]]
    all_to_all x0 -> x1, waiting for transfers between devices: none -> 6.37 us  [per_device(): small = lax.all_to_all(small, 'dp', 0, 0)]
    another operation x2 -> x0, local copies, waits for them, and re-layouts: 6.12 us -> none  [the longest x1 5.26 us: per_device(): jnp.stack(squares)]
    reduce_sum x7 -> x0, other arithmetic: 6.07 us -> none  [the longest x4 4.1 us: per_device(): jnp.sum(st[2] * st[2])]
    all_to_all x0 -> x1, starting transfers between devices: none -> 5.83 us  [per_device(): small = lax.all_to_all(small, 'dp', 0, 0)]
    convert_element_type x29 -> x0, other arithmetic: 5.11 us -> none  [the longest x2 1.75 us: per_device(): low = [m.astype(BF) for m in masters]]
  transfers between devices with their start and end apart: 55 -> 35, of which waited for: 21 -> 18; matrix products, arithmetic and copies ran while one was open for 14% -> 0% of each run, Pallas kernels for 8% -> 10%
where the time goes in v2:
time: 150 us; the launch traced here: 149 us
  waiting for transfers between devices  62.7 us (42%)
  starting transfers between devices  43.4 us (29%)
  Pallas kernels  37.2 us (25%)
  local copies, waits for them, and re-layouts  4.6 us (3%)
    ppermute x20, waiting for transfers between devices, swap(): return lax.ppermute(block, ('pipe', 'dp'), route)  52.4 us
    ppermute x20, starting transfers between devices, swap(): return lax.ppermute(block, ('pipe', 'dp'), route)  34.3 us
    pallas_call x9, Pallas kernels, run_kernel(): pl.pallas_call(kernel, name=name, out_shape=[struct(*v) for v in outs.val...  30.9 us
    all_to_all x1, waiting for transfers between devices, per_device(): small = lax.all_to_all(small, 'dp', 0, 0)  6.37 us
    pallas_call x25, Pallas kernels, small_kernel(): pl.pallas_call(run, name=name, out_shape=outs, in_specs=[VM] * len(inputs...  6.25 us
    all_to_all x1, starting transfers between devices, per_device(): small = lax.all_to_all(small, 'dp', 0, 0)  5.83 us
    ppermute x14, waiting for transfers between devices, swap_cores(): return lax.ppermute(block, 'pipe', [(0, 1), (1, 0)])  3.97 us
    unnamed x72, local copies, waits for them, and re-layouts  3.95 us
  transfers between devices with their start and end apart: 35, of which 18 were waited for; matrix products, arithmetic and copies ran while one was open for 0% of the time, Pallas kernels for 10%

profile of v2, /device:TPU:0, one launch (start us, length us, event | category | flops | bytes accessed | tf_op | source)
XLA Modules:
  0.0 149.3 jit_solution(10853944808622290291)
XLA Ops:
  4.3 4.1 %collective-permute-start.1 = (bf16[1,24,1536]{2,1,0:T(8,128)(2,1)S(1)}, bf16[1,24,1536]{2,1,0:T(8,128)(2,1)S(1)}, u32[]{:S(2)}, u32[]{:S(2)}) collective-permute-start(bf16[1,24,1536]{2,1,0:T(8,128)(2,1)S(1)} %bitcast.70), channel_id=1, source_target_pairs={{0,8},{1,9},{2,10},{3,11},{4,12},{5,13},{6,14},{7,15},{8,0},{9,1},... | collective-permute-start | bytes 221192 | tf_op jit(solution)/shard_map/ppermute | solution.py:464
  11.7 3.1 %collective-permute-start.2 = (bf16[2,24,1536]{2,1,0:T(8,128)(2,1)S(1)}, bf16[2,24,1536]{2,1,0:T(8,128)(2,1)S(1)}, u32[]{:S(2)}, u32[]{:S(2)}) collective-permute-start(bf16[2,24,1536]{2,1,0:T(8,128)(2,1)S(1)} %join.9.refs_2_.refs_0_), channel_id=1, source_target_pairs={{0,4},{1,5},{2,6},{3,7},{4,0},{5,1},{6,2},{7,3},{8,12},{9,13},{10,... | collective-permute-start | bytes 442376 | tf_op jit(solution)/shard_map/ppermute | solution.py:464
  14.8 3.6 %collective-permute-start.7 = (bf16[2,24,1536]{2,1,0:T(8,128)(2,1)S(1)}, bf16[2,24,1536]{2,1,0:T(8,128)(2,1)S(1)}, u32[]{:S(2)}, u32[]{:S(2)}) collective-permute-start(bf16[2,24,1536]{2,1,0:T(8,128)(2,1)S(1)} %join.10.refs_2_.refs_0_), channel_id=1, source_target_pairs={{0,8},{1,9},{2,10},{3,11},{4,12},{5,13},{6,14},{7,15},{8,0},{9,1},... | collective-permute-start | bytes 442376 | tf_op jit(solution)/shard_map/ppermute | solution.py:464
  20.6 2.6 %collective-permute-done.7.refs_1_ = bf16[2,24,1536]{2,1,0:T(8,128)(2,1)S(1)} collective-permute-done((bf16[2,24,1536]{2,1,0:T(8,128)(2,1)S(1)}, bf16[2,24,1536]{2,1,0:T(8,128)(2,1)S(1)}, u32[]{:S(2)}, u32[]{:S(2)}) %collective-permute-start.7) | collective-permute-done | bytes 147488 | tf_op jit(solution)/shard_map/ppermute | solution.py:464
  23.3 2.9 %collective-permute-start.11 = (bf16[4,24,1536]{2,1,0:T(8,128)(2,1)S(1)}, bf16[4,24,1536]{2,1,0:T(8,128)(2,1)S(1)}, u32[]{:S(2)}, u32[]{:S(2)}) collective-permute-start(bf16[4,24,1536]{2,1,0:T(8,128)(2,1)S(1)} %join.13.refs_2_.refs_0_), channel_id=1, source_target_pairs={{0,4},{1,5},{2,6},{3,7},{4,0},{5,1},{6,2},{7,3},{8,12},{9,13},{10,... | collective-permute-start | bytes 884744 | tf_op jit(solution)/shard_map/ppermute | solution.py:464
  35.5 9.2 %collective-permute-done.16.refs_1_ = bf16[8,4,24,384]{3,2,1,0:T(8,128)(2,1)S(1)} collective-permute-done((bf16[8,4,24,384]{3,2,1,0:T(8,128)(2,1)S(1)}, bf16[8,4,24,384]{3,2,1,0:T(8,128)(2,1)S(1)}, u32[]{:S(2)}, u32[]{:S(2)}) %collective-permute-start.16) | collective-permute-done | bytes 589856 | tf_op jit(solution)/shard_map/ppermute | solution.py:464
  45.7 3.8 %collective-permute-done.8.refs_1_ = bf16[8,24,1536]{2,1,0:T(8,128)(2,1)S(1)} collective-permute-done((bf16[8,24,1536]{2,1,0:T(8,128)(2,1)S(1)}, bf16[8,24,1536]{2,1,0:T(8,128)(2,1)S(1)}, u32[]{:S(2)}, u32[]{:S(2)}) %collective-permute-start.8) | collective-permute-done | bytes 589856 | tf_op jit(solution)/shard_map/ppermute | solution.py:464
  52.2 3.3 %extractor_attention.1 = (bf16[512,384]{1,0:T(8,128)(2,1)S(1)}, bf16[512,1152]{1,0:T(8,128)(2,1)S(1)}, bf16[3,1152,256]{2,1,0:T(8,128)(2,1)S(1)}, bf16[384,512]{...) custom-call(f32[2,384]{1,0:T(2,128)S(1)} %bitcast.75, ...), custom_call_target="tpu_custom_call" | custom-call | flops 60000002048 | bytes 6000000 | tf_op jit(solution)/shard_map/extractor_attention/pallas_call | solution.py:368
  55.5 3.2 %extractor_feed.1 = (bf16[512,1536]{1,0:T(8,128)(2,1)S(1)}, bf16[512,1536]{1,0:T(8,128)(2,1)S(1)}, f32[512,384]{1,0:T(8,128)S(1)}) custom-call(bf16[512,384]{1,0:T(8,128)(2,1)S(1)} %get-tuple-element.116.refs_0_.refs_5_, f32[512,384]{1,0:T(8,128)S(1)} %get-tuple-element.117.refs_1_.refs_6_, bf16[2,1,512,384]{3,2,1,0:T(8,128)(2,1)S(1)} %copy-done.25, ...), custom_call_target="tpu_custom_call" | custom-call | flops 40000000000 | bytes 4000000 | tf_op jit(solution)/shard_map/extractor_feed/pallas_call | solution.py:368
  58.8 3.2 %generator_attention.1 = (bf16[512,384]{1,0:T(8,128)(2,1)S(1)}, bf16[512,1152]{1,0:T(8,128)(2,1)S(1)}, bf16[3,1152,256]{2,1,0:T(8,128)(2,1)S(1)}, bf16[384,512]{...) custom-call(f32[2,384]{1,0:T(2,128)S(1)} %bitcast.76, ...), custom_call_target="tpu_custom_call" | custom-call | flops 60000002048 | bytes 6000000 | tf_op jit(solution)/shard_map/generator_attention/pallas_call | solution.py:368
  62.0 7.3 %generator_feed.1 = (f32[512,384]{1,0:T(8,128)S(1)}, f32[512,384]{1,0:T(8,128)S(1)}, bf16[512,384]{1,0:T(8,128)(2,1)S(1)}, f32[1,384]{1,0:T(1,128)S(1)}, bf16[16...) custom-call(f32[2,384]{1,0:T(2,128)S(1)} %bitcast.77, f32[2,384]{1,0:T(2,128)S(1)} %collective-permute-done.refs_1_, ...), custom_call_target="tpu_custom_call" | custom-call | flops 99999997952 | bytes 10000000 | tf_op jit(solution)/shard_map/generator_feed/pallas_call | solution.py:368
  69.4 3.8 %generator_attention_back.1 = (bf16[16,24,768]{2,1,0:T(8,128)(2,1)S(1)}, bf16[16,24,768]{2,1,0:T(8,128)(2,1)S(1)}, bf16[512,1152]{1,0:T(8,128)(2,1)S(1)}) custom-call(bf16[512,384]{1,0:T(8,128)(2,1)S(1)} %get-tuple-element.126.refs_0_, bf16[384,512]{1,0:T(8,128)(2,1)S(1)} %get-tuple-element.127.refs_1_, bf16[512,1152]{1,0:T(8,128)(2,1)S(1)} %get-tuple-element.128.refs_2_, ...), custom_call_target="tpu_custom_call" | custom-call | flops 60000002048 | bytes 6000000 | tf_op jit(solution)/shard_map/generator_attention_back/pallas_call | solution.py:368
  79.5 4.1 %extractor_feed_back.1 = (bf16[16,2,24,768]{3,2,1,0:T(8,128)(2,1)S(1)}, bf16[16,2,24,768]{3,2,1,0:T(8,128)(2,1)S(1)}, f32[512,384]{1,0:T(8,128)S(1)}, bf16[512,384]{1,0:T(8,128)(2,1)S(1)}, f32[1,384]{1,0:T(1,128)S(1)}) custom-call(f32[2,384]{1,0:T(2,128)S(1)} %bitcast.79, f32[2,384]{1,0:T(2,128)S(1)} %collective-permute-done.refs_1_, ...), custom_call_target="tpu_custom_call" | custom-call | flops 70000001024 | bytes 7000000 | tf_op jit(solution)/shard_map/extractor_feed_back/pallas_call | solution.py:368
  83.7 3.8 %extractor_attention_back.1 = (bf16[16,24,768]{2,1,0:T(8,128)(2,1)S(1)}, bf16[16,24,768]{2,1,0:T(8,128)(2,1)S(1)}, bf16[512,1152]{1,0:T(8,128)(2,1)S(1)}) custom-call(bf16[512,384]{1,0:T(8,128)(2,1)S(1)} %get-tuple-element.141.refs_0_, bf16[384,512]{1,0:T(8,128)(2,1)S(1)} %get-tuple-element.142.refs_1_, bf16[512,1152]{1,0:T(8,128)(2,1)S(1)} %get-tuple-element.143.refs_2_, ...), custom_call_target="tpu_custom_call" | custom-call | flops 60000002048 | bytes 6000000 | tf_op jit(solution)/shard_map/extractor_attention_back/pallas_call | solution.py:368
  88.0 2.4 %collective-permute-done.23.refs_1_ = bf16[8,3,24,768]{3,2,1,0:T(8,128)(2,1)S(1)} collective-permute-done((bf16[8,3,24,768]{3,2,1,0:T(8,128)(2,1)S(1)}, bf16[8,3,24,768]{3,2,1,0:T(8,128)(2,1)S(1)}, u32[]{:S(2)}, u32[]{:S(2)}) %collective-permute-start.23) | collective-permute-done | bytes 884768 | tf_op jit(solution)/shard_map/ppermute | solution.py:464
  90.7 2.9 %collective-permute-start.29 = (bf16[4,3,24,768]{3,2,1,0:T(8,128)(2,1)S(1)}, bf16[4,3,24,768]{3,2,1,0:T(8,128)(2,1)S(1)}, u32[]{:S(2)}, u32[]{:S(2)}) collective-permute-start(bf16[4,3,24,768]{3,2,1,0:T(8,128)(2,1)S(1)} %get-tuple-element.158.refs_11_), channel_id=1, source_target_pairs={{0,8},{1,9},{2,10},{3,11},{4,12},{5,13},{6,14},{7,15},{8,0},{9,1},... | collective-permute-start | bytes 1327112 | tf_op jit(solution)/shard_map/ppermute | solution.py:464
  96.7 10.4 %collective-permute-done.25.refs_1_ = bf16[8,3,24,768]{3,2,1,0:T(8,128)(2,1)S(1)} collective-permute-done((bf16[8,3,24,768]{3,2,1,0:T(8,128)(2,1)S(1)}, bf16[8,3,24,768]{3,2,1,0:T(8,128)(2,1)S(1)}, u32[]{:S(2)}, u32[]{:S(2)}) %collective-permute-start.25) | collective-permute-done | bytes 884768 | tf_op jit(solution)/shard_map/ppermute | solution.py:464
  109.5 2.2 %collective-permute-start.30 = (bf16[2,3,24,768]{3,2,1,0:T(8,128)(2,1)S(1)}, bf16[2,3,24,768]{3,2,1,0:T(8,128)(2,1)S(1)}, u32[]{:S(2)}, u32[]{:S(2)}) collective-permute-start(bf16[2,3,24,768]{3,2,1,0:T(8,128)(2,1)S(1)} %get-tuple-element.171), channel_id=1, source_target_pairs={{0,4},{1,5},{2,6},{3,7},{4,0},{5,1},{6,2},{7,3},{8,12},{9,13},{10,... | collective-permute-start | bytes 663560 | tf_op jit(solution)/shard_map/ppermute | solution.py:464
  111.7 3.9 %collective-permute-done.26.refs_1_ = bf16[4,3,24,768]{3,2,1,0:T(8,128)(2,1)S(1)} collective-permute-done((bf16[4,3,24,768]{3,2,1,0:T(8,128)(2,1)S(1)}, bf16[4,3,24,768]{3,2,1,0:T(8,128)(2,1)S(1)}, u32[]{:S(2)}, u32[]{:S(2)}) %collective-permute-start.26) | collective-permute-done | bytes 442400 | tf_op jit(solution)/shard_map/ppermute | solution.py:464
  115.9 4.0 %collective-permute-done.30.refs_1_ = bf16[2,3,24,768]{3,2,1,0:T(8,128)(2,1)S(1)} collective-permute-done((bf16[2,3,24,768]{3,2,1,0:T(8,128)(2,1)S(1)}, bf16[2,3,24,768]{3,2,1,0:T(8,128)(2,1)S(1)}, u32[]{:S(2)}, u32[]{:S(2)}) %collective-permute-start.30) | collective-permute-done | bytes 221216 | tf_op jit(solution)/shard_map/ppermute | solution.py:464
  120.8 5.5 %collective-permute-done.27.refs_1_ = bf16[2,3,24,768]{3,2,1,0:T(8,128)(2,1)S(1)} collective-permute-done((bf16[2,3,24,768]{3,2,1,0:T(8,128)(2,1)S(1)}, bf16[2,3,24,768]{3,2,1,0:T(8,128)(2,1)S(1)}, u32[]{:S(2)}, u32[]{:S(2)}) %collective-permute-start.27) | collective-permute-done | bytes 221216 | tf_op jit(solution)/shard_map/ppermute | solution.py:464
  126.8 4.5 %collective-permute-done.28.refs_1_ = bf16[1,3,24,768]{3,2,1,0:T(8,128)(2,1)S(1)} collective-permute-done((bf16[1,3,24,768]{3,2,1,0:T(8,128)(2,1)S(1)}, bf16[1,3,24,768]{3,2,1,0:T(8,128)(2,1)S(1)}, u32[]{:S(2)}, u32[]{:S(2)}) %collective-permute-start.28) | collective-permute-done | bytes 110624 | tf_op jit(solution)/shard_map/ppermute | solution.py:464
  134.1 5.8 %all-to-all-start = ((f32[16,3,384]{2,1,0:T(4,128)}), f32[16,3,384]{2,1,0:T(4,128)S(1)}, u32[]{:S(2)}, u32[]{:S(2)}) async-start(f32[16,3,384]{2,1,0:T(4,128)} %get-tuple-element.186), calls=%async_computation | async-start | bytes 196608 | tf_op jit(solution)/shard_map/all_to_all | solution.py:864
  141.2 6.4 %all-to-all-done.refs_0_ = f32[16,3,384]{2,1,0:T(4,128)S(1)} async-done(((f32[16,3,384]{2,1,0:T(4,128)}), f32[16,3,384]{2,1,0:T(4,128)S(1)}, u32[]{:S(2)}, u32[]{:S(2)}) %all-to-all-start) | async-done | bytes 73760 | tf_op jit(solution)/shard_map/all_to_all | solution.py:864
  (153 shorter events, 42.0 us)
Async XLA Ops:
  4.3 7.4 %collective-permute-start.1 = (bf16[1,24,1536]{2,1,0:T(8,128)(2,1)S(1)}, bf16[1,24,1536]{2,1,0:T(8,128)(2,1)S(1)}, u32[]{:S(2)}, u32[]{:S(2)}) collective-permute-start(bf16[1,24,1536]{2,1,0:T(8,128)(2,1)S(1)} %bitcast.70), channel_id=1, source_target_pairs={{0,8},{1,9},{2,10},{3,11},{4,12},{5,13},{6,14},{7,15},{8,0},{9,1},... | collective-permute-start | bytes 221192 | tf_op jit(solution)/shard_map/ppermute | solution.py:464
  8.4 6.4 %collective-permute-start.4 = (bf16[1,24,1536]{2,1,0:T(8,128)(2,1)S(1)}, bf16[1,24,1536]{2,1,0:T(8,128)(2,1)S(1)}, u32[]{:S(2)}, u32[]{:S(2)}) collective-permute-start(bf16[1,24,1536]{2,1,0:T(8,128)(2,1)S(1)} %bitcast.68), channel_id=1, source_target_pairs={{0,2},{1,3},{2,0},{3,1},{4,6},{5,7},{6,4},{7,5},{8,10},{9,11},{10,... | collective-permute-start | bytes 221192 | tf_op jit(solution)/shard_map/ppermute | solution.py:464
  9.9 8.5 %collective-permute-start.3 = (bf16[1,4,24,384]{3,2,1,0:T(8,128)(2,1)S(1)}, bf16[1,4,24,384]{3,2,1,0:T(8,128)(2,1)S(1)}, u32[]{:S(2)}, u32[]{:S(2)}) collective-permute-start(bf16[1,4,24,384]{3,2,1,0:T(8,128)(2,1)S(1)} %bitcast.66), channel_id=1, source_target_pairs={{0,8},{1,9},{2,10},{3,11},{4,12},{5,13},{6,14},{7,15},{8,0},{9,1},... | collective-permute-start | bytes 221192 | tf_op jit(solution)/shard_map/ppermute | solution.py:464
  11.7 8.3 %collective-permute-start.2 = (bf16[2,24,1536]{2,1,0:T(8,128)(2,1)S(1)}, bf16[2,24,1536]{2,1,0:T(8,128)(2,1)S(1)}, u32[]{:S(2)}, u32[]{:S(2)}) collective-permute-start(bf16[2,24,1536]{2,1,0:T(8,128)(2,1)S(1)} %join.9.refs_2_.refs_0_), channel_id=1, source_target_pairs={{0,4},{1,5},{2,6},{3,7},{4,0},{5,1},{6,2},{7,3},{8,12},{9,13},{10,... | collective-permute-start | bytes 442376 | tf_op jit(solution)/shard_map/ppermute | solution.py:464
  14.8 8.4 %collective-permute-start.7 = (bf16[2,24,1536]{2,1,0:T(8,128)(2,1)S(1)}, bf16[2,24,1536]{2,1,0:T(8,128)(2,1)S(1)}, u32[]{:S(2)}, u32[]{:S(2)}) collective-permute-start(bf16[2,24,1536]{2,1,0:T(8,128)(2,1)S(1)} %join.10.refs_2_.refs_0_), channel_id=1, source_target_pairs={{0,8},{1,9},{2,10},{3,11},{4,12},{5,13},{6,14},{7,15},{8,0},{9,1},... | collective-permute-start | bytes 442376 | tf_op jit(solution)/shard_map/ppermute | solution.py:464
  18.4 7.7 %collective-permute-start.6 = (bf16[2,4,24,384]{3,2,1,0:T(8,128)(2,1)S(1)}, bf16[2,4,24,384]{3,2,1,0:T(8,128)(2,1)S(1)}, u32[]{:S(2)}, u32[]{:S(2)}) collective-permute-start(bf16[2,4,24,384]{3,2,1,0:T(8,128)(2,1)S(1)} %join.11.refs_2_.refs_0_), channel_id=1, source_target_pairs={{0,2},{1,3},{2,0},{3,1},{4,6},{5,7},{6,4},{7,5},{8,10},{9,11},{10,... | collective-permute-start | bytes 442376 | tf_op jit(solution)/shard_map/ppermute | solution.py:464
  20.0 9.9 %collective-permute-start.5 = (bf16[4,24,1536]{2,1,0:T(8,128)(2,1)S(1)}, bf16[4,24,1536]{2,1,0:T(8,128)(2,1)S(1)}, u32[]{:S(2)}, u32[]{:S(2)}) collective-permute-start(bf16[4,24,1536]{2,1,0:T(8,128)(2,1)S(1)} %join.12.refs_2_.refs_0_), channel_id=1, source_target_pairs={{0,2},{1,3},{2,0},{3,1},{4,6},{5,7},{6,4},{7,5},{8,10},{9,11},{10,... | collective-permute-start | bytes 884744 | tf_op jit(solution)/shard_map/ppermute | solution.py:464
  23.3 7.6 %collective-permute-start.11 = (bf16[4,24,1536]{2,1,0:T(8,128)(2,1)S(1)}, bf16[4,24,1536]{2,1,0:T(8,128)(2,1)S(1)}, u32[]{:S(2)}, u32[]{:S(2)}) collective-permute-start(bf16[4,24,1536]{2,1,0:T(8,128)(2,1)S(1)} %join.13.refs_2_.refs_0_), channel_id=1, source_target_pairs={{0,4},{1,5},{2,6},{3,7},{4,0},{5,1},{6,2},{7,3},{8,12},{9,13},{10,... | collective-permute-start | bytes 884744 | tf_op jit(solution)/shard_map/ppermute | solution.py:464
  26.2 6.9 %collective-permute-start.15 = (bf16[4,4,24,384]{3,2,1,0:T(8,128)(2,1)S(1)}, bf16[4,4,24,384]{3,2,1,0:T(8,128)(2,1)S(1)}, u32[]{:S(2)}, u32[]{:S(2)}) collective-permute-start(bf16[4,4,24,384]{3,2,1,0:T(8,128)(2,1)S(1)} %join.14.refs_2_.refs_0_), channel_id=1, source_target_pairs={{0,1},{1,0},{2,3},{3,2},{4,5},{5,4},{6,7},{7,6},{8,9},{9,8},{10,11... | collective-permute-start | bytes 884744 | tf_op jit(solution)/shard_map/ppermute | solution.py:464
  33.2 11.5 %collective-permute-start.16 = (bf16[8,4,24,384]{3,2,1,0:T(8,128)(2,1)S(1)}, bf16[8,4,24,384]{3,2,1,0:T(8,128)(2,1)S(1)}, u32[]{:S(2)}, u32[]{:S(2)}) collective-permute-start(bf16[8,4,24,384]{3,2,1,0:T(8,128)(2,1)S(1)} %join.17.refs_0_), channel_id=1, source_target_pairs={{0,4},{1,5},{2,6},{3,7},{4,0},{5,1},{6,2},{7,3},{8,12},{9,13},{10,... | collective-permute-start | bytes 1769480 | tf_op jit(solution)/shard_map/ppermute | solution.py:464
  33.2 12.0 %collective-permute-start.12 = (bf16[8,24,1536]{2,1,0:T(8,128)(2,1)S(1)}, bf16[8,24,1536]{2,1,0:T(8,128)(2,1)S(1)}, u32[]{:S(2)}, u32[]{:S(2)}) collective-permute-start(bf16[8,24,1536]{2,1,0:T(8,128)(2,1)S(1)} %join.16.refs_0_.refs_2_), channel_id=1, source_target_pairs={{0,1},{1,0},{2,3},{3,2},{4,5},{5,4},{6,7},{7,6},{8,9},{9,8},{10,11... | collective-permute-start | bytes 1769480 | tf_op jit(solution)/shard_map/ppermute | solution.py:464
  35.3 9.9 %collective-permute-start.17 = (bf16[8,4,24,384]{3,2,1,0:T(8,128)(2,1)S(1)}, bf16[8,4,24,384]{3,2,1,0:T(8,128)(2,1)S(1)}, u32[]{:S(2)}, u32[]{:S(2)}) collective-permute-start(bf16[8,4,24,384]{3,2,1,0:T(8,128)(2,1)S(1)} %join.17.refs_0_), channel_id=1, source_target_pairs={{0,16},{16,0},{1,17},{17,1},{2,18},{18,2},{3,19},{19,3},{4,20},{20... | collective-permute-start | bytes 1769480 | tf_op jit(solution)/shard_map/ppermute | solution.py:458
  35.3 14.2 %collective-permute-start.8 = (bf16[8,24,1536]{2,1,0:T(8,128)(2,1)S(1)}, bf16[8,24,1536]{2,1,0:T(8,128)(2,1)S(1)}, u32[]{:S(2)}, u32[]{:S(2)}) collective-permute-start(bf16[8,24,1536]{2,1,0:T(8,128)(2,1)S(1)} %join.15.refs_0_.refs_2_), channel_id=1, source_target_pairs={{0,1},{1,0},{2,3},{3,2},{4,5},{5,4},{6,7},{7,6},{8,9},{9,8},{10,11... | collective-permute-start | bytes 1769480 | tf_op jit(solution)/shard_map/ppermute | solution.py:464
  77.4 13.1 %collective-permute-start.23 = (bf16[8,3,24,768]{3,2,1,0:T(8,128)(2,1)S(1)}, bf16[8,3,24,768]{3,2,1,0:T(8,128)(2,1)S(1)}, u32[]{:S(2)}, u32[]{:S(2)}) collective-permute-start(bf16[8,3,24,768]{3,2,1,0:T(8,128)(2,1)S(1)} %get-tuple-element.140.refs_9_), channel_id=1, source_target_pairs={{0,1},{1,0},{2,3},{3,2},{4,5},{5,4},{6,7},{7,6},{8,9},{9,8},{10,11... | collective-permute-start | bytes 2654216 | tf_op jit(solution)/shard_map/ppermute | solution.py:464
  83.6 9.9 %collective-permute-start.22 = (bf16[16,2,24,768]{3,2,1,0:T(8,128)(2,1)S(1)}, bf16[16,2,24,768]{3,2,1,0:T(8,128)(2,1)S(1)}, u32[]{:S(2)}, u32[]{:S(2)}) collective-permute-start(bf16[16,2,24,768]{3,2,1,0:T(8,128)(2,1)S(1)} %get-tuple-element.155), channel_id=1, source_target_pairs={{0,16},{16,0},{1,17},{17,1},{2,18},{18,2},{3,19},{19,3},{4,20},{20... | collective-permute-start | bytes 3538952 | tf_op jit(solution)/shard_map/ppermute | solution.py:458
  87.5 6.1 %collective-permute-start.21 = (bf16[16,24,768]{2,1,0:T(8,128)(2,1)S(1)}, bf16[16,24,768]{2,1,0:T(8,128)(2,1)S(1)}, u32[]{:S(2)}, u32[]{:S(2)}) collective-permute-start(bf16[16,24,768]{2,1,0:T(8,128)(2,1)S(1)} %get-tuple-element.153), channel_id=1, source_target_pairs={{0,16},{16,0},{1,17},{17,1},{2,18},{18,2},{3,19},{19,3},{4,20},{20... | collective-permute-start | bytes 1769480 | tf_op jit(solution)/shard_map/ppermute | solution.py:458
  90.7 18.5 %collective-permute-start.29 = (bf16[4,3,24,768]{3,2,1,0:T(8,128)(2,1)S(1)}, bf16[4,3,24,768]{3,2,1,0:T(8,128)(2,1)S(1)}, u32[]{:S(2)}, u32[]{:S(2)}) collective-permute-start(bf16[4,3,24,768]{3,2,1,0:T(8,128)(2,1)S(1)} %get-tuple-element.158.refs_11_), channel_id=1, source_target_pairs={{0,8},{1,9},{2,10},{3,11},{4,12},{5,13},{6,14},{7,15},{8,0},{9,1},... | collective-permute-start | bytes 1327112 | tf_op jit(solution)/shard_map/ppermute | solution.py:464
  94.0 13.1 %collective-permute-start.25 = (bf16[8,3,24,768]{3,2,1,0:T(8,128)(2,1)S(1)}, bf16[8,3,24,768]{3,2,1,0:T(8,128)(2,1)S(1)}, u32[]{:S(2)}, u32[]{:S(2)}) collective-permute-start(bf16[8,3,24,768]{3,2,1,0:T(8,128)(2,1)S(1)} %get-tuple-element.156.refs_10_), channel_id=1, source_target_pairs={{0,2},{1,3},{2,0},{3,1},{4,6},{5,7},{6,4},{7,5},{8,10},{9,11},{10,... | collective-permute-start | bytes 2654216 | tf_op jit(solution)/shard_map/ppermute | solution.py:464
  107.3 8.4 %collective-permute-start.26 = (bf16[4,3,24,768]{3,2,1,0:T(8,128)(2,1)S(1)}, bf16[4,3,24,768]{3,2,1,0:T(8,128)(2,1)S(1)}, u32[]{:S(2)}, u32[]{:S(2)}) collective-permute-start(bf16[4,3,24,768]{3,2,1,0:T(8,128)(2,1)S(1)} %get-tuple-element.164), channel_id=1, source_target_pairs={{0,1},{1,0},{2,3},{3,2},{4,5},{5,4},{6,7},{7,6},{8,9},{9,8},{10,11... | collective-permute-start | bytes 1327112 | tf_op jit(solution)/shard_map/ppermute | solution.py:464
  109.2 30.7 %collective-permute-start.24 = (f32[512,384]{1,0:T(8,128)S(1)}, f32[512,384]{1,0:T(8,128)S(1)}, u32[]{:S(2)}, u32[]{:S(2)}) collective-permute-start(f32[512,384]{1,0:T(8,128)S(1)} %get-tuple-element.160), channel_id=1, source_target_pairs={{0,16},{16,0},{1,17},{17,1},{2,18},{18,2},{3,19},{19,3},{4,20},{20... | collective-permute-start | bytes 2359304 | tf_op jit(solution)/shard_map/ppermute | solution.py:458
  109.5 10.4 %collective-permute-start.30 = (bf16[2,3,24,768]{3,2,1,0:T(8,128)(2,1)S(1)}, bf16[2,3,24,768]{3,2,1,0:T(8,128)(2,1)S(1)}, u32[]{:S(2)}, u32[]{:S(2)}) collective-permute-start(bf16[2,3,24,768]{3,2,1,0:T(8,128)(2,1)S(1)} %get-tuple-element.171), channel_id=1, source_target_pairs={{0,4},{1,5},{2,6},{3,7},{4,0},{5,1},{6,2},{7,3},{8,12},{9,13},{10,... | collective-permute-start | bytes 663560 | tf_op jit(solution)/shard_map/ppermute | solution.py:464
  115.8 10.6 %collective-permute-start.27 = (bf16[2,3,24,768]{3,2,1,0:T(8,128)(2,1)S(1)}, bf16[2,3,24,768]{3,2,1,0:T(8,128)(2,1)S(1)}, u32[]{:S(2)}, u32[]{:S(2)}) collective-permute-start(bf16[2,3,24,768]{3,2,1,0:T(8,128)(2,1)S(1)} %get-tuple-element.166), channel_id=1, source_target_pairs={{0,8},{1,9},{2,10},{3,11},{4,12},{5,13},{6,14},{7,15},{8,0},{9,1},... | collective-permute-start | bytes 663560 | tf_op jit(solution)/shard_map/ppermute | solution.py:464
  120.0 6.8 %collective-permute-start.31 = (bf16[1,3,24,768]{3,2,1,0:T(8,128)(2,1)S(1)}, bf16[1,3,24,768]{3,2,1,0:T(8,128)(2,1)S(1)}, u32[]{:S(2)}, u32[]{:S(2)}) collective-permute-start(bf16[1,3,24,768]{3,2,1,0:T(8,128)(2,1)S(1)} %get-tuple-element.173), channel_id=1, source_target_pairs={{0,2},{1,3},{2,0},{3,1},{4,6},{5,7},{6,4},{7,5},{8,10},{9,11},{10,... | collective-permute-start | bytes 331784 | tf_op jit(solution)/shard_map/ppermute | solution.py:464
  134.1 13.5 %all-to-all-start = ((f32[16,3,384]{2,1,0:T(4,128)}), f32[16,3,384]{2,1,0:T(4,128)S(1)}, u32[]{:S(2)}, u32[]{:S(2)}) async-start(f32[16,3,384]{2,1,0:T(4,128)} %get-tuple-element.186), calls=%async_computation | async-start | bytes 196608 | tf_op jit(solution)/shard_map/all_to_all | solution.py:864
  (47 other events, 410.0 us)

commit v3 on v2

--- a/solution.py
+++ b/solution.py
@@ -254,11 +254,11 @@
         rest = tuple(range(4, self.bits))
         x, y, near, far = 0, 1, 2, 3
         gathers = (
-            ((far, near, y, x), (far, x, near, y)),
-            ((y, far, near, x), (near, far, x, y)),
-            ((far, y, x, near), (far, x, y, near)),
-        )
-        scatters = (((y, x, far, near), (x, y, near, far)), ((x, far, near, y), (y, near, far, x)))
+            ((y, far, x, near), (far, near, y, x)),
+            ((near, x, far, y), (far, x, near, y)),
+            ((near, far, y, x), (far, x, y, near)),
+        )
+        scatters = (((y, x, near, far), (near, y, x, far)), ((near, x, y, far), (y, x, far, near)))
         self.gather_orders = tuple(tuple(rest + o for o in pair) for pair in gathers)
         self.scatter_orders = tuple(tuple(o + rest for o in pair) for pair in scatters)
         self.thin = (D // self.count) % 8 != 0
@@ -279,7 +279,7 @@
         if self.thin:
             return {"gp_": [((D, WIDE), BF)], "gq_": [((D, WIDE), BF), ((FF, D), BF)]}
         n, r = self.slabs, self.rows
-        return {"gp_": [((n, r, HALF), BF)] * 2, "gq_": [((n, 2, r, HALF), BF)] * 2}
+        return {"gp_": [((n, 1, r, HALF), BF)] * 2, "gq_": [((n, 2, r, HALF), BF)] * 2}
 
 
 class Emit:
@@ -311,7 +311,7 @@
         shape = (plan.slabs, plan.rows, D)
 
         def put(which, place, value):
-            self.first[which][place, :, at : at + D] = value
+            self.first[which][place, 0, :, at : at + D] = value
 
         self.halves(zero.reshape(shape), one.reshape(shape), put)
 
@@ -373,7 +373,7 @@
         out_specs=[VM] * len(outs),
         scratch_shapes=[pltpu.VMEM(*v) for v in scratch.values()],
         compiler_params=limit(size),
-        cost_estimate=pl.CostEstimate(flops=int(cost * 1e10), bytes_accessed=int(cost * 1e6), transcendentals=0),
+        cost_estimate=pl.CostEstimate(flops=int(cost * 1e10), bytes_accessed=8, transcendentals=0),
     )(*[v for v, _ in arrays.values()], *after)
     return dict(zip(outs, result))
 
@@ -489,26 +489,20 @@
     return (a.astype(F32) + b.astype(F32)).astype(BF)
 
 
-def add_first(first, second, after=()):
-    def kernel(a, b, c, d, *outs):
-        n = outs[0].shape[0]
-        for i, out in enumerate(outs):
-            for j in range(n):
-                out[j, 0] = added(a[n * i + j], b[n * i + j])
-                out[j, 1:3] = added(c[n * i + j], d[n * i + j])
-
-    n, r, width = first[0].shape
-    return small_kernel("add_first", kernel, [struct((n // 2, 3, r, width), BF)] * 2, *first, *second, after=after)
-
-
-def add_split(a, b, after=()):
-    def kernel(a, b, *outs):
-        n = outs[0].shape[0]
-        for i, out in enumerate(outs):
-            for j in range(n):
-                out[j] = added(a[n * i + j], b[n * i + j])
-
-    return small_kernel("add_split", kernel, [struct((a.shape[0] // 2, *a.shape[1:]), BF)] * 2, a, b, after=after)
+def add_split(pairs, after=()):
+    def kernel(*refs):
+        outs, n, at = refs[-2:], refs[-1].shape[0], 0
+        for k in range(0, len(refs) - 2, 2):
+            a, b = refs[k : k + 2]
+            wide = a.shape[1]
+            for i, out in enumerate(outs):
+                for j in range(n):
+                    out[j, at : at + wide] = added(a[n * i + j], b[n * i + j])
+            at += wide
+
+    n, _, r, width = pairs[0][0].shape
+    outs = [struct((n // 2, sum(a.shape[1] for a, _ in pairs), r, width), BF)] * 2
+    return small_kernel("add_split", kernel, outs, *[v for pair in pairs for v in pair], after=after)
 
 
 def behind(value, *others):
@@ -516,29 +510,32 @@
 
 
 class Scatter:
-    def __init__(self, plan, block, first, second):
+    def __init__(self, plan, block, *halves):
         self.orders, self.turn = plan.scatter_orders[block], 0
-        self.keep, self.send = add_first(first, second)
-
-    def came(self, *after):
-        send = behind(self.send, *after) if after else self.send
-        value = swap(send, (self.orders[0][self.turn], self.orders[1][self.turn]))
+        self.pairs = [(mine, swap_cores(other)) for mine, other in halves]
+
+    def step(self, *after):
+        keep, send = add_split(self.pairs, after)
+        self.pairs = [(keep, swap(send, (self.orders[0][self.turn], self.orders[1][self.turn])))]
         self.turn += 1
-        return value
-
-    def step(self, start_after=(), end_after=()):
-        self.keep, self.send = add_split(self.keep, self.came(*start_after), end_after)
+        return keep
 
 
 def owners(zero, one):
-    def kernel(a, b, c, d, own, send):
+    zero, one = ([pair for sums in v for pair in sums.pairs] for v in (zero, one))
+
+    def total(refs):
+        return jnp.concatenate([a[0].astype(F32) + b[0].astype(F32) for a, b in zip(refs[0::2], refs[1::2])], 0)
+
+    def kernel(*refs):
+        own, send = refs[-2:]
+        a, b = total(refs[: 2 * len(zero)]), total(refs[2 * len(zero) : -2])
         leading = lax.axis_index("pipe") == 0
-        zero, one = a[0].astype(F32) + b[0].astype(F32), c[0].astype(F32) + d[0].astype(F32)
-        own[...] = jnp.where(leading, zero, one).astype(BF)
-        send[...] = jnp.where(leading, one, zero).astype(BF)
-
-    like = struct(zero[0].shape[1:], BF)
-    return small_kernel("owners", kernel, [like, like], *zero, *one)
+        own[...] = jnp.where(leading, a, b).astype(BF)
+        send[...] = jnp.where(leading, b, a).astype(BF)
+
+    like = struct((3, *zero[0][0].shape[2:]), BF)
+    return small_kernel("owners", kernel, [like, like], *[v for pair in zero + one for v in pair])
 
 
 def thin_arrange(plan, flow, own, got):
@@ -556,9 +553,10 @@
     core, me = lax.axis_index("pipe"), lax.axis_index("dp")
     n, r = plan.count, D // plan.count
     parts = grads[0].reshape(n, r, 2, HALF).transpose(2, 0, 1, 3)
+    parts = parts[:, :, None]
     if bundle:
-        down = grads[1].reshape(n, 2, 2, r, D).transpose(1, 0, 3, 2, 4).reshape(2, n, r, HALF)
-        parts = jnp.stack([parts, down], 2)
+        down = grads[1].reshape(n, 2, 2, r, D).transpose(1, 0, 3, 2, 4).reshape(2, n, 1, r, HALF)
+        parts = jnp.concatenate([parts, down], 2)
     index = jnp.arange(n, dtype=jnp.int32)
     halves = [jnp.zeros_like(parts[h]).at[plan.place(block, h, index, me)].set(parts[h]) for h in (0, 1)]
     return [jnp.where(core == 0, halves[i], halves[1 - i]) for i in (0, 1)]
@@ -584,27 +582,12 @@
     return (drift, spread, update)
 
 
-def prepare(plan, masters):
+def update_moments(plan, own, got, masters, firsts, seconds, gain_own, gain_got):
     r = D // plan.count
 
-    def kernel(wi, wo, wu, wd, wide, up, down, row):
-        wide[:, : 3 * D] = wi[...].astype(BF)
-        wide[:, 3 * D :] = wo[...].astype(BF)
-        up[...] = wu[...].astype(BF)
-        for q in range(4):
-            down[q] = wd[r * q : r * q + r, :].astype(BF)
-        row[...] = lanes([(i, square_sum(m[...])) for i, m in enumerate((wi, wo, wu, wd))])
-
-    outs = [struct((r, WIDE), BF), struct((r, WIDE), BF), struct((4, r, D), BF), struct((1, D), F32)]
-    return small_kernel("prepare", kernel, outs, *masters)
-
-
-def update_moments(plan, own, got, masters, firsts, seconds, weight_row, gain_own, gain_got):
-    r = D // plan.count
-
     def kernel(own, got, *refs):
-        masters, firsts, seconds, (weight_row, gain_own, gain_got) = refs[0:4], refs[4:8], refs[8:12], refs[12:15]
-        drifts, spreads, updates, small = refs[15:19], refs[19:23], refs[23:27], refs[27]
+        masters, firsts, seconds, (gain_own, gain_got) = refs[0:4], refs[4:8], refs[8:12], refs[12:14]
+        drifts, spreads, updates, small = refs[14:18], refs[18:22], refs[22:26], refs[26]
         leading = lax.axis_index("pipe") == 0
         a, b = own[...].astype(F32), got[...].astype(F32)
         h = (jnp.where(leading, a, b), jnp.where(leading, b, a))
@@ -619,7 +602,7 @@
                 for q in (0, 1)
             ],
         ]
-        sums = []
+        sums = [(m, square_sum(masters[m][...])) for m in range(4)]
         for m in range(4):
             total = jnp.zeros((1, 1), F32)
             for at, grad in grads[m]:
@@ -627,7 +610,7 @@
                 drifts[m][at], spreads[m][at], updates[m][at] = drift, spread, update
                 total = total + square_sum(update)
             sums.append((4 + m, total))
-        row = lanes(sums) + weight_row[...]
+        row = lanes(sums)
         gain = gain_own[...] + gain_got[...]
         for i in range(plan.count):
             small[i, 0:1, :] = row
@@ -635,7 +618,7 @@
 
     like = [struct(m.shape, F32) for m in masters]
     outs = like * 3 + [struct((plan.count, 3, D), F32)]
-    res = small_kernel("moments", kernel, outs, own, got, *masters, *firsts, *seconds, weight_row, gain_own, gain_got)
+    res = small_kernel("moments", kernel, outs, own, got, *masters, *firsts, *seconds, gain_own, gain_got)
     return res[0:4], res[4:8], res[8:12], res[12]
 
 
@@ -656,23 +639,26 @@
         gain_step = jnp.sqrt(jnp.sum(update * update, axis=1, keepdims=True))
         gain_new[...] = gains[...] - rate * (gain_weight / gain_step) * update
         for i in range(4):
-            pairs[i : i + 1, 0:1] = weight[i]
-            pairs[i : i + 1, 1:2] = step[i]
-        pairs[4:6, 0:1] = gain_weight
-        pairs[4:6, 1:2] = gain_step
+            pairs[0:1, i : i + 1] = weight[i]
+            pairs[1:2, i : i + 1] = step[i]
+        for i in range(2):
+            pairs[0:1, 4 + i : 5 + i] = gain_weight[i : i + 1, :]
+            pairs[1:2, 4 + i : 5 + i] = gain_step[i : i + 1, :]
 
     outs = [struct(m.shape, F32) for m in masters] + [struct(m.shape, BF) for m in masters]
-    outs += [struct((2, D), F32)] * 3 + [struct((6, 2), F32)]
-    return small_kernel("finish", kernel, outs, small, *masters, *updates, gains, gain_first, gain_second)
+    outs += [struct((2, D), F32)] * 3 + [struct((2, 6), F32)]
+    res = small_kernel("finish", kernel, outs, small, *masters, *updates, gains, gain_first, gain_second)
+    return [*res[:-1], res[-1].T]
 
 
 def lay_results(own, got):
-    def kernel(own, got, out):
+    def kernel(own, got, out, done):
         core = lax.axis_index("pipe")
         out[core] = own[...]
         out[1 - core] = got[...]
-
-    return small_kernel("lay_results", kernel, [struct((2, *own.shape), F32)], own, got)[0]
+        done[...] = jnp.zeros(done.shape, F32)
+
+    return small_kernel("lay_results", kernel, [struct((2, *own.shape), F32), struct((8, 128), F32)], own, got)
 
 
 def solution(mesh):
@@ -705,12 +691,20 @@
         firsts = (first_in[0], first_out[0], first_up[0], first_down[0])
         seconds = (second_in[0], second_out[0], second_up[0], second_down[0])
 
-        wide, up, down, weight_row = prepare(plan, masters)
-        flows = gather(plan, (wide, up, down))
-        got = [tuple(swap_cores(v) for v in pieces) for pieces in flows]
+        low = [m.astype(BF) for m in masters]
+        wide = jnp.concatenate(low[:2], 1)
+        flows = gather(plan, (wide, low[2], low[3].reshape(4, -1, D)))
         gains_got = swap_cores(gains[0])
         put = thin_arrange if plan.thin else arrange
-        both = [put(plan, f, flows[f], got[f]) for f in range(3)]
+        both = [None] * 3
+
+        def place_flow(flow, *after):
+            first, second = flows[flow]
+            if after:
+                second = behind(second, *after)
+            both[flow] = put(plan, flow, (first, second), (swap_cores(first), swap_cores(second)))
+
+        place_flow(0)
 
         def weights(block, *which):
             return {n: both[f][block] for f, n in enumerate(("wide", "up", "down")) if n in which}
@@ -731,11 +725,9 @@
         def refs_of(k, table):
             return [k[n] for n in table]
 
-        def traded(source, table, block, bundle):
+        def halves(source, table, block, bundle):
             values = [source[n] for n in table]
-            if plan.thin:
-                values = thin_halves(plan, block, values, bundle)
-            return values[0], swap_cores(values[1])
+            return thin_halves(plan, block, values, bundle) if plan.thin else values
 
         def body(k, gain):
             attention_half(k["x"], k, k["wide"], gain, L)
@@ -743,8 +735,11 @@
         attention_scratch = pick("q2", "vT", "bias", "ss")
         one = run_kernel(
             "extractor_attention", body, 0, {**gain_refs, **x0, **seg, **weights(0, "wide")},
-            pick("n1", "pk", "pt", "attT", "mid", "n2"), attention_scratch, 6,
-        )
+            pick("n1", "pk", "pt", "attT", "mid", "n2"), attention_scratch, 1e-9,
+        )
+
+        place_flow(1)
+        place_flow(2)
 
         def body(k, gain):
             def out(value):
@@ -755,7 +750,7 @@
         two = run_kernel(
             "extractor_feed", body, 0,
             {**there(one, "n2", "mid"), "pr": (prompts, ("core", 0)), **weights(0, "up", "down")},
-            pick("act", "gp", "x1"), pick("hs"), 4,
+            pick("act", "gp", "x1"), pick("hs"), 1e-9,
         )
 
         def body(k, gain):
@@ -763,7 +758,7 @@
 
         three = run_kernel(
             "generator_attention", body, 1, {**gain_refs, **there(two, "x1"), **seg, **weights(1, "wide")},
-            pick("n1", "pk", "pt", "attT", "mid", "n2"), attention_scratch, 6,
+            pick("n1", "pk", "pt", "attT", "mid", "n2"), attention_scratch, 1e-9,
         )
 
         def body(k, gain):
@@ -792,9 +787,6 @@
             {**there(four, "dmb"), **there(three, "attT", "pk", "pt", "n1"), **weights(1, "wide")},
             {**g_first, **pick("dpk")}, back_scratch, 6,
         )
-
-        second_one = traded(four, g_second, 1, 1)
-
         def body(k, gain):
             k["dg"][...] = input_back(k["x1"], k, k["wide"], gain, None, k["dxb"])
 
@@ -803,7 +795,8 @@
             {**gain_refs, **there(five, "dpk"), **there(four, "dmid"), **there(two, "x1"), **weights(1, "wide")},
             pick("dg", "dxb"), pick("dn"), 3,
         )
-        sum_one = Scatter(plan, 1, traded(five, g_first, 1, 0), second_one)
+        sum_one = Scatter(plan, 1, halves(five, g_first, 1, 0), halves(four, g_second, 1, 1))
+        last = sum_one.step(six["dxb"])
 
         def body(k, gain):
             emit = Emit(plan, 0, None, refs_of(k, g_second))
@@ -812,9 +805,8 @@
         seven = run_kernel(
             "extractor_feed_back", body, 0,
             {**gain_refs, **there(six, "dxb"), **there(two, "act", "gp"), **there(one, "n2", "mid"), **weights(0, "up", "down")},
-            {**g_second, **pick("dmid", "dmb", "dg")}, pick("dh", "dn"), 7, after=[sum_one.send],
-        )
-        second_zero = traded(seven, g_second, 0, 1)
+            {**g_second, **pick("dmid", "dmb", "dg")}, pick("dh", "dn"), 7, after=[last],
+        )
 
         def body(k, gain):
             emit = Emit(plan, 0, refs_of(k, g_first), None)
@@ -825,8 +817,9 @@
             {**there(seven, "dmb"), **there(one, "attT", "pk", "pt", "n1"), **weights(0, "wide")},
             {**g_first, **pick("dpk")}, back_scratch, 6,
         )
-        sum_one.step(end_after=[eight["dpk"]])
-        sum_zero = Scatter(plan, 0, traded(eight, g_first, 0, 0), second_zero)
+        sum_zero = Scatter(plan, 0, halves(eight, g_first, 0, 0), halves(seven, g_second, 0, 1))
+        last = sum_one.step(eight["dpk"])
+        last = sum_zero.step(last)
 
         def body(k, gain):
             dg = input_back(k["x"], k, k["wide"], gain, k["dx"], None)
@@ -842,24 +835,24 @@
             {**gain_refs, **there(eight, "dpk"), **there(seven, "dmid"), **x0, **weights(0, "wide"), **there(four, "y2"),
              "g01": seven["dg"], "g10": six["dg"], "g11": four["dg"]},
             {"own": sh["dx"], "send": sh["dx"], "gain_own": ((2, D), F32), "gain_send": ((2, D), F32)},
-            pick("dn", "dx"), 3, after=[sum_zero.send, sum_one.send],
-        )
-        token = [nine["gain_own"]]
-        sum_one.step(end_after=token)
-        sum_zero.step(end_after=token)
-        for turn in range(plan.bits - 3):
-            sum_one.step()
-            sum_zero.step()
-        sum_zero.step()
-        zero = sum_zero.keep, sum_zero.came()
-        one = sum_one.keep, sum_one.came()
-        own, send = owners(zero, one)
+            pick("dn", "dx"), 3, after=[last],
+        )
+        gain_got = swap_cores(nine["gain_send"])
+        result, laid = lay_results(nine["own"], swap_cores(nine["send"]))
+        section_result = result[None, :, None]
+        last = sum_one.step(nine["gain_own"])
+        last = sum_zero.step(last, gain_got)
+        beside = (laid,)
+        while sum_zero.turn < plan.bits:
+            if sum_one.turn < plan.bits:
+                last = sum_one.step(last)
+            last = sum_zero.step(last, *beside)
+            beside = ()
+        own, send = owners((sum_zero,), (sum_one,))
         grad_got = swap_cores(send)
 
-        result = lay_results(nine["own"], swap_cores(nine["send"]))
-        section_result = result[None, :, None]
         drifts, spreads, updates, small = update_moments(
-            plan, own, grad_got, masters, firsts, seconds, weight_row, nine["gain_own"], swap_cores(nine["gain_send"])
+            plan, own, grad_got, masters, firsts, seconds, nine["gain_own"], gain_got
         )
         small = lax.all_to_all(small, "dp", 0, 0)
         done = finish(small, masters, updates, gains[0], gain_first[0], gain_second[0])

time: 150 us -> 143 us (0.953)
  starting transfers between devices: 43.4 us -> 25.1 us
  blocking collectives: 0 us -> 11.3 us
  other arithmetic: 0 us -> 3.52 us
  local copies, waits for them, and re-layouts: 4.6 us -> 2.24 us
  waiting for transfers between devices: 62.7 us -> 61.2 us
    ppermute x20, starting transfers between devices: 34.3 us -> 21.7 us  [swap(): return lax.ppermute(block, ('pipe', 'dp'), route)]
    all_to_all x0 -> x1, blocking collectives: none -> 11.3 us  [per_device(): small = lax.all_to_all(small, 'dp', 0, 0)]
    all_to_all x1 -> x0, waiting for transfers between devices: 6.37 us -> none  [per_device(): small = lax.all_to_all(small, 'dp', 0, 0)]
    all_to_all x1 -> x0, starting transfers between devices: 5.83 us -> none  [per_device(): small = lax.all_to_all(small, 'dp', 0, 0)]
    convert_element_type x0 -> x4, other arithmetic: none -> 3.52 us  [per_device(): low = [m.astype(BF) for m in masters]]
    ppermute x14, waiting for transfers between devices: 3.97 us -> 6.84 us  [swap_cores(): return lax.ppermute(block, 'pipe', [(0, 1), (1, 0)])]
    ppermute x20, waiting for transfers between devices: 52.4 us -> 54.4 us  [swap(): return lax.ppermute(block, ('pipe', 'dp'), route)]
    unnamed x72 -> x64, local copies, waits for them, and re-layouts: 3.95 us -> 2.24 us
  transfers between devices with their start and end apart: 35 -> 34, of which waited for: 18 -> 21; matrix products, arithmetic and copies ran while one was open for 0% -> 1% of each run, Pallas kernels for 10% -> 9%
where the time goes in v3:
time: 143 us
  waiting for transfers between devices  61.2 us (43%)
  Pallas kernels  37.5 us (26%)
  starting transfers between devices  25.1 us (18%)
  blocking collectives  11.3 us (8%)
  other arithmetic  3.52 us (2%)
  local copies, waits for them, and re-layouts  2.24 us (2%)
  between operations  1.5 us (1%)
    ppermute x20, waiting for transfers between devices, swap(): return lax.ppermute(block, ('pipe', 'dp'), route)  54.4 us
    pallas_call x9, Pallas kernels, run_kernel(): pl.pallas_call(kernel, name=name, out_shape=[struct(*v) for v in outs.val...  31.4 us
    ppermute x20, starting transfers between devices, swap(): return lax.ppermute(block, ('pipe', 'dp'), route)  21.7 us
    all_to_all x1, blocking collectives, per_device(): small = lax.all_to_all(small, 'dp', 0, 0)  11.3 us
    ppermute x14, waiting for transfers between devices, swap_cores(): return lax.ppermute(block, 'pipe', [(0, 1), (1, 0)])  6.84 us
    pallas_call x24, Pallas kernels, small_kernel(): pl.pallas_call(run, name=name, out_shape=outs, in_specs=[VM] * len(inputs...  6.12 us
    convert_element_type x4, other arithmetic, per_device(): low = [m.astype(BF) for m in masters]  3.52 us
    ppermute x14, starting transfers between devices, swap_cores(): return lax.ppermute(block, 'pipe', [(0, 1), (1, 0)])  3.37 us
  transfers between devices with their start and end apart: 34, of which 21 were waited for; matrix products, arithmetic and copies ran while one was open for 1% of the time, Pallas kernels for 9%

profile of v3, /device:TPU:0, one launch (start us, length us, event | category | flops | bytes accessed | tf_op | source)
XLA Modules:
  0.0 142.5 jit_solution(16222557606265173833)
XLA Ops:
  2.3 3.0 %collective-permute-start.1 = (bf16[1,24,1536]{2,1,0:T(8,128)(2,1)S(1)}, bf16[1,24,1536]{2,1,0:T(8,128)(2,1)S(1)}, u32[]{:S(2)}, u32[]{:S(2)}) collective-permute-start(bf16[1,24,1536]{2,1,0:T(8,128)(2,1)S(1)} %maximum_bitcast_fusion.refs_0_), channel_id=1, source_target_pairs={{0,2},{1,3},{2,0},{3,1},{4,6},{5,7},{6,4},{7,5},{8,10},{9,11},{10,... | collective-permute-start | bytes 221192 | tf_op jit(solution)/shard_map/ppermute | solution.py:464
  9.4 2.7 %collective-permute-start.2 = (bf16[2,24,1536]{2,1,0:T(8,128)(2,1)S(1)}, bf16[2,24,1536]{2,1,0:T(8,128)(2,1)S(1)}, u32[]{:S(2)}, u32[]{:S(2)}) collective-permute-start(bf16[2,24,1536]{2,1,0:T(8,128)(2,1)S(1)} %join.9.refs_2_.refs_0_), channel_id=1, source_target_pairs={{0,8},{1,9},{2,10},{3,11},{4,12},{5,13},{6,14},{7,15},{8,0},{9,1},... | collective-permute-start | bytes 442376 | tf_op jit(solution)/shard_map/ppermute | solution.py:464
  13.6 2.2 %collective-permute-done.3.refs_1_ = bf16[1,4,24,384]{3,2,1,0:T(8,128)(2,1)S(1)} collective-permute-done((bf16[1,4,24,384]{3,2,1,0:T(8,128)(2,1)S(1)}, bf16[1,4,24,384]{3,2,1,0:T(8,128)(2,1)S(1)}, u32[]{:S(2)}, u32[]{:S(2)}) %collective-permute-start.3) | collective-permute-done | bytes 73760 | tf_op jit(solution)/shard_map/ppermute | solution.py:464
  18.9 1.7 %collective-permute-start.11 = (bf16[4,24,1536]{2,1,0:T(8,128)(2,1)S(1)}, bf16[4,24,1536]{2,1,0:T(8,128)(2,1)S(1)}, u32[]{:S(2)}, u32[]{:S(2)}) collective-permute-start(bf16[4,24,1536]{2,1,0:T(8,128)(2,1)S(1)} %join.13.refs_2_.refs_0_), channel_id=1, source_target_pairs={{0,8},{1,9},{2,10},{3,11},{4,12},{5,13},{6,14},{7,15},{8,0},{9,1},... | collective-permute-start | bytes 884744 | tf_op jit(solution)/shard_map/ppermute | solution.py:464
  20.6 1.8 %collective-permute-done.6.refs_1_ = bf16[2,4,24,384]{3,2,1,0:T(8,128)(2,1)S(1)} collective-permute-done((bf16[2,4,24,384]{3,2,1,0:T(8,128)(2,1)S(1)}, bf16[2,4,24,384]{3,2,1,0:T(8,128)(2,1)S(1)}, u32[]{:S(2)}, u32[]{:S(2)}) %collective-permute-start.6) | collective-permute-done | bytes 147488 | tf_op jit(solution)/shard_map/ppermute | solution.py:464
  23.7 6.2 %collective-permute-done.11.refs_1_ = bf16[4,24,1536]{2,1,0:T(8,128)(2,1)S(1)} collective-permute-done((bf16[4,24,1536]{2,1,0:T(8,128)(2,1)S(1)}, bf16[4,24,1536]{2,1,0:T(8,128)(2,1)S(1)}, u32[]{:S(2)}, u32[]{:S(2)}) %collective-permute-start.11) | collective-permute-done | bytes 294944 | tf_op jit(solution)/shard_map/ppermute | solution.py:464
  33.2 11.5 %collective-permute-done.16.refs_1_ = bf16[8,4,24,384]{3,2,1,0:T(8,128)(2,1)S(1)} collective-permute-done((bf16[8,4,24,384]{3,2,1,0:T(8,128)(2,1)S(1)}, bf16[8,4,24,384]{3,2,1,0:T(8,128)(2,1)S(1)}, u32[]{:S(2)}, u32[]{:S(2)}) %collective-permute-start.16) | collective-permute-done | bytes 589856 | tf_op jit(solution)/shard_map/ppermute | solution.py:464
  50.4 3.4 %extractor_attention.1 = (bf16[512,384]{1,0:T(8,128)(2,1)S(1)}, bf16[512,1152]{1,0:T(8,128)(2,1)S(1)}, bf16[3,1152,256]{2,1,0:T(8,128)(2,1)S(1)}, bf16[384,512]{...) custom-call(f32[2,384]{1,0:T(2,128)S(1)} %bitcast.81, ...), custom_call_target="tpu_custom_call" | custom-call | flops 10 | bytes 8 | tf_op jit(solution)/shard_map/extractor_attention/pallas_call | solution.py:368
  53.8 3.2 %extractor_feed.1 = (bf16[512,1536]{1,0:T(8,128)(2,1)S(1)}, bf16[512,1536]{1,0:T(8,128)(2,1)S(1)}, f32[512,384]{1,0:T(8,128)S(1)}) custom-call(bf16[512,384]{1,0:T(8,128)(2,1)S(1)} %get-tuple-element.111.refs_0_.refs_5_, f32[512,384]{1,0:T(8,128)S(1)} %get-tuple-element.112.refs_1_.refs_6_, bf16[2,1,512,384]{3,2,1,0:T(8,128)(2,1)S(1)} %copy-done.13, ...), custom_call_target="tpu_custom_call" | custom-call | flops 10 | bytes 8 | tf_op jit(solution)/shard_map/extractor_feed/pallas_call | solution.py:368
  57.1 3.3 %generator_attention.1 = (bf16[512,384]{1,0:T(8,128)(2,1)S(1)}, bf16[512,1152]{1,0:T(8,128)(2,1)S(1)}, bf16[3,1152,256]{2,1,0:T(8,128)(2,1)S(1)}, bf16[384,512]{...) custom-call(f32[2,384]{1,0:T(2,128)S(1)} %bitcast.82, ...), custom_call_target="tpu_custom_call" | custom-call | flops 10 | bytes 8 | tf_op jit(solution)/shard_map/generator_attention/pallas_call | solution.py:368
  60.5 7.3 %generator_feed.1 = (f32[512,384]{1,0:T(8,128)S(1)}, f32[512,384]{1,0:T(8,128)S(1)}, bf16[512,384]{1,0:T(8,128)(2,1)S(1)}, f32[1,384]{1,0:T(1,128)S(1)}, bf16[16...) custom-call(f32[2,384]{1,0:T(2,128)S(1)} %bitcast.83, f32[2,384]{1,0:T(2,128)S(1)} %collective-permute-done.refs_1_, ...), custom_call_target="tpu_custom_call" | custom-call | flops 99999997952 | bytes 8 | tf_op jit(solution)/shard_map/generator_feed/pallas_call | solution.py:368
  67.8 3.9 %generator_attention_back.1 = (bf16[16,1,24,768]{3,2,1,0:T(8,128)(2,1)S(1)}, bf16[16,1,24,768]{3,2,1,0:T(8,128)(2,1)S(1)}, bf16[512,1152]{1,0:T(8,128)(2,1)S(1)}) custom-call(bf16[512,384]{1,0:T(8,128)(2,1)S(1)} %get-tuple-element.121.refs_0_, bf16[384,512]{1,0:T(8,128)(2,1)S(1)} %get-tuple-element.122.refs_1_, ...), custom_call_target="tpu_custom_call" | custom-call | flops 60000002048 | bytes 8 | tf_op jit(solution)/shard_map/generator_attention_back/pallas_call | solution.py:368
  73.8 1.7 %collective-permute-done.20.refs_3_ = bf16[16,2,24,768]{3,2,1,0:T(8,128)(2,1)S(1)} collective-permute-done((bf16[16,2,24,768]{3,2,1,0:T(8,128)(2,1)S(1)}, bf16[16,2,24,768]{3,2,1,0:T(8,128)(2,1)S(1)}, u32[]{:S(2)}, u32[]{:S(2)}) %collective-permute-start.20) | collective-permute-done | bytes 1179680 | tf_op jit(solution)/shard_map/ppermute | solution.py:458
  77.4 4.2 %extractor_feed_back.1 = (bf16[16,2,24,768]{3,2,1,0:T(8,128)(2,1)S(1)}, bf16[16,2,24,768]{3,2,1,0:T(8,128)(2,1)S(1)}, f32[512,384]{1,0:T(8,128)S(1)}, bf16[512,384]{1,0:T(8,128)(2,1)S(1)}, f32[1,384]{1,0:T(1,128)S(1)}) custom-call(f32[2,384]{1,0:T(2,128)S(1)} %bitcast.85, f32[2,384]{1,0:T(2,128)S(1)} %collective-permute-done.refs_1_, ...), custom_call_target="tpu_custom_call" | custom-call | flops 70000001024 | bytes 8 | tf_op jit(solution)/shard_map/extractor_feed_back/pallas_call | solution.py:368
  81.8 3.9 %extractor_attention_back.1 = (bf16[16,1,24,768]{3,2,1,0:T(8,128)(2,1)S(1)}, bf16[16,1,24,768]{3,2,1,0:T(8,128)(2,1)S(1)}, bf16[512,1152]{1,0:T(8,128)(2,1)S(1)}) custom-call(bf16[512,384]{1,0:T(8,128)(2,1)S(1)} %get-tuple-element.136.refs_0_, bf16[384,512]{1,0:T(8,128)(2,1)S(1)} %get-tuple-element.137.refs_1_, ...), custom_call_target="tpu_custom_call" | custom-call | flops 60000002048 | bytes 8 | tf_op jit(solution)/shard_map/extractor_attention_back/pallas_call | solution.py:368
  86.1 2.9 %collective-permute-done.23.refs_1_ = bf16[8,3,24,768]{3,2,1,0:T(8,128)(2,1)S(1)} collective-permute-done((bf16[8,3,24,768]{3,2,1,0:T(8,128)(2,1)S(1)}, bf16[8,3,24,768]{3,2,1,0:T(8,128)(2,1)S(1)}, u32[]{:S(2)}, u32[]{:S(2)}) %collective-permute-start.23) | collective-permute-done | bytes 884768 | tf_op jit(solution)/shard_map/ppermute | solution.py:464
  89.2 2.5 %collective-permute-start.26 = (bf16[4,3,24,768]{3,2,1,0:T(8,128)(2,1)S(1)}, bf16[4,3,24,768]{3,2,1,0:T(8,128)(2,1)S(1)}, u32[]{:S(2)}, u32[]{:S(2)}) collective-permute-start(bf16[4,3,24,768]{3,2,1,0:T(8,128)(2,1)S(1)} %get-tuple-element.158), channel_id=1, source_target_pairs={{0,1},{1,0},{2,3},{3,2},{4,5},{5,4},{6,7},{7,6},{8,9},{9,8},{10,11... | collective-permute-start | bytes 1327112 | tf_op jit(solution)/shard_map/ppermute | solution.py:464
  94.6 6.7 %collective-permute-done.26.refs_1_ = bf16[4,3,24,768]{3,2,1,0:T(8,128)(2,1)S(1)} collective-permute-done((bf16[4,3,24,768]{3,2,1,0:T(8,128)(2,1)S(1)}, bf16[4,3,24,768]{3,2,1,0:T(8,128)(2,1)S(1)}, u32[]{:S(2)}, u32[]{:S(2)}) %collective-permute-start.26) | collective-permute-done | bytes 442400 | tf_op jit(solution)/shard_map/ppermute | solution.py:464
  101.5 3.8 %collective-permute-done.25.refs_1_ = bf16[8,3,24,768]{3,2,1,0:T(8,128)(2,1)S(1)} collective-permute-done((bf16[8,3,24,768]{3,2,1,0:T(8,128)(2,1)S(1)}, bf16[8,3,24,768]{3,2,1,0:T(8,128)(2,1)S(1)}, u32[]{:S(2)}, u32[]{:S(2)}) %collective-permute-start.25) | collective-permute-done | bytes 884768 | tf_op jit(solution)/shard_map/ppermute | solution.py:464
  106.9 6.5 %collective-permute-done.29.refs_1_ = bf16[2,3,24,768]{3,2,1,0:T(8,128)(2,1)S(1)} collective-permute-done((bf16[2,3,24,768]{3,2,1,0:T(8,128)(2,1)S(1)}, bf16[2,3,24,768]{3,2,1,0:T(8,128)(2,1)S(1)}, u32[]{:S(2)}, u32[]{:S(2)}) %collective-permute-start.29) | collective-permute-done | bytes 221216 | tf_op jit(solution)/shard_map/ppermute | solution.py:464
  114.1 1.8 %collective-permute-start.32 = (bf16[1,3,24,768]{3,2,1,0:T(8,128)(2,1)S(1)}, bf16[1,3,24,768]{3,2,1,0:T(8,128)(2,1)S(1)}, u32[]{:S(2)}, u32[]{:S(2)}) collective-permute-start(bf16[1,3,24,768]{3,2,1,0:T(8,128)(2,1)S(1)} %get-tuple-element.171), channel_id=1, source_target_pairs={{0,8},{1,9},{2,10},{3,11},{4,12},{5,13},{6,14},{7,15},{8,0},{9,1},... | collective-permute-start | bytes 331784 | tf_op jit(solution)/shard_map/ppermute | solution.py:464
  115.9 5.2 %collective-permute-done.30.refs_1_ = bf16[2,3,24,768]{3,2,1,0:T(8,128)(2,1)S(1)} collective-permute-done((bf16[2,3,24,768]{3,2,1,0:T(8,128)(2,1)S(1)}, bf16[2,3,24,768]{3,2,1,0:T(8,128)(2,1)S(1)}, u32[]{:S(2)}, u32[]{:S(2)}) %collective-permute-start.30) | collective-permute-done | bytes 221216 | tf_op jit(solution)/shard_map/ppermute | solution.py:464
  121.3 5.8 %collective-permute-done.31.refs_1_ = bf16[1,3,24,768]{3,2,1,0:T(8,128)(2,1)S(1)} collective-permute-done((bf16[1,3,24,768]{3,2,1,0:T(8,128)(2,1)S(1)}, bf16[1,3,24,768]{3,2,1,0:T(8,128)(2,1)S(1)}, u32[]{:S(2)}, u32[]{:S(2)}) %collective-permute-start.31) | collective-permute-done | bytes 110624 | tf_op jit(solution)/shard_map/ppermute | solution.py:464
  130.0 11.3 %all_to_all.5.refs_0_ = f32[16,3,384]{2,1,0:T(4,128)S(1)} all-to-all(f32[16,3,384]{2,1,0:T(4,128)S(1)} %get-tuple-element.182), channel_id=1, replica_groups=mesh['pipe'=2,'dp'=16] {'dp'}, dimensions={0} | all-to-all | bytes 147456 | tf_op jit(solution)/shard_map/all_to_all | solution.py:857
  (147 shorter events, 34.5 us)
Async XLA Ops:
  2.3 7.0 %collective-permute-start.1 = (bf16[1,24,1536]{2,1,0:T(8,128)(2,1)S(1)}, bf16[1,24,1536]{2,1,0:T(8,128)(2,1)S(1)}, u32[]{:S(2)}, u32[]{:S(2)}) collective-permute-start(bf16[1,24,1536]{2,1,0:T(8,128)(2,1)S(1)} %maximum_bitcast_fusion.refs_0_), channel_id=1, source_target_pairs={{0,2},{1,3},{2,0},{3,1},{4,6},{5,7},{6,4},{7,5},{8,10},{9,11},{10,... | collective-permute-start | bytes 221192 | tf_op jit(solution)/shard_map/ppermute | solution.py:464
  8.9 7.0 %collective-permute-start.3 = (bf16[1,4,24,384]{3,2,1,0:T(8,128)(2,1)S(1)}, bf16[1,4,24,384]{3,2,1,0:T(8,128)(2,1)S(1)}, u32[]{:S(2)}, u32[]{:S(2)}) collective-permute-start(bf16[1,4,24,384]{3,2,1,0:T(8,128)(2,1)S(1)} %bitcast.70), channel_id=1, source_target_pairs={{0,4},{1,5},{2,6},{3,7},{4,0},{5,1},{6,2},{7,3},{8,12},{9,13},{10,... | collective-permute-start | bytes 221192 | tf_op jit(solution)/shard_map/ppermute | solution.py:464
  9.4 7.4 %collective-permute-start.2 = (bf16[2,24,1536]{2,1,0:T(8,128)(2,1)S(1)}, bf16[2,24,1536]{2,1,0:T(8,128)(2,1)S(1)}, u32[]{:S(2)}, u32[]{:S(2)}) collective-permute-start(bf16[2,24,1536]{2,1,0:T(8,128)(2,1)S(1)} %join.9.refs_2_.refs_0_), channel_id=1, source_target_pairs={{0,8},{1,9},{2,10},{3,11},{4,12},{5,13},{6,14},{7,15},{8,0},{9,1},... | collective-permute-start | bytes 442376 | tf_op jit(solution)/shard_map/ppermute | solution.py:464
  12.1 6.8 %collective-permute-start.7 = (bf16[2,24,1536]{2,1,0:T(8,128)(2,1)S(1)}, bf16[2,24,1536]{2,1,0:T(8,128)(2,1)S(1)}, u32[]{:S(2)}, u32[]{:S(2)}) collective-permute-start(bf16[2,24,1536]{2,1,0:T(8,128)(2,1)S(1)} %join.10.refs_2_.refs_0_), channel_id=1, source_target_pairs={{0,1},{1,0},{2,3},{3,2},{4,5},{5,4},{6,7},{7,6},{8,9},{9,8},{10,11... | collective-permute-start | bytes 442376 | tf_op jit(solution)/shard_map/ppermute | solution.py:464
  15.9 6.6 %collective-permute-start.6 = (bf16[2,4,24,384]{3,2,1,0:T(8,128)(2,1)S(1)}, bf16[2,4,24,384]{3,2,1,0:T(8,128)(2,1)S(1)}, u32[]{:S(2)}, u32[]{:S(2)}) collective-permute-start(bf16[2,4,24,384]{3,2,1,0:T(8,128)(2,1)S(1)} %join.11.refs_2_.refs_0_), channel_id=1, source_target_pairs={{0,8},{1,9},{2,10},{3,11},{4,12},{5,13},{6,14},{7,15},{8,0},{9,1},... | collective-permute-start | bytes 442376 | tf_op jit(solution)/shard_map/ppermute | solution.py:464
  16.8 6.8 %collective-permute-start.5 = (bf16[4,24,1536]{2,1,0:T(8,128)(2,1)S(1)}, bf16[4,24,1536]{2,1,0:T(8,128)(2,1)S(1)}, u32[]{:S(2)}, u32[]{:S(2)}) collective-permute-start(bf16[4,24,1536]{2,1,0:T(8,128)(2,1)S(1)} %join.12.refs_2_.refs_0_), channel_id=1, source_target_pairs={{0,1},{1,0},{2,3},{3,2},{4,5},{5,4},{6,7},{7,6},{8,9},{9,8},{10,11... | collective-permute-start | bytes 884744 | tf_op jit(solution)/shard_map/ppermute | solution.py:464
  18.9 10.9 %collective-permute-start.11 = (bf16[4,24,1536]{2,1,0:T(8,128)(2,1)S(1)}, bf16[4,24,1536]{2,1,0:T(8,128)(2,1)S(1)}, u32[]{:S(2)}, u32[]{:S(2)}) collective-permute-start(bf16[4,24,1536]{2,1,0:T(8,128)(2,1)S(1)} %join.13.refs_2_.refs_0_), channel_id=1, source_target_pairs={{0,8},{1,9},{2,10},{3,11},{4,12},{5,13},{6,14},{7,15},{8,0},{9,1},... | collective-permute-start | bytes 884744 | tf_op jit(solution)/shard_map/ppermute | solution.py:464
  22.5 7.4 %collective-permute-start.15 = (bf16[4,4,24,384]{3,2,1,0:T(8,128)(2,1)S(1)}, bf16[4,4,24,384]{3,2,1,0:T(8,128)(2,1)S(1)}, u32[]{:S(2)}, u32[]{:S(2)}) collective-permute-start(bf16[4,4,24,384]{3,2,1,0:T(8,128)(2,1)S(1)} %join.14.refs_2_.refs_0_), channel_id=1, source_target_pairs={{0,2},{1,3},{2,0},{3,1},{4,6},{5,7},{6,4},{7,5},{8,10},{9,11},{10,... | collective-permute-start | bytes 884744 | tf_op jit(solution)/shard_map/ppermute | solution.py:464
  29.9 14.7 %collective-permute-start.16 = (bf16[8,4,24,384]{3,2,1,0:T(8,128)(2,1)S(1)}, bf16[8,4,24,384]{3,2,1,0:T(8,128)(2,1)S(1)}, u32[]{:S(2)}, u32[]{:S(2)}) collective-permute-start(bf16[8,4,24,384]{3,2,1,0:T(8,128)(2,1)S(1)} %join.17.refs_0_), channel_id=1, source_target_pairs={{0,1},{1,0},{2,3},{3,2},{4,5},{5,4},{6,7},{7,6},{8,9},{9,8},{10,11... | collective-permute-start | bytes 1769480 | tf_op jit(solution)/shard_map/ppermute | solution.py:464
  31.5 13.6 %collective-permute-start.12 = (bf16[8,24,1536]{2,1,0:T(8,128)(2,1)S(1)}, bf16[8,24,1536]{2,1,0:T(8,128)(2,1)S(1)}, u32[]{:S(2)}, u32[]{:S(2)}) collective-permute-start(bf16[8,24,1536]{2,1,0:T(8,128)(2,1)S(1)} %join.16.refs_0_.refs_2_), channel_id=1, source_target_pairs={{0,2},{1,3},{2,0},{3,1},{4,6},{5,7},{6,4},{7,5},{8,10},{9,11},{10,... | collective-permute-start | bytes 1769480 | tf_op jit(solution)/shard_map/ppermute | solution.py:464
  32.1 13.1 %collective-permute-start.17 = (bf16[8,4,24,384]{3,2,1,0:T(8,128)(2,1)S(1)}, bf16[8,4,24,384]{3,2,1,0:T(8,128)(2,1)S(1)}, u32[]{:S(2)}, u32[]{:S(2)}) collective-permute-start(bf16[8,4,24,384]{3,2,1,0:T(8,128)(2,1)S(1)} %join.17.refs_0_), channel_id=1, source_target_pairs={{0,16},{16,0},{1,17},{17,1},{2,18},{18,2},{3,19},{19,3},{4,20},{20... | collective-permute-start | bytes 1769480 | tf_op jit(solution)/shard_map/ppermute | solution.py:458
  32.1 13.6 %collective-permute-start.8 = (bf16[8,24,1536]{2,1,0:T(8,128)(2,1)S(1)}, bf16[8,24,1536]{2,1,0:T(8,128)(2,1)S(1)}, u32[]{:S(2)}, u32[]{:S(2)}) collective-permute-start(bf16[8,24,1536]{2,1,0:T(8,128)(2,1)S(1)} %join.15.refs_0_.refs_2_), channel_id=1, source_target_pairs={{0,4},{1,5},{2,6},{3,7},{4,0},{5,1},{6,2},{7,3},{8,12},{9,13},{10,... | collective-permute-start | bytes 1769480 | tf_op jit(solution)/shard_map/ppermute | solution.py:464
  75.9 13.1 %collective-permute-start.23 = (bf16[8,3,24,768]{3,2,1,0:T(8,128)(2,1)S(1)}, bf16[8,3,24,768]{3,2,1,0:T(8,128)(2,1)S(1)}, u32[]{:S(2)}, u32[]{:S(2)}) collective-permute-start(bf16[8,3,24,768]{3,2,1,0:T(8,128)(2,1)S(1)} %get-tuple-element.151), channel_id=1, source_target_pairs={{0,4},{1,5},{2,6},{3,7},{4,0},{5,1},{6,2},{7,3},{8,12},{9,13},{10,... | collective-permute-start | bytes 2654216 | tf_op jit(solution)/shard_map/ppermute | solution.py:464
  81.6 10.2 %collective-permute-start.22 = (bf16[16,2,24,768]{3,2,1,0:T(8,128)(2,1)S(1)}, bf16[16,2,24,768]{3,2,1,0:T(8,128)(2,1)S(1)}, u32[]{:S(2)}, u32[]{:S(2)}) collective-permute-start(bf16[16,2,24,768]{3,2,1,0:T(8,128)(2,1)S(1)} %get-tuple-element.150), channel_id=1, source_target_pairs={{0,16},{16,0},{1,17},{17,1},{2,18},{18,2},{3,19},{19,3},{4,20},{20... | collective-permute-start | bytes 3538952 | tf_op jit(solution)/shard_map/ppermute | solution.py:458
  85.7 6.1 %collective-permute-start.21 = (bf16[16,1,24,768]{3,2,1,0:T(8,128)(2,1)S(1)}, bf16[16,1,24,768]{3,2,1,0:T(8,128)(2,1)S(1)}, u32[]{:S(2)}, u32[]{:S(2)}) collective-permute-start(bf16[16,1,24,768]{3,2,1,0:T(8,128)(2,1)S(1)} %get-tuple-element.148), channel_id=1, source_target_pairs={{0,16},{16,0},{1,17},{17,1},{2,18},{18,2},{3,19},{19,3},{4,20},{20... | collective-permute-start | bytes 1769480 | tf_op jit(solution)/shard_map/ppermute | solution.py:458
  89.2 12.2 %collective-permute-start.26 = (bf16[4,3,24,768]{3,2,1,0:T(8,128)(2,1)S(1)}, bf16[4,3,24,768]{3,2,1,0:T(8,128)(2,1)S(1)}, u32[]{:S(2)}, u32[]{:S(2)}) collective-permute-start(bf16[4,3,24,768]{3,2,1,0:T(8,128)(2,1)S(1)} %get-tuple-element.158), channel_id=1, source_target_pairs={{0,1},{1,0},{2,3},{3,2},{4,5},{5,4},{6,7},{7,6},{8,9},{9,8},{10,11... | collective-permute-start | bytes 1327112 | tf_op jit(solution)/shard_map/ppermute | solution.py:464
  92.2 13.1 %collective-permute-start.25 = (bf16[8,3,24,768]{3,2,1,0:T(8,128)(2,1)S(1)}, bf16[8,3,24,768]{3,2,1,0:T(8,128)(2,1)S(1)}, u32[]{:S(2)}, u32[]{:S(2)}) collective-permute-start(bf16[8,3,24,768]{3,2,1,0:T(8,128)(2,1)S(1)} %get-tuple-element.157), channel_id=1, source_target_pairs={{0,2},{1,3},{2,0},{3,1},{4,6},{5,7},{6,4},{7,5},{8,10},{9,11},{10,... | collective-permute-start | bytes 2654216 | tf_op jit(solution)/shard_map/ppermute | solution.py:464
  94.1 11.6 %collective-permute-start.24 = (f32[512,384]{1,0:T(8,128)S(1)}, f32[512,384]{1,0:T(8,128)S(1)}, u32[]{:S(2)}, u32[]{:S(2)}) collective-permute-start(f32[512,384]{1,0:T(8,128)S(1)} %get-tuple-element.155), channel_id=1, source_target_pairs={{0,16},{16,0},{1,17},{17,1},{2,18},{18,2},{3,19},{19,3},{4,20},{20... | collective-permute-start | bytes 2359304 | tf_op jit(solution)/shard_map/ppermute | solution.py:458
  94.1 7.3 %collective-permute-start.27 = (f32[2,384]{1,0:T(2,128)S(1)}, f32[2,384]{1,0:T(2,128)S(1)}, u32[]{:S(2)}, u32[]{:S(2)}) collective-permute-start(f32[2,384]{1,0:T(2,128)S(1)} %get-tuple-element.161), channel_id=1, source_target_pairs={{0,16},{16,0},{1,17},{17,1},{2,18},{18,2},{3,19},{19,3},{4,20},{20... | collective-permute-start | bytes 9224 | tf_op jit(solution)/shard_map/ppermute | solution.py:458
  105.5 8.4 %collective-permute-start.28 = (bf16[4,3,24,768]{3,2,1,0:T(8,128)(2,1)S(1)}, bf16[4,3,24,768]{3,2,1,0:T(8,128)(2,1)S(1)}, u32[]{:S(2)}, u32[]{:S(2)}) collective-permute-start(bf16[4,3,24,768]{3,2,1,0:T(8,128)(2,1)S(1)} %get-tuple-element.163), channel_id=1, source_target_pairs={{0,1},{1,0},{2,3},{3,2},{4,5},{5,4},{6,7},{7,6},{8,9},{9,8},{10,11... | collective-permute-start | bytes 1327112 | tf_op jit(solution)/shard_map/ppermute | solution.py:464
  105.6 7.8 %collective-permute-start.29 = (bf16[2,3,24,768]{3,2,1,0:T(8,128)(2,1)S(1)}, bf16[2,3,24,768]{3,2,1,0:T(8,128)(2,1)S(1)}, u32[]{:S(2)}, u32[]{:S(2)}) collective-permute-start(bf16[2,3,24,768]{3,2,1,0:T(8,128)(2,1)S(1)} %get-tuple-element.164), channel_id=1, source_target_pairs={{0,2},{1,3},{2,0},{3,1},{4,6},{5,7},{6,4},{7,5},{8,10},{9,11},{10,... | collective-permute-start | bytes 663560 | tf_op jit(solution)/shard_map/ppermute | solution.py:464
  114.0 7.2 %collective-permute-start.30 = (bf16[2,3,24,768]{3,2,1,0:T(8,128)(2,1)S(1)}, bf16[2,3,24,768]{3,2,1,0:T(8,128)(2,1)S(1)}, u32[]{:S(2)}, u32[]{:S(2)}) collective-permute-start(bf16[2,3,24,768]{3,2,1,0:T(8,128)(2,1)S(1)} %get-tuple-element.168), channel_id=1, source_target_pairs={{0,4},{1,5},{2,6},{3,7},{4,0},{5,1},{6,2},{7,3},{8,12},{9,13},{10,... | collective-permute-start | bytes 663560 | tf_op jit(solution)/shard_map/ppermute | solution.py:464
  114.1 7.2 %collective-permute-start.32 = (bf16[1,3,24,768]{3,2,1,0:T(8,128)(2,1)S(1)}, bf16[1,3,24,768]{3,2,1,0:T(8,128)(2,1)S(1)}, u32[]{:S(2)}, u32[]{:S(2)}) collective-permute-start(bf16[1,3,24,768]{3,2,1,0:T(8,128)(2,1)S(1)} %get-tuple-element.171), channel_id=1, source_target_pairs={{0,8},{1,9},{2,10},{3,11},{4,12},{5,13},{6,14},{7,15},{8,0},{9,1},... | collective-permute-start | bytes 331784 | tf_op jit(solution)/shard_map/ppermute | solution.py:464
  121.2 5.9 %collective-permute-start.31 = (bf16[1,3,24,768]{3,2,1,0:T(8,128)(2,1)S(1)}, bf16[1,3,24,768]{3,2,1,0:T(8,128)(2,1)S(1)}, u32[]{:S(2)}, u32[]{:S(2)}) collective-permute-start(bf16[1,3,24,768]{3,2,1,0:T(8,128)(2,1)S(1)} %get-tuple-element.170), channel_id=1, source_target_pairs={{0,8},{1,9},{2,10},{3,11},{4,12},{5,13},{6,14},{7,15},{8,0},{9,1},... | collective-permute-start | bytes 331784 | tf_op jit(solution)/shard_map/ppermute | solution.py:464
  (42 other events, 334.2 us)

commit v4 on v3

--- a/solution.py
+++ b/solution.py
@@ -25,7 +25,7 @@
 QB = 128
 REACH = 256
 ROWS = 64
-CHUNK = 384
+CHUNK = 512
 WIDE = 4 * D
 HALF = WIDE // 2
 PAIRS = HEADS // 2
@@ -177,8 +177,7 @@
     norm_into(x, gain[0:1, :], k["n1"])
     make_bias(k["seg"], k["bias"], length)
     pk = k["pk"]
-    for c in range(0, 3 * D, D):
-        pk[:, c : c + D] = dot(k["n1"][...], wide[:, c : c + D]).astype(BF)
+    pk[...] = dot(k["n1"][...], wide[:, : 3 * D]).astype(BF)
     attend(pk, k, length)
     mid = k["mid"]
     mid[...] = x[...].astype(F32) + dot(k["attT"][...], wide[:, 3 * D :], 0, 0)
@@ -219,13 +218,10 @@
     da[...] = dot(dmb[...], wide[:, 3 * D :], 1, 1).astype(BF)
     attend_back(k["pk"], k["pt"], da, k, length)
 
-    def grad(lo):
-        if lo < 3 * D:
-            return dot(k["n1"][...], dpk[:, lo : lo + D], 0, 0)
-        return dot(k["attT"][...], dmb[...])
-
-    for at in range(0, HALF, D):
-        emit.wide(grad, at)
+    n1 = k["n1"]
+    zero = dot(n1[...], dpk[:, :HALF], 0, 0)
+    emit.wide(zero[:, :D], dot(n1[...], dpk[:, HALF:], 0, 0), 0)
+    emit.wide(zero[:, D:], dot(k["attT"][...], dmb[...]), D)
 
 
 def input_back(x, k, wide, gain, out, low):
@@ -301,9 +297,8 @@
             for s in range(value.shape[0]):
                 put(which, self.places[which][first + s], value[s])
 
-    def wide(self, make, at):
+    def wide(self, zero, one, at):
         plan = self.plan
-        zero, one = make(at), make(HALF + at)
         if plan.thin:
             self.first[0][:, at : at + D] = zero.astype(BF)
             self.first[0][:, HALF + at : HALF + at + D] = one.astype(BF)
@@ -318,25 +313,24 @@
     def up(self, make):
         plan = self.plan
         if plan.thin:
-            for lo in range(0, FF, D):
-                self.second[0][:, lo : lo + D] = make(lo, D).astype(BF)
+            for lo in (0, HALF):
+                self.second[0][:, lo : lo + HALF] = make(lo, HALF).astype(BF)
             return
-        shape = (plan.slabs, plan.rows, D)
-        for lo in range(0, HALF, D):
-
-            def put(which, place, value, lo=lo):
-                self.second[which][place, 0, :, lo : lo + D] = value
-
-            self.halves(make(lo, D).reshape(shape), make(HALF + lo, D).reshape(shape), put)
+        shape = (plan.slabs, plan.rows, HALF)
+
+        def put(which, place, value):
+            self.second[which][place, 0, :, :] = value
+
+        self.halves(make(0, HALF).reshape(shape), make(HALF, HALF).reshape(shape), put)
 
     def down(self, make):
         plan = self.plan
-        for lo in range(0, FF, D):
-            value = make(lo, D)
+        for lo in range(0, FF, HALF):
+            value = make(lo, HALF)
             if plan.thin:
-                self.second[1][lo : lo + D, :] = value.astype(BF)
+                self.second[1][lo : lo + HALF, :] = value.astype(BF)
                 continue
-            value = value.reshape(D // (4 * plan.rows), 2, 2 * plan.rows, D)
+            value = value.reshape(HALF // (4 * plan.rows), 2, 2 * plan.rows, D)
 
             def put(which, place, value, r=plan.rows):
                 self.second[which][place, 1, :, 0:D] = value[:r]
@@ -392,7 +386,7 @@
     )(*inputs, *after)
 
 
-def arrange(plan, flow, own, got):
+def arrange(plan, flow, own, got, after):
     n, each = plan.slabs, plan.slabs // 2
 
     def kernel(a0, b0, a1, b1, zero, one):
@@ -414,7 +408,7 @@
             move(a1, b1, zero, 0)
 
     like = struct((n, *own[0].shape[1:]), BF)
-    out = small_kernel("arrange", kernel, [like, like], *own, *got)
+    out = small_kernel("arrange", kernel, [like, like], *own, *got, after=after)
     return [v.reshape(plan.weight_shape(flow)) for v in out]
 
 
@@ -473,11 +467,12 @@
     return small_kernel("join", kernel, [struct((2 * a.shape[0], *a.shape[1:]), a.dtype)], a, b, after=after)[0]
 
 
-def gather(plan, shards):
+def gather(plan, shards, early):
     held = [shard[None] for shard in shards]
     last = ()
     for turn in range(plan.bits):
         came = [swap(held[f], (orders[0][turn], orders[1][turn])) for f, orders in enumerate(plan.gather_orders)]
+        last = (*last, early) if turn == 1 else last
         if turn < plan.bits - 1:
             for f in range(3):
                 held[f] = join(held[f], came[f], last)
@@ -510,15 +505,29 @@
 
 
 class Scatter:
-    def __init__(self, plan, block, *halves):
-        self.orders, self.turn = plan.scatter_orders[block], 0
-        self.pairs = [(mine, swap_cores(other)) for mine, other in halves]
+    def __init__(self, plan, block):
+        self.orders, self.turn, self.pairs = plan.scatter_orders[block], 0, []
+
+    def exchange(self, pairs, turn, after):
+        keep, send = add_split(pairs, after)
+        return keep, swap(send, (self.orders[0][turn], self.orders[1][turn]))
+
+    def begin(self, parts, *after):
+        self.pairs = [self.exchange(parts, 0, after)]
+        self.turn = 1
+        return self.pairs[0][0]
+
+    def part(self, mine, came, *after):
+        self.pairs.append(self.exchange([(mine, came)], 0, after))
+        self.turn = 1
+        return self.pairs[-1][0]
 
     def step(self, *after):
-        keep, send = add_split(self.pairs, after)
-        self.pairs = [(keep, swap(send, (self.orders[0][self.turn], self.orders[1][self.turn])))]
+        if self.turn == 1:
+            self.pairs.reverse()
+        self.pairs = [self.exchange(self.pairs, self.turn, after)]
         self.turn += 1
-        return keep
+        return self.pairs[0][0]
 
 
 def owners(zero, one):
@@ -538,7 +547,7 @@
     return small_kernel("owners", kernel, [like, like], *[v for pair in zero + one for v in pair])
 
 
-def thin_arrange(plan, flow, own, got):
+def thin_arrange(plan, flow, own, got, after):
     core, me = lax.axis_index("pipe"), lax.axis_index("dp")
     index = jnp.arange(plan.count, dtype=jnp.int32)
     out = []
@@ -693,16 +702,13 @@
 
         low = [m.astype(BF) for m in masters]
         wide = jnp.concatenate(low[:2], 1)
-        flows = gather(plan, (wide, low[2], low[3].reshape(4, -1, D)))
         gains_got = swap_cores(gains[0])
+        flows = gather(plan, (wide, low[2], low[3].reshape(4, -1, D)), gains_got)
         put = thin_arrange if plan.thin else arrange
         both = [None] * 3
 
         def place_flow(flow, *after):
-            first, second = flows[flow]
-            if after:
-                second = behind(second, *after)
-            both[flow] = put(plan, flow, (first, second), (swap_cores(first), swap_cores(second)))
+            both[flow] = put(plan, flow, flows[flow], tuple(swap_cores(v) for v in flows[flow]), after)
 
         place_flow(0)
 
@@ -725,21 +731,23 @@
         def refs_of(k, table):
             return [k[n] for n in table]
 
-        def halves(source, table, block, bundle):
+        def traded(source, table, block, bundle):
             values = [source[n] for n in table]
-            return thin_halves(plan, block, values, bundle) if plan.thin else values
+            if plan.thin:
+                values = thin_halves(plan, block, values, bundle)
+            return values[0], swap_cores(values[1])
 
         def body(k, gain):
             attention_half(k["x"], k, k["wide"], gain, L)
 
         attention_scratch = pick("q2", "vT", "bias", "ss")
         one = run_kernel(
-            "extractor_attention", body, 0, {**gain_refs, **x0, **seg, **weights(0, "wide")},
+            "extractor_attention", body, 0, {**gain_refs, **x0, **seg, "pr": (prompts, ("core", 0)), **weights(0, "wide")},
             pick("n1", "pk", "pt", "attT", "mid", "n2"), attention_scratch, 1e-9,
         )
 
-        place_flow(1)
-        place_flow(2)
+        place_flow(1, one["n2"])
+        place_flow(2, one["n2"])
 
         def body(k, gain):
             def out(value):
@@ -750,7 +758,7 @@
         two = run_kernel(
             "extractor_feed", body, 0,
             {**there(one, "n2", "mid"), "pr": (prompts, ("core", 0)), **weights(0, "up", "down")},
-            pick("act", "gp", "x1"), pick("hs"), 1e-9,
+            pick("act", "gp", "x1"), pick("hs"), 3.2,
         )
 
         def body(k, gain):
@@ -776,6 +784,7 @@
             {**pick("y2", "dmid", "dmb", "dg"), **g_second}, pick("act", "gp", "hs", "dh", "dn"), 10,
         )
 
+        second_one = traded(four, g_second, 1, 1)
         back_scratch = pick("q2", "d2", "kT", "ss", "ds", "dqT", "dk", "dv", "da")
 
         def body(k, gain):
@@ -787,6 +796,9 @@
             {**there(four, "dmb"), **there(three, "attT", "pk", "pt", "n1"), **weights(1, "wide")},
             {**g_first, **pick("dpk")}, back_scratch, 6,
         )
+        sum_one = Scatter(plan, 1)
+        first_one = traded(five, g_first, 1, 0)
+
         def body(k, gain):
             k["dg"][...] = input_back(k["x1"], k, k["wide"], gain, None, k["dxb"])
 
@@ -795,8 +807,7 @@
             {**gain_refs, **there(five, "dpk"), **there(four, "dmid"), **there(two, "x1"), **weights(1, "wide")},
             pick("dg", "dxb"), pick("dn"), 3,
         )
-        sum_one = Scatter(plan, 1, halves(five, g_first, 1, 0), halves(four, g_second, 1, 1))
-        last = sum_one.step(six["dxb"])
+        last = sum_one.begin([first_one, second_one], six["dxb"])
 
         def body(k, gain):
             emit = Emit(plan, 0, None, refs_of(k, g_second))
@@ -807,6 +818,7 @@
             {**gain_refs, **there(six, "dxb"), **there(two, "act", "gp"), **there(one, "n2", "mid"), **weights(0, "up", "down")},
             {**g_second, **pick("dmid", "dmb", "dg")}, pick("dh", "dn"), 7, after=[last],
         )
+        second_zero = traded(seven, g_second, 0, 1)
 
         def body(k, gain):
             emit = Emit(plan, 0, refs_of(k, g_first), None)
@@ -817,9 +829,10 @@
             {**there(seven, "dmb"), **there(one, "attT", "pk", "pt", "n1"), **weights(0, "wide")},
             {**g_first, **pick("dpk")}, back_scratch, 6,
         )
-        sum_zero = Scatter(plan, 0, halves(eight, g_first, 0, 0), halves(seven, g_second, 0, 1))
-        last = sum_one.step(eight["dpk"])
-        last = sum_zero.step(last)
+        first_zero = traded(eight, g_first, 0, 0)
+        sum_zero = Scatter(plan, 0)
+        last = sum_zero.begin([first_zero, second_zero], eight["dpk"])
+        last = sum_one.step(last)
 
         def body(k, gain):
             dg = input_back(k["x"], k, k["wide"], gain, k["dx"], None)

time: 143 us -> 139 us (0.972)
  waiting for transfers between devices: 61.2 us -> 55.7 us
  starting transfers between devices: 25.1 us -> 28.4 us
    ppermute x20, waiting for transfers between devices: 54.4 us -> 49.5 us  [swap(): return lax.ppermute(block, ('pipe', 'dp'), route)]
    ppermute x20, starting transfers between devices: 21.7 us -> 24.9 us  [swap(): return lax.ppermute(block, ('pipe', 'dp'), route)]
  transfers between devices with their start and end apart: 34 -> 34, of which waited for: 21 -> 18; matrix products, arithmetic and copies ran while one was open for 1% -> 1% of each run, Pallas kernels for 9% -> 12%
where the time goes in v4:
time: 139 us; the launch traced here: 138 us
  waiting for transfers between devices  55.7 us (40%)
  Pallas kernels  36.3 us (26%)
  starting transfers between devices  28.4 us (20%)
  blocking collectives  11.3 us (8%)
  other arithmetic  3.53 us (3%)
  local copies, waits for them, and re-layouts  1.65 us (1%)
  between operations  1.45 us (1%)
    ppermute x20, waiting for transfers between devices, swap(): return lax.ppermute(block, ('pipe', 'dp'), route)  49.5 us
    pallas_call x9, Pallas kernels, run_kernel(): pl.pallas_call(kernel, name=name, out_shape=[struct(*v) for v in outs.val...  30.1 us
    ppermute x20, starting transfers between devices, swap(): return lax.ppermute(block, ('pipe', 'dp'), route)  24.9 us
    all_to_all x1, blocking collectives, per_device(): small = lax.all_to_all(small, 'dp', 0, 0)  11.3 us
    ppermute x14, waiting for transfers between devices, swap_cores(): return lax.ppermute(block, 'pipe', [(0, 1), (1, 0)])  6.18 us
    pallas_call x24, Pallas kernels, small_kernel(): pl.pallas_call(run, name=name, out_shape=outs, in_specs=[VM] * len(inputs...  6.16 us
    convert_element_type x4, other arithmetic, per_device(): low = [m.astype(BF) for m in masters]  3.52 us
    ppermute x14, starting transfers between devices, swap_cores(): return lax.ppermute(block, 'pipe', [(0, 1), (1, 0)])  3.51 us
  transfers between devices with their start and end apart: 34, of which 18 were waited for; matrix products, arithmetic and copies ran while one was open for 1% of the time, Pallas kernels for 12%

profile of v4, /device:TPU:0, one launch (start us, length us, event | category | flops | bytes accessed | tf_op | source)
XLA Modules:
  0.0 138.3 jit_solution(7967044485326116901)
XLA Ops:
  2.4 3.0 %collective-permute-start.1 = (bf16[1,24,1536]{2,1,0:T(8,128)(2,1)S(1)}, bf16[1,24,1536]{2,1,0:T(8,128)(2,1)S(1)}, u32[]{:S(2)}, u32[]{:S(2)}) collective-permute-start(bf16[1,24,1536]{2,1,0:T(8,128)(2,1)S(1)} %maximum_bitcast_fusion.refs_0_), channel_id=1, source_target_pairs={{0,2},{1,3},{2,0},{3,1},{4,6},{5,7},{6,4},{7,5},{8,10},{9,11},{10,... | collective-permute-start | bytes 221192 | tf_op jit(solution)/shard_map/ppermute | solution.py:458
  9.4 2.7 %collective-permute-start.2 = (bf16[2,24,1536]{2,1,0:T(8,128)(2,1)S(1)}, bf16[2,24,1536]{2,1,0:T(8,128)(2,1)S(1)}, u32[]{:S(2)}, u32[]{:S(2)}) collective-permute-start(bf16[2,24,1536]{2,1,0:T(8,128)(2,1)S(1)} %join.9.refs_2_.refs_0_), channel_id=1, source_target_pairs={{0,8},{1,9},{2,10},{3,11},{4,12},{5,13},{6,14},{7,15},{8,0},{9,1},... | collective-permute-start | bytes 442376 | tf_op jit(solution)/shard_map/ppermute | solution.py:458
  13.6 2.2 %collective-permute-done.3.refs_1_ = bf16[1,4,24,384]{3,2,1,0:T(8,128)(2,1)S(1)} collective-permute-done((bf16[1,4,24,384]{3,2,1,0:T(8,128)(2,1)S(1)}, bf16[1,4,24,384]{3,2,1,0:T(8,128)(2,1)S(1)}, u32[]{:S(2)}, u32[]{:S(2)}) %collective-permute-start.3) | collective-permute-done | bytes 73760 | tf_op jit(solution)/shard_map/ppermute | solution.py:458
  19.6 2.1 %collective-permute-start.11 = (bf16[4,24,1536]{2,1,0:T(8,128)(2,1)S(1)}, bf16[4,24,1536]{2,1,0:T(8,128)(2,1)S(1)}, u32[]{:S(2)}, u32[]{:S(2)}) collective-permute-start(bf16[4,24,1536]{2,1,0:T(8,128)(2,1)S(1)} %join.13.refs_2_.refs_0_), channel_id=1, source_target_pairs={{0,8},{1,9},{2,10},{3,11},{4,12},{5,13},{6,14},{7,15},{8,0},{9,1},... | collective-permute-start | bytes 884744 | tf_op jit(solution)/shard_map/ppermute | solution.py:458
  22.6 2.2 %collective-permute-done.5.refs_1_ = bf16[4,24,1536]{2,1,0:T(8,128)(2,1)S(1)} collective-permute-done((bf16[4,24,1536]{2,1,0:T(8,128)(2,1)S(1)}, bf16[4,24,1536]{2,1,0:T(8,128)(2,1)S(1)}, u32[]{:S(2)}, u32[]{:S(2)}) %collective-permute-start.5) | collective-permute-done | bytes 294944 | tf_op jit(solution)/shard_map/ppermute | solution.py:458
  25.8 4.8 %collective-permute-done.11.refs_1_ = bf16[4,24,1536]{2,1,0:T(8,128)(2,1)S(1)} collective-permute-done((bf16[4,24,1536]{2,1,0:T(8,128)(2,1)S(1)}, bf16[4,24,1536]{2,1,0:T(8,128)(2,1)S(1)}, u32[]{:S(2)}, u32[]{:S(2)}) %collective-permute-start.11) | collective-permute-done | bytes 294944 | tf_op jit(solution)/shard_map/ppermute | solution.py:458
  32.3 9.4 %collective-permute-done.8.refs_1_ = bf16[8,24,1536]{2,1,0:T(8,128)(2,1)S(1)} collective-permute-done((bf16[8,24,1536]{2,1,0:T(8,128)(2,1)S(1)}, bf16[8,24,1536]{2,1,0:T(8,128)(2,1)S(1)}, u32[]{:S(2)}, u32[]{:S(2)}) %collective-permute-start.8) | collective-permute-done | bytes 589856 | tf_op jit(solution)/shard_map/ppermute | solution.py:458
  42.8 1.9 %collective-permute-done.12.refs_1_ = bf16[8,24,1536]{2,1,0:T(8,128)(2,1)S(1)} collective-permute-done((bf16[8,24,1536]{2,1,0:T(8,128)(2,1)S(1)}, bf16[8,24,1536]{2,1,0:T(8,128)(2,1)S(1)}, u32[]{:S(2)}, u32[]{:S(2)}) %collective-permute-start.12) | collective-permute-done | bytes 589856 | tf_op jit(solution)/shard_map/ppermute | solution.py:458
  45.4 3.4 %extractor_attention.1 = (bf16[512,384]{1,0:T(8,128)(2,1)S(1)}, bf16[512,1152]{1,0:T(8,128)(2,1)S(1)}, bf16[3,1152,256]{2,1,0:T(8,128)(2,1)S(1)}, bf16[384,512]{...) custom-call(f32[2,384]{1,0:T(2,128)S(1)} %bitcast.77, ...), custom_call_target="tpu_custom_call" | custom-call | flops 10 | bytes 8 | tf_op jit(solution)/shard_map/extractor_attention/pallas_call | solution.py:362
  50.2 3.2 %extractor_feed.1 = (bf16[512,1536]{1,0:T(8,128)(2,1)S(1)}, bf16[512,1536]{1,0:T(8,128)(2,1)S(1)}, f32[512,384]{1,0:T(8,128)S(1)}) custom-call(bf16[512,384]{1,0:T(8,128)(2,1)S(1)} %get-tuple-element.111.refs_4_.refs_0_.refs_5_, f32[512,384]{1,0:T(8,128)S(1)} %get-tuple-element.112.refs_1_.refs_6_, bf16[2,1,512,384]{3,2,1,0:T(8,128)(2,1)S(1)} %copy-done.9, ...), custom_call_target="tpu_custom_call" | custom-call | flops 32000000000 | bytes 8 | tf_op jit(solution)/shard_map/extractor_feed/pallas_call | solution.py:362
  53.4 3.3 %generator_attention.1 = (bf16[512,384]{1,0:T(8,128)(2,1)S(1)}, bf16[512,1152]{1,0:T(8,128)(2,1)S(1)}, bf16[3,1152,256]{2,1,0:T(8,128)(2,1)S(1)}, bf16[384,512]{...) custom-call(f32[2,384]{1,0:T(2,128)S(1)} %bitcast.78, ...), custom_call_target="tpu_custom_call" | custom-call | flops 10 | bytes 8 | tf_op jit(solution)/shard_map/generator_attention/pallas_call | solution.py:362
  56.8 6.3 %generator_feed.1 = (f32[512,384]{1,0:T(8,128)S(1)}, f32[512,384]{1,0:T(8,128)S(1)}, bf16[512,384]{1,0:T(8,128)(2,1)S(1)}, f32[1,384]{1,0:T(1,128)S(1)}, bf16[16...) custom-call(f32[2,384]{1,0:T(2,128)S(1)} %bitcast.79, ...), custom_call_target="tpu_custom_call" | custom-call | flops 99999997952 | bytes 8 | tf_op jit(solution)/shard_map/generator_feed/pallas_call | solution.py:362
  63.1 4.1 %generator_attention_back.1 = (bf16[16,1,24,768]{3,2,1,0:T(8,128)(2,1)S(1)}, bf16[16,1,24,768]{3,2,1,0:T(8,128)(2,1)S(1)}, bf16[512,1152]{1,0:T(8,128)(2,1)S(1)}) custom-call(bf16[512,384]{1,0:T(8,128)(2,1)S(1)} %get-tuple-element.121.refs_0_, bf16[384,512]{1,0:T(8,128)(2,1)S(1)} %get-tuple-element.122.refs_1_, ...), custom_call_target="tpu_custom_call" | custom-call | flops 60000002048 | bytes 8 | tf_op jit(solution)/shard_map/generator_attention_back/pallas_call | solution.py:362
  69.2 1.7 %collective-permute-done.20.refs_3_ = bf16[16,2,24,768]{3,2,1,0:T(8,128)(2,1)S(1)} collective-permute-done((bf16[16,2,24,768]{3,2,1,0:T(8,128)(2,1)S(1)}, bf16[16,2,24,768]{3,2,1,0:T(8,128)(2,1)S(1)}, u32[]{:S(2)}, u32[]{:S(2)}) %collective-permute-start.20) | collective-permute-done | bytes 1179680 | tf_op jit(solution)/shard_map/ppermute | solution.py:452
  72.9 3.5 %extractor_feed_back.1 = (bf16[16,2,24,768]{3,2,1,0:T(8,128)(2,1)S(1)}, bf16[16,2,24,768]{3,2,1,0:T(8,128)(2,1)S(1)}, f32[512,384]{1,0:T(8,128)S(1)}, bf16[512,384]{1,0:T(8,128)(2,1)S(1)}, f32[1,384]{1,0:T(1,128)S(1)}) custom-call(f32[2,384]{1,0:T(2,128)S(1)} %bitcast.81, f32[2,384]{1,0:T(2,128)S(1)} %collective-permute-done.refs_3_.refs_1_, ...), custom_call_target="tpu_custom_call" | custom-call | flops 70000001024 | bytes 8 | tf_op jit(solution)/shard_map/extractor_feed_back/pallas_call | solution.py:362
  76.6 3.8 %extractor_attention_back.1 = (bf16[16,1,24,768]{3,2,1,0:T(8,128)(2,1)S(1)}, bf16[16,1,24,768]{3,2,1,0:T(8,128)(2,1)S(1)}, bf16[512,1152]{1,0:T(8,128)(2,1)S(1)}) custom-call(bf16[512,384]{1,0:T(8,128)(2,1)S(1)} %get-tuple-element.136.refs_0_, bf16[384,512]{1,0:T(8,128)(2,1)S(1)} %get-tuple-element.137.refs_1_, ...), custom_call_target="tpu_custom_call" | custom-call | flops 60000002048 | bytes 8 | tf_op jit(solution)/shard_map/extractor_attention_back/pallas_call | solution.py:362
  84.7 2.5 %collective-permute-start.26 = (bf16[4,3,24,768]{3,2,1,0:T(8,128)(2,1)S(1)}, bf16[4,3,24,768]{3,2,1,0:T(8,128)(2,1)S(1)}, u32[]{:S(2)}, u32[]{:S(2)}) collective-permute-start(bf16[4,3,24,768]{3,2,1,0:T(8,128)(2,1)S(1)} %get-tuple-element.158), channel_id=1, source_target_pairs={{0,1},{1,0},{2,3},{3,2},{4,5},{5,4},{6,7},{7,6},{8,9},{9,8},{10,11... | collective-permute-start | bytes 1327112 | tf_op jit(solution)/shard_map/ppermute | solution.py:458
  89.5 7.3 %collective-permute-done.26.refs_1_ = bf16[4,3,24,768]{3,2,1,0:T(8,128)(2,1)S(1)} collective-permute-done((bf16[4,3,24,768]{3,2,1,0:T(8,128)(2,1)S(1)}, bf16[4,3,24,768]{3,2,1,0:T(8,128)(2,1)S(1)}, u32[]{:S(2)}, u32[]{:S(2)}) %collective-permute-start.26) | collective-permute-done | bytes 442400 | tf_op jit(solution)/shard_map/ppermute | solution.py:458
  96.9 3.3 %collective-permute-done.25.refs_1_ = bf16[8,3,24,768]{3,2,1,0:T(8,128)(2,1)S(1)} collective-permute-done((bf16[8,3,24,768]{3,2,1,0:T(8,128)(2,1)S(1)}, bf16[8,3,24,768]{3,2,1,0:T(8,128)(2,1)S(1)}, u32[]{:S(2)}, u32[]{:S(2)}) %collective-permute-start.25) | collective-permute-done | bytes 884768 | tf_op jit(solution)/shard_map/ppermute | solution.py:458
  102.1 6.2 %collective-permute-done.29.refs_1_ = bf16[2,3,24,768]{3,2,1,0:T(8,128)(2,1)S(1)} collective-permute-done((bf16[2,3,24,768]{3,2,1,0:T(8,128)(2,1)S(1)}, bf16[2,3,24,768]{3,2,1,0:T(8,128)(2,1)S(1)}, u32[]{:S(2)}, u32[]{:S(2)}) %collective-permute-start.29) | collective-permute-done | bytes 221216 | tf_op jit(solution)/shard_map/ppermute | solution.py:458
  109.3 3.0 %collective-permute-start.32 = (bf16[1,3,24,768]{3,2,1,0:T(8,128)(2,1)S(1)}, bf16[1,3,24,768]{3,2,1,0:T(8,128)(2,1)S(1)}, u32[]{:S(2)}, u32[]{:S(2)}) collective-permute-start(bf16[1,3,24,768]{3,2,1,0:T(8,128)(2,1)S(1)} %get-tuple-element.171), channel_id=1, source_target_pairs={{0,8},{1,9},{2,10},{3,11},{4,12},{5,13},{6,14},{7,15},{8,0},{9,1},... | collective-permute-start | bytes 331784 | tf_op jit(solution)/shard_map/ppermute | solution.py:458
  112.4 3.7 %collective-permute-done.30.refs_1_ = bf16[2,3,24,768]{3,2,1,0:T(8,128)(2,1)S(1)} collective-permute-done((bf16[2,3,24,768]{3,2,1,0:T(8,128)(2,1)S(1)}, bf16[2,3,24,768]{3,2,1,0:T(8,128)(2,1)S(1)}, u32[]{:S(2)}, u32[]{:S(2)}) %collective-permute-start.30) | collective-permute-done | bytes 221216 | tf_op jit(solution)/shard_map/ppermute | solution.py:458
  117.1 5.8 %collective-permute-done.31.refs_1_ = bf16[1,3,24,768]{3,2,1,0:T(8,128)(2,1)S(1)} collective-permute-done((bf16[1,3,24,768]{3,2,1,0:T(8,128)(2,1)S(1)}, bf16[1,3,24,768]{3,2,1,0:T(8,128)(2,1)S(1)}, u32[]{:S(2)}, u32[]{:S(2)}) %collective-permute-start.31) | collective-permute-done | bytes 110624 | tf_op jit(solution)/shard_map/ppermute | solution.py:458
  125.8 11.3 %all_to_all.5.refs_0_ = f32[16,3,384]{2,1,0:T(4,128)S(1)} all-to-all(f32[16,3,384]{2,1,0:T(4,128)S(1)} %get-tuple-element.182), channel_id=1, replica_groups=mesh['pipe'=2,'dp'=16] {'dp'}, dimensions={0} | all-to-all | bytes 147456 | tf_op jit(solution)/shard_map/all_to_all | solution.py:870
  (147 shorter events, 36.0 us)
Async XLA Ops:
  2.4 7.0 %collective-permute-start.1 = (bf16[1,24,1536]{2,1,0:T(8,128)(2,1)S(1)}, bf16[1,24,1536]{2,1,0:T(8,128)(2,1)S(1)}, u32[]{:S(2)}, u32[]{:S(2)}) collective-permute-start(bf16[1,24,1536]{2,1,0:T(8,128)(2,1)S(1)} %maximum_bitcast_fusion.refs_0_), channel_id=1, source_target_pairs={{0,2},{1,3},{2,0},{3,1},{4,6},{5,7},{6,4},{7,5},{8,10},{9,11},{10,... | collective-permute-start | bytes 221192 | tf_op jit(solution)/shard_map/ppermute | solution.py:458
  8.9 7.0 %collective-permute-start.3 = (bf16[1,4,24,384]{3,2,1,0:T(8,128)(2,1)S(1)}, bf16[1,4,24,384]{3,2,1,0:T(8,128)(2,1)S(1)}, u32[]{:S(2)}, u32[]{:S(2)}) collective-permute-start(bf16[1,4,24,384]{3,2,1,0:T(8,128)(2,1)S(1)} %bitcast.66), channel_id=1, source_target_pairs={{0,4},{1,5},{2,6},{3,7},{4,0},{5,1},{6,2},{7,3},{8,12},{9,13},{10,... | collective-permute-start | bytes 221192 | tf_op jit(solution)/shard_map/ppermute | solution.py:458
  9.4 8.6 %collective-permute-start.2 = (bf16[2,24,1536]{2,1,0:T(8,128)(2,1)S(1)}, bf16[2,24,1536]{2,1,0:T(8,128)(2,1)S(1)}, u32[]{:S(2)}, u32[]{:S(2)}) collective-permute-start(bf16[2,24,1536]{2,1,0:T(8,128)(2,1)S(1)} %join.9.refs_2_.refs_0_), channel_id=1, source_target_pairs={{0,8},{1,9},{2,10},{3,11},{4,12},{5,13},{6,14},{7,15},{8,0},{9,1},... | collective-permute-start | bytes 442376 | tf_op jit(solution)/shard_map/ppermute | solution.py:458
  12.1 7.5 %collective-permute-start.7 = (bf16[2,24,1536]{2,1,0:T(8,128)(2,1)S(1)}, bf16[2,24,1536]{2,1,0:T(8,128)(2,1)S(1)}, u32[]{:S(2)}, u32[]{:S(2)}) collective-permute-start(bf16[2,24,1536]{2,1,0:T(8,128)(2,1)S(1)} %join.10.refs_2_.refs_0_), channel_id=1, source_target_pairs={{0,1},{1,0},{2,3},{3,2},{4,5},{5,4},{6,7},{7,6},{8,9},{9,8},{10,11... | collective-permute-start | bytes 442376 | tf_op jit(solution)/shard_map/ppermute | solution.py:458
  15.9 6.6 %collective-permute-start.6 = (bf16[2,4,24,384]{3,2,1,0:T(8,128)(2,1)S(1)}, bf16[2,4,24,384]{3,2,1,0:T(8,128)(2,1)S(1)}, u32[]{:S(2)}, u32[]{:S(2)}) collective-permute-start(bf16[2,4,24,384]{3,2,1,0:T(8,128)(2,1)S(1)} %join.11.refs_2_.refs_0_), channel_id=1, source_target_pairs={{0,8},{1,9},{2,10},{3,11},{4,12},{5,13},{6,14},{7,15},{8,0},{9,1},... | collective-permute-start | bytes 442376 | tf_op jit(solution)/shard_map/ppermute | solution.py:458
  18.0 6.8 %collective-permute-start.5 = (bf16[4,24,1536]{2,1,0:T(8,128)(2,1)S(1)}, bf16[4,24,1536]{2,1,0:T(8,128)(2,1)S(1)}, u32[]{:S(2)}, u32[]{:S(2)}) collective-permute-start(bf16[4,24,1536]{2,1,0:T(8,128)(2,1)S(1)} %join.12.refs_2_.refs_0_), channel_id=1, source_target_pairs={{0,1},{1,0},{2,3},{3,2},{4,5},{5,4},{6,7},{7,6},{8,9},{9,8},{10,11... | collective-permute-start | bytes 884744 | tf_op jit(solution)/shard_map/ppermute | solution.py:458
  19.6 11.0 %collective-permute-start.11 = (bf16[4,24,1536]{2,1,0:T(8,128)(2,1)S(1)}, bf16[4,24,1536]{2,1,0:T(8,128)(2,1)S(1)}, u32[]{:S(2)}, u32[]{:S(2)}) collective-permute-start(bf16[4,24,1536]{2,1,0:T(8,128)(2,1)S(1)} %join.13.refs_2_.refs_0_), channel_id=1, source_target_pairs={{0,8},{1,9},{2,10},{3,11},{4,12},{5,13},{6,14},{7,15},{8,0},{9,1},... | collective-permute-start | bytes 884744 | tf_op jit(solution)/shard_map/ppermute | solution.py:458
  22.5 8.1 %collective-permute-start.15 = (bf16[4,4,24,384]{3,2,1,0:T(8,128)(2,1)S(1)}, bf16[4,4,24,384]{3,2,1,0:T(8,128)(2,1)S(1)}, u32[]{:S(2)}, u32[]{:S(2)}) collective-permute-start(bf16[4,4,24,384]{3,2,1,0:T(8,128)(2,1)S(1)} %join.14.refs_2_.refs_0_), channel_id=1, source_target_pairs={{0,2},{1,3},{2,0},{3,1},{4,6},{5,7},{6,4},{7,5},{8,10},{9,11},{10,... | collective-permute-start | bytes 884744 | tf_op jit(solution)/shard_map/ppermute | solution.py:458
  24.8 16.8 %collective-permute-start.8 = (bf16[8,24,1536]{2,1,0:T(8,128)(2,1)S(1)}, bf16[8,24,1536]{2,1,0:T(8,128)(2,1)S(1)}, u32[]{:S(2)}, u32[]{:S(2)}) collective-permute-start(bf16[8,24,1536]{2,1,0:T(8,128)(2,1)S(1)} %join.15.refs_0_.refs_2_), channel_id=1, source_target_pairs={{0,4},{1,5},{2,6},{3,7},{4,0},{5,1},{6,2},{7,3},{8,12},{9,13},{10,... | collective-permute-start | bytes 1769480 | tf_op jit(solution)/shard_map/ppermute | solution.py:458
  30.7 11.5 %collective-permute-start.16 = (bf16[8,4,24,384]{3,2,1,0:T(8,128)(2,1)S(1)}, bf16[8,4,24,384]{3,2,1,0:T(8,128)(2,1)S(1)}, u32[]{:S(2)}, u32[]{:S(2)}) collective-permute-start(bf16[8,4,24,384]{3,2,1,0:T(8,128)(2,1)S(1)} %join.17.refs_0_), channel_id=1, source_target_pairs={{0,1},{1,0},{2,3},{3,2},{4,5},{5,4},{6,7},{7,6},{8,9},{9,8},{10,11... | collective-permute-start | bytes 1769480 | tf_op jit(solution)/shard_map/ppermute | solution.py:458
  32.0 12.7 %collective-permute-start.12 = (bf16[8,24,1536]{2,1,0:T(8,128)(2,1)S(1)}, bf16[8,24,1536]{2,1,0:T(8,128)(2,1)S(1)}, u32[]{:S(2)}, u32[]{:S(2)}) collective-permute-start(bf16[8,24,1536]{2,1,0:T(8,128)(2,1)S(1)} %join.16.refs_0_.refs_2_), channel_id=1, source_target_pairs={{0,2},{1,3},{2,0},{3,1},{4,6},{5,7},{6,4},{7,5},{8,10},{9,11},{10,... | collective-permute-start | bytes 1769480 | tf_op jit(solution)/shard_map/ppermute | solution.py:458
  32.3 12.4 %collective-permute-start.9 = (bf16[8,24,1536]{2,1,0:T(8,128)(2,1)S(1)}, bf16[8,24,1536]{2,1,0:T(8,128)(2,1)S(1)}, u32[]{:S(2)}, u32[]{:S(2)}) collective-permute-start(bf16[8,24,1536]{2,1,0:T(8,128)(2,1)S(1)} %join.15.refs_0_.refs_2_), channel_id=1, source_target_pairs={{0,16},{16,0},{1,17},{17,1},{2,18},{18,2},{3,19},{19,3},{4,20},{20... | collective-permute-start | bytes 1769480 | tf_op jit(solution)/shard_map/ppermute | solution.py:452
  41.7 7.1 %collective-permute-start.17 = (bf16[8,4,24,384]{3,2,1,0:T(8,128)(2,1)S(1)}, bf16[8,4,24,384]{3,2,1,0:T(8,128)(2,1)S(1)}, u32[]{:S(2)}, u32[]{:S(2)}) collective-permute-start(bf16[8,4,24,384]{3,2,1,0:T(8,128)(2,1)S(1)} %join.17.refs_0_), channel_id=1, source_target_pairs={{0,16},{16,0},{1,17},{17,1},{2,18},{18,2},{3,19},{19,3},{4,20},{20... | collective-permute-start | bytes 1769480 | tf_op jit(solution)/shard_map/ppermute | solution.py:452
  42.2 6.6 %collective-permute-start.18 = (bf16[8,4,24,384]{3,2,1,0:T(8,128)(2,1)S(1)}, bf16[8,4,24,384]{3,2,1,0:T(8,128)(2,1)S(1)}, u32[]{:S(2)}, u32[]{:S(2)}) collective-permute-start(bf16[8,4,24,384]{3,2,1,0:T(8,128)(2,1)S(1)} %collective-permute-done.16.refs_1_), channel_id=1, source_target_pairs={{0,16},{16,0},{1,17},{17,1},{2,18},{18,2},{3,19},{19,3},{4,20},{20... | collective-permute-start | bytes 1769480 | tf_op jit(solution)/shard_map/ppermute | solution.py:452
  71.4 13.1 %collective-permute-start.21 = (bf16[8,3,24,768]{3,2,1,0:T(8,128)(2,1)S(1)}, bf16[8,3,24,768]{3,2,1,0:T(8,128)(2,1)S(1)}, u32[]{:S(2)}, u32[]{:S(2)}) collective-permute-start(bf16[8,3,24,768]{3,2,1,0:T(8,128)(2,1)S(1)} %get-tuple-element.147), channel_id=1, source_target_pairs={{0,4},{1,5},{2,6},{3,7},{4,0},{5,1},{6,2},{7,3},{8,12},{9,13},{10,... | collective-permute-start | bytes 2654216 | tf_op jit(solution)/shard_map/ppermute | solution.py:458
  84.7 12.1 %collective-permute-start.26 = (bf16[4,3,24,768]{3,2,1,0:T(8,128)(2,1)S(1)}, bf16[4,3,24,768]{3,2,1,0:T(8,128)(2,1)S(1)}, u32[]{:S(2)}, u32[]{:S(2)}) collective-permute-start(bf16[4,3,24,768]{3,2,1,0:T(8,128)(2,1)S(1)} %get-tuple-element.158), channel_id=1, source_target_pairs={{0,1},{1,0},{2,3},{3,2},{4,5},{5,4},{6,7},{7,6},{8,9},{9,8},{10,11... | collective-permute-start | bytes 1327112 | tf_op jit(solution)/shard_map/ppermute | solution.py:458
  87.2 13.0 %collective-permute-start.25 = (bf16[8,3,24,768]{3,2,1,0:T(8,128)(2,1)S(1)}, bf16[8,3,24,768]{3,2,1,0:T(8,128)(2,1)S(1)}, u32[]{:S(2)}, u32[]{:S(2)}) collective-permute-start(bf16[8,3,24,768]{3,2,1,0:T(8,128)(2,1)S(1)} %get-tuple-element.157), channel_id=1, source_target_pairs={{0,2},{1,3},{2,0},{3,1},{4,6},{5,7},{6,4},{7,5},{8,10},{9,11},{10,... | collective-permute-start | bytes 2654216 | tf_op jit(solution)/shard_map/ppermute | solution.py:458
  88.9 11.9 %collective-permute-start.24 = (f32[512,384]{1,0:T(8,128)S(1)}, f32[512,384]{1,0:T(8,128)S(1)}, u32[]{:S(2)}, u32[]{:S(2)}) collective-permute-start(f32[512,384]{1,0:T(8,128)S(1)} %get-tuple-element.155), channel_id=1, source_target_pairs={{0,16},{16,0},{1,17},{17,1},{2,18},{18,2},{3,19},{19,3},{4,20},{20... | collective-permute-start | bytes 2359304 | tf_op jit(solution)/shard_map/ppermute | solution.py:452
  89.0 7.9 %collective-permute-start.27 = (f32[2,384]{1,0:T(2,128)S(1)}, f32[2,384]{1,0:T(2,128)S(1)}, u32[]{:S(2)}, u32[]{:S(2)}) collective-permute-start(f32[2,384]{1,0:T(2,128)S(1)} %get-tuple-element.161), channel_id=1, source_target_pairs={{0,16},{16,0},{1,17},{17,1},{2,18},{18,2},{3,19},{19,3},{4,20},{20... | collective-permute-start | bytes 9224 | tf_op jit(solution)/shard_map/ppermute | solution.py:452
  100.4 8.4 %collective-permute-start.28 = (bf16[4,3,24,768]{3,2,1,0:T(8,128)(2,1)S(1)}, bf16[4,3,24,768]{3,2,1,0:T(8,128)(2,1)S(1)}, u32[]{:S(2)}, u32[]{:S(2)}) collective-permute-start(bf16[4,3,24,768]{3,2,1,0:T(8,128)(2,1)S(1)} %get-tuple-element.163), channel_id=1, source_target_pairs={{0,1},{1,0},{2,3},{3,2},{4,5},{5,4},{6,7},{7,6},{8,9},{9,8},{10,11... | collective-permute-start | bytes 1327112 | tf_op jit(solution)/shard_map/ppermute | solution.py:458
  100.6 7.8 %collective-permute-start.29 = (bf16[2,3,24,768]{3,2,1,0:T(8,128)(2,1)S(1)}, bf16[2,3,24,768]{3,2,1,0:T(8,128)(2,1)S(1)}, u32[]{:S(2)}, u32[]{:S(2)}) collective-permute-start(bf16[2,3,24,768]{3,2,1,0:T(8,128)(2,1)S(1)} %get-tuple-element.164), channel_id=1, source_target_pairs={{0,2},{1,3},{2,0},{3,1},{4,6},{5,7},{6,4},{7,5},{8,10},{9,11},{10,... | collective-permute-start | bytes 663560 | tf_op jit(solution)/shard_map/ppermute | solution.py:458
  108.9 7.2 %collective-permute-start.30 = (bf16[2,3,24,768]{3,2,1,0:T(8,128)(2,1)S(1)}, bf16[2,3,24,768]{3,2,1,0:T(8,128)(2,1)S(1)}, u32[]{:S(2)}, u32[]{:S(2)}) collective-permute-start(bf16[2,3,24,768]{3,2,1,0:T(8,128)(2,1)S(1)} %get-tuple-element.168), channel_id=1, source_target_pairs={{0,4},{1,5},{2,6},{3,7},{4,0},{5,1},{6,2},{7,3},{8,12},{9,13},{10,... | collective-permute-start | bytes 663560 | tf_op jit(solution)/shard_map/ppermute | solution.py:458
  109.3 7.8 %collective-permute-start.32 = (bf16[1,3,24,768]{3,2,1,0:T(8,128)(2,1)S(1)}, bf16[1,3,24,768]{3,2,1,0:T(8,128)(2,1)S(1)}, u32[]{:S(2)}, u32[]{:S(2)}) collective-permute-start(bf16[1,3,24,768]{3,2,1,0:T(8,128)(2,1)S(1)} %get-tuple-element.171), channel_id=1, source_target_pairs={{0,8},{1,9},{2,10},{3,11},{4,12},{5,13},{6,14},{7,15},{8,0},{9,1},... | collective-permute-start | bytes 331784 | tf_op jit(solution)/shard_map/ppermute | solution.py:458
  116.2 6.8 %collective-permute-start.31 = (bf16[1,3,24,768]{3,2,1,0:T(8,128)(2,1)S(1)}, bf16[1,3,24,768]{3,2,1,0:T(8,128)(2,1)S(1)}, u32[]{:S(2)}, u32[]{:S(2)}) collective-permute-start(bf16[1,3,24,768]{3,2,1,0:T(8,128)(2,1)S(1)} %get-tuple-element.170), channel_id=1, source_target_pairs={{0,8},{1,9},{2,10},{3,11},{4,12},{5,13},{6,14},{7,15},{8,0},{9,1},... | collective-permute-start | bytes 331784 | tf_op jit(solution)/shard_map/ppermute | solution.py:458
  (42 other events, 363.0 us)

commit v5 on v4

--- a/solution.py
+++ b/solution.py
@@ -853,14 +853,13 @@
         gain_got = swap_cores(nine["gain_send"])
         result, laid = lay_results(nine["own"], swap_cores(nine["send"]))
         section_result = result[None, :, None]
-        last = sum_one.step(nine["gain_own"])
-        last = sum_zero.step(last, gain_got)
-        beside = (laid,)
-        while sum_zero.turn < plan.bits:
-            if sum_one.turn < plan.bits:
-                last = sum_one.step(last)
-            last = sum_zero.step(last, *beside)
-            beside = ()
+        last = sum_zero.step(nine["gain_own"], gain_got)
+        last = sum_one.step(last)
+        last = sum_zero.step(last, laid)
+        while min(sum_one.turn, sum_zero.turn) < plan.bits:
+            for sums in (sum_one, sum_zero):
+                if sums.turn < plan.bits:
+                    last = sums.step(last)
         own, send = owners((sum_zero,), (sum_one,))
         grad_got = swap_cores(send)
 

time: 139 us -> 137 us (0.986)
  waiting for transfers between devices: 55.7 us -> 48.1 us
  starting transfers between devices: 28.4 us -> 32.2 us
    ppermute x20, waiting for transfers between devices: 49.5 us -> 41.9 us  [swap(): return lax.ppermute(block, ('pipe', 'dp'), route)]
    ppermute x20, starting transfers between devices: 24.9 us -> 28.7 us  [swap(): return lax.ppermute(block, ('pipe', 'dp'), route)]
where the time goes in v5:
time: 137 us
  waiting for transfers between devices  48.1 us (35%)
  Pallas kernels  36.3 us (26%)
  starting transfers between devices  32.2 us (24%)
  blocking collectives  12.6 us (9%)
  other arithmetic  3.53 us (3%)
  local copies, waits for them, and re-layouts  2.56 us (2%)
  between operations  1.42 us (1%)
    ppermute x20, waiting for transfers between devices, swap(): return lax.ppermute(block, ('pipe', 'dp'), route)  41.9 us
    pallas_call x9, Pallas kernels, run_kernel(): pl.pallas_call(kernel, name=name, out_shape=[struct(*v) for v in outs.val...  30.1 us
    ppermute x20, starting transfers between devices, swap(): return lax.ppermute(block, ('pipe', 'dp'), route)  28.7 us
    all_to_all x1, blocking collectives, per_device(): small = lax.all_to_all(small, 'dp', 0, 0)  12.6 us
    pallas_call x24, Pallas kernels, small_kernel(): pl.pallas_call(run, name=name, out_shape=outs, in_specs=[VM] * len(inputs...  6.19 us
    ppermute x14, waiting for transfers between devices, swap_cores(): return lax.ppermute(block, 'pipe', [(0, 1), (1, 0)])  6.18 us
    convert_element_type x4, other arithmetic, per_device(): low = [m.astype(BF) for m in masters]  3.52 us
    ppermute x14, starting transfers between devices, swap_cores(): return lax.ppermute(block, 'pipe', [(0, 1), (1, 0)])  3.51 us
  transfers between devices with their start and end apart: 34, of which 18 were waited for; matrix products, arithmetic and copies ran while one was open for 1% of the time, Pallas kernels for 12%

profile of v5, /device:TPU:0, one launch (start us, length us, event | category | flops | bytes accessed | tf_op | source)
XLA Modules:
  0.0 136.7 jit_solution(11903931478561239361)
XLA Ops:
  2.4 3.0 %collective-permute-start.1 = (bf16[1,24,1536]{2,1,0:T(8,128)(2,1)S(1)}, bf16[1,24,1536]{2,1,0:T(8,128)(2,1)S(1)}, u32[]{:S(2)}, u32[]{:S(2)}) collective-permute-start(bf16[1,24,1536]{2,1,0:T(8,128)(2,1)S(1)} %maximum_bitcast_fusion.refs_0_), channel_id=1, source_target_pairs={{0,2},{1,3},{2,0},{3,1},{4,6},{5,7},{6,4},{7,5},{8,10},{9,11},{10,... | collective-permute-start | bytes 221192 | tf_op jit(solution)/shard_map/ppermute | solution.py:458
  9.4 2.7 %collective-permute-start.2 = (bf16[2,24,1536]{2,1,0:T(8,128)(2,1)S(1)}, bf16[2,24,1536]{2,1,0:T(8,128)(2,1)S(1)}, u32[]{:S(2)}, u32[]{:S(2)}) collective-permute-start(bf16[2,24,1536]{2,1,0:T(8,128)(2,1)S(1)} %join.9.refs_2_.refs_0_), channel_id=1, source_target_pairs={{0,8},{1,9},{2,10},{3,11},{4,12},{5,13},{6,14},{7,15},{8,0},{9,1},... | collective-permute-start | bytes 442376 | tf_op jit(solution)/shard_map/ppermute | solution.py:458
  13.6 2.2 %collective-permute-done.3.refs_1_ = bf16[1,4,24,384]{3,2,1,0:T(8,128)(2,1)S(1)} collective-permute-done((bf16[1,4,24,384]{3,2,1,0:T(8,128)(2,1)S(1)}, bf16[1,4,24,384]{3,2,1,0:T(8,128)(2,1)S(1)}, u32[]{:S(2)}, u32[]{:S(2)}) %collective-permute-start.3) | collective-permute-done | bytes 73760 | tf_op jit(solution)/shard_map/ppermute | solution.py:458
  19.6 2.1 %collective-permute-start.11 = (bf16[4,24,1536]{2,1,0:T(8,128)(2,1)S(1)}, bf16[4,24,1536]{2,1,0:T(8,128)(2,1)S(1)}, u32[]{:S(2)}, u32[]{:S(2)}) collective-permute-start(bf16[4,24,1536]{2,1,0:T(8,128)(2,1)S(1)} %join.13.refs_2_.refs_0_), channel_id=1, source_target_pairs={{0,8},{1,9},{2,10},{3,11},{4,12},{5,13},{6,14},{7,15},{8,0},{9,1},... | collective-permute-start | bytes 884744 | tf_op jit(solution)/shard_map/ppermute | solution.py:458
  22.6 2.2 %collective-permute-done.5.refs_1_ = bf16[4,24,1536]{2,1,0:T(8,128)(2,1)S(1)} collective-permute-done((bf16[4,24,1536]{2,1,0:T(8,128)(2,1)S(1)}, bf16[4,24,1536]{2,1,0:T(8,128)(2,1)S(1)}, u32[]{:S(2)}, u32[]{:S(2)}) %collective-permute-start.5) | collective-permute-done | bytes 294944 | tf_op jit(solution)/shard_map/ppermute | solution.py:458
  25.8 4.8 %collective-permute-done.11.refs_1_ = bf16[4,24,1536]{2,1,0:T(8,128)(2,1)S(1)} collective-permute-done((bf16[4,24,1536]{2,1,0:T(8,128)(2,1)S(1)}, bf16[4,24,1536]{2,1,0:T(8,128)(2,1)S(1)}, u32[]{:S(2)}, u32[]{:S(2)}) %collective-permute-start.11) | collective-permute-done | bytes 294944 | tf_op jit(solution)/shard_map/ppermute | solution.py:458
  32.3 9.4 %collective-permute-done.8.refs_1_ = bf16[8,24,1536]{2,1,0:T(8,128)(2,1)S(1)} collective-permute-done((bf16[8,24,1536]{2,1,0:T(8,128)(2,1)S(1)}, bf16[8,24,1536]{2,1,0:T(8,128)(2,1)S(1)}, u32[]{:S(2)}, u32[]{:S(2)}) %collective-permute-start.8) | collective-permute-done | bytes 589856 | tf_op jit(solution)/shard_map/ppermute | solution.py:458
  42.8 1.9 %collective-permute-done.12.refs_1_ = bf16[8,24,1536]{2,1,0:T(8,128)(2,1)S(1)} collective-permute-done((bf16[8,24,1536]{2,1,0:T(8,128)(2,1)S(1)}, bf16[8,24,1536]{2,1,0:T(8,128)(2,1)S(1)}, u32[]{:S(2)}, u32[]{:S(2)}) %collective-permute-start.12) | collective-permute-done | bytes 589856 | tf_op jit(solution)/shard_map/ppermute | solution.py:458
  45.4 3.4 %extractor_attention.1 = (bf16[512,384]{1,0:T(8,128)(2,1)S(1)}, bf16[512,1152]{1,0:T(8,128)(2,1)S(1)}, bf16[3,1152,256]{2,1,0:T(8,128)(2,1)S(1)}, bf16[384,512]{...) custom-call(f32[2,384]{1,0:T(2,128)S(1)} %bitcast.77, ...), custom_call_target="tpu_custom_call" | custom-call | flops 10 | bytes 8 | tf_op jit(solution)/shard_map/extractor_attention/pallas_call | solution.py:362
  50.2 3.2 %extractor_feed.1 = (bf16[512,1536]{1,0:T(8,128)(2,1)S(1)}, bf16[512,1536]{1,0:T(8,128)(2,1)S(1)}, f32[512,384]{1,0:T(8,128)S(1)}) custom-call(bf16[512,384]{1,0:T(8,128)(2,1)S(1)} %get-tuple-element.111.refs_4_.refs_0_.refs_5_, f32[512,384]{1,0:T(8,128)S(1)} %get-tuple-element.112.refs_1_.refs_6_, bf16[2,1,512,384]{3,2,1,0:T(8,128)(2,1)S(1)} %copy-done.9, ...), custom_call_target="tpu_custom_call" | custom-call | flops 32000000000 | bytes 8 | tf_op jit(solution)/shard_map/extractor_feed/pallas_call | solution.py:362
  53.4 3.3 %generator_attention.1 = (bf16[512,384]{1,0:T(8,128)(2,1)S(1)}, bf16[512,1152]{1,0:T(8,128)(2,1)S(1)}, bf16[3,1152,256]{2,1,0:T(8,128)(2,1)S(1)}, bf16[384,512]{...) custom-call(f32[2,384]{1,0:T(2,128)S(1)} %bitcast.78, ...), custom_call_target="tpu_custom_call" | custom-call | flops 10 | bytes 8 | tf_op jit(solution)/shard_map/generator_attention/pallas_call | solution.py:362
  56.8 6.3 %generator_feed.1 = (f32[512,384]{1,0:T(8,128)S(1)}, f32[512,384]{1,0:T(8,128)S(1)}, bf16[512,384]{1,0:T(8,128)(2,1)S(1)}, f32[1,384]{1,0:T(1,128)S(1)}, bf16[16...) custom-call(f32[2,384]{1,0:T(2,128)S(1)} %bitcast.79, ...), custom_call_target="tpu_custom_call" | custom-call | flops 99999997952 | bytes 8 | tf_op jit(solution)/shard_map/generator_feed/pallas_call | solution.py:362
  63.1 4.1 %generator_attention_back.1 = (bf16[16,1,24,768]{3,2,1,0:T(8,128)(2,1)S(1)}, bf16[16,1,24,768]{3,2,1,0:T(8,128)(2,1)S(1)}, bf16[512,1152]{1,0:T(8,128)(2,1)S(1)}) custom-call(bf16[512,384]{1,0:T(8,128)(2,1)S(1)} %get-tuple-element.121.refs_0_, bf16[384,512]{1,0:T(8,128)(2,1)S(1)} %get-tuple-element.122.refs_1_, ...), custom_call_target="tpu_custom_call" | custom-call | flops 60000002048 | bytes 8 | tf_op jit(solution)/shard_map/generator_attention_back/pallas_call | solution.py:362
  72.9 3.5 %extractor_feed_back.1 = (bf16[16,2,24,768]{3,2,1,0:T(8,128)(2,1)S(1)}, bf16[16,2,24,768]{3,2,1,0:T(8,128)(2,1)S(1)}, f32[512,384]{1,0:T(8,128)S(1)}, bf16[512,384]{1,0:T(8,128)(2,1)S(1)}, f32[1,384]{1,0:T(1,128)S(1)}) custom-call(f32[2,384]{1,0:T(2,128)S(1)} %bitcast.81, f32[2,384]{1,0:T(2,128)S(1)} %collective-permute-done.refs_3_.refs_1_, ...), custom_call_target="tpu_custom_call" | custom-call | flops 70000001024 | bytes 8 | tf_op jit(solution)/shard_map/extractor_feed_back/pallas_call | solution.py:362
  76.6 3.8 %extractor_attention_back.1 = (bf16[16,1,24,768]{3,2,1,0:T(8,128)(2,1)S(1)}, bf16[16,1,24,768]{3,2,1,0:T(8,128)(2,1)S(1)}, bf16[512,1152]{1,0:T(8,128)(2,1)S(1)}) custom-call(bf16[512,384]{1,0:T(8,128)(2,1)S(1)} %get-tuple-element.136.refs_0_, bf16[384,512]{1,0:T(8,128)(2,1)S(1)} %get-tuple-element.137.refs_1_, ...), custom_call_target="tpu_custom_call" | custom-call | flops 60000002048 | bytes 8 | tf_op jit(solution)/shard_map/extractor_attention_back/pallas_call | solution.py:362
  87.6 2.4 %collective-permute-start.28 = (bf16[4,3,24,768]{3,2,1,0:T(8,128)(2,1)S(1)}, bf16[4,3,24,768]{3,2,1,0:T(8,128)(2,1)S(1)}, u32[]{:S(2)}, u32[]{:S(2)}) collective-permute-start(bf16[4,3,24,768]{3,2,1,0:T(8,128)(2,1)S(1)} %get-tuple-element.162), channel_id=1, source_target_pairs={{0,1},{1,0},{2,3},{3,2},{4,5},{5,4},{6,7},{7,6},{8,9},{9,8},{10,11... | collective-permute-start | bytes 1327112 | tf_op jit(solution)/shard_map/ppermute | solution.py:458
  90.1 6.0 %collective-permute-done.25.refs_1_ = bf16[8,3,24,768]{3,2,1,0:T(8,128)(2,1)S(1)} collective-permute-done((bf16[8,3,24,768]{3,2,1,0:T(8,128)(2,1)S(1)}, bf16[8,3,24,768]{3,2,1,0:T(8,128)(2,1)S(1)}, u32[]{:S(2)}, u32[]{:S(2)}) %collective-permute-start.25) | collective-permute-done | bytes 884768 | tf_op jit(solution)/shard_map/ppermute | solution.py:458
  96.2 2.5 %collective-permute-start.27 = (bf16[4,3,24,768]{3,2,1,0:T(8,128)(2,1)S(1)}, bf16[4,3,24,768]{3,2,1,0:T(8,128)(2,1)S(1)}, u32[]{:S(2)}, u32[]{:S(2)}) collective-permute-start(bf16[4,3,24,768]{3,2,1,0:T(8,128)(2,1)S(1)} %get-tuple-element.161), channel_id=1, source_target_pairs={{0,1},{1,0},{2,3},{3,2},{4,5},{5,4},{6,7},{7,6},{8,9},{9,8},{10,11... | collective-permute-start | bytes 1327112 | tf_op jit(solution)/shard_map/ppermute | solution.py:458
  101.2 4.0 %collective-permute-done.27.refs_1_ = bf16[4,3,24,768]{3,2,1,0:T(8,128)(2,1)S(1)} collective-permute-done((bf16[4,3,24,768]{3,2,1,0:T(8,128)(2,1)S(1)}, bf16[4,3,24,768]{3,2,1,0:T(8,128)(2,1)S(1)}, u32[]{:S(2)}, u32[]{:S(2)}) %collective-permute-start.27) | collective-permute-done | bytes 442400 | tf_op jit(solution)/shard_map/ppermute | solution.py:458
  106.6 2.7 %collective-permute-start.32 = (bf16[1,3,24,768]{3,2,1,0:T(8,128)(2,1)S(1)}, bf16[1,3,24,768]{3,2,1,0:T(8,128)(2,1)S(1)}, u32[]{:S(2)}, u32[]{:S(2)}) collective-permute-start(bf16[1,3,24,768]{3,2,1,0:T(8,128)(2,1)S(1)} %get-tuple-element.171), channel_id=1, source_target_pairs={{0,8},{1,9},{2,10},{3,11},{4,12},{5,13},{6,14},{7,15},{8,0},{9,1},... | collective-permute-start | bytes 331784 | tf_op jit(solution)/shard_map/ppermute | solution.py:458
  109.4 3.7 %collective-permute-done.29.refs_1_ = bf16[2,3,24,768]{3,2,1,0:T(8,128)(2,1)S(1)} collective-permute-done((bf16[2,3,24,768]{3,2,1,0:T(8,128)(2,1)S(1)}, bf16[2,3,24,768]{3,2,1,0:T(8,128)(2,1)S(1)}, u32[]{:S(2)}, u32[]{:S(2)}) %collective-permute-start.29) | collective-permute-done | bytes 221216 | tf_op jit(solution)/shard_map/ppermute | solution.py:458
  113.1 1.9 %collective-permute-start.31 = (bf16[1,3,24,768]{3,2,1,0:T(8,128)(2,1)S(1)}, bf16[1,3,24,768]{3,2,1,0:T(8,128)(2,1)S(1)}, u32[]{:S(2)}, u32[]{:S(2)}) collective-permute-start(bf16[1,3,24,768]{3,2,1,0:T(8,128)(2,1)S(1)} %get-tuple-element.170), channel_id=1, source_target_pairs={{0,8},{1,9},{2,10},{3,11},{4,12},{5,13},{6,14},{7,15},{8,0},{9,1},... | collective-permute-start | bytes 331784 | tf_op jit(solution)/shard_map/ppermute | solution.py:458
  115.0 5.0 %collective-permute-done.31.refs_1_ = bf16[1,3,24,768]{3,2,1,0:T(8,128)(2,1)S(1)} collective-permute-done((bf16[1,3,24,768]{3,2,1,0:T(8,128)(2,1)S(1)}, bf16[1,3,24,768]{3,2,1,0:T(8,128)(2,1)S(1)}, u32[]{:S(2)}, u32[]{:S(2)}) %collective-permute-start.31) | collective-permute-done | bytes 110624 | tf_op jit(solution)/shard_map/ppermute | solution.py:458
  122.9 12.6 %all_to_all.5.refs_0_ = f32[16,3,384]{2,1,0:T(4,128)S(1)} all-to-all(f32[16,3,384]{2,1,0:T(4,128)S(1)} %get-tuple-element.182), channel_id=1, replica_groups=mesh['pipe'=2,'dp'=16] {'dp'}, dimensions={0} | all-to-all | bytes 147456 | tf_op jit(solution)/shard_map/all_to_all | solution.py:869
  (147 shorter events, 38.5 us)
Async XLA Ops:
  2.4 7.0 %collective-permute-start.1 = (bf16[1,24,1536]{2,1,0:T(8,128)(2,1)S(1)}, bf16[1,24,1536]{2,1,0:T(8,128)(2,1)S(1)}, u32[]{:S(2)}, u32[]{:S(2)}) collective-permute-start(bf16[1,24,1536]{2,1,0:T(8,128)(2,1)S(1)} %maximum_bitcast_fusion.refs_0_), channel_id=1, source_target_pairs={{0,2},{1,3},{2,0},{3,1},{4,6},{5,7},{6,4},{7,5},{8,10},{9,11},{10,... | collective-permute-start | bytes 221192 | tf_op jit(solution)/shard_map/ppermute | solution.py:458
  8.9 7.0 %collective-permute-start.3 = (bf16[1,4,24,384]{3,2,1,0:T(8,128)(2,1)S(1)}, bf16[1,4,24,384]{3,2,1,0:T(8,128)(2,1)S(1)}, u32[]{:S(2)}, u32[]{:S(2)}) collective-permute-start(bf16[1,4,24,384]{3,2,1,0:T(8,128)(2,1)S(1)} %bitcast.66), channel_id=1, source_target_pairs={{0,4},{1,5},{2,6},{3,7},{4,0},{5,1},{6,2},{7,3},{8,12},{9,13},{10,... | collective-permute-start | bytes 221192 | tf_op jit(solution)/shard_map/ppermute | solution.py:458
  9.4 8.6 %collective-permute-start.2 = (bf16[2,24,1536]{2,1,0:T(8,128)(2,1)S(1)}, bf16[2,24,1536]{2,1,0:T(8,128)(2,1)S(1)}, u32[]{:S(2)}, u32[]{:S(2)}) collective-permute-start(bf16[2,24,1536]{2,1,0:T(8,128)(2,1)S(1)} %join.9.refs_2_.refs_0_), channel_id=1, source_target_pairs={{0,8},{1,9},{2,10},{3,11},{4,12},{5,13},{6,14},{7,15},{8,0},{9,1},... | collective-permute-start | bytes 442376 | tf_op jit(solution)/shard_map/ppermute | solution.py:458
  12.1 7.5 %collective-permute-start.7 = (bf16[2,24,1536]{2,1,0:T(8,128)(2,1)S(1)}, bf16[2,24,1536]{2,1,0:T(8,128)(2,1)S(1)}, u32[]{:S(2)}, u32[]{:S(2)}) collective-permute-start(bf16[2,24,1536]{2,1,0:T(8,128)(2,1)S(1)} %join.10.refs_2_.refs_0_), channel_id=1, source_target_pairs={{0,1},{1,0},{2,3},{3,2},{4,5},{5,4},{6,7},{7,6},{8,9},{9,8},{10,11... | collective-permute-start | bytes 442376 | tf_op jit(solution)/shard_map/ppermute | solution.py:458
  15.9 6.6 %collective-permute-start.6 = (bf16[2,4,24,384]{3,2,1,0:T(8,128)(2,1)S(1)}, bf16[2,4,24,384]{3,2,1,0:T(8,128)(2,1)S(1)}, u32[]{:S(2)}, u32[]{:S(2)}) collective-permute-start(bf16[2,4,24,384]{3,2,1,0:T(8,128)(2,1)S(1)} %join.11.refs_2_.refs_0_), channel_id=1, source_target_pairs={{0,8},{1,9},{2,10},{3,11},{4,12},{5,13},{6,14},{7,15},{8,0},{9,1},... | collective-permute-start | bytes 442376 | tf_op jit(solution)/shard_map/ppermute | solution.py:458
  18.0 6.8 %collective-permute-start.5 = (bf16[4,24,1536]{2,1,0:T(8,128)(2,1)S(1)}, bf16[4,24,1536]{2,1,0:T(8,128)(2,1)S(1)}, u32[]{:S(2)}, u32[]{:S(2)}) collective-permute-start(bf16[4,24,1536]{2,1,0:T(8,128)(2,1)S(1)} %join.12.refs_2_.refs_0_), channel_id=1, source_target_pairs={{0,1},{1,0},{2,3},{3,2},{4,5},{5,4},{6,7},{7,6},{8,9},{9,8},{10,11... | collective-permute-start | bytes 884744 | tf_op jit(solution)/shard_map/ppermute | solution.py:458
  19.6 11.0 %collective-permute-start.11 = (bf16[4,24,1536]{2,1,0:T(8,128)(2,1)S(1)}, bf16[4,24,1536]{2,1,0:T(8,128)(2,1)S(1)}, u32[]{:S(2)}, u32[]{:S(2)}) collective-permute-start(bf16[4,24,1536]{2,1,0:T(8,128)(2,1)S(1)} %join.13.refs_2_.refs_0_), channel_id=1, source_target_pairs={{0,8},{1,9},{2,10},{3,11},{4,12},{5,13},{6,14},{7,15},{8,0},{9,1},... | collective-permute-start | bytes 884744 | tf_op jit(solution)/shard_map/ppermute | solution.py:458
  22.5 8.1 %collective-permute-start.15 = (bf16[4,4,24,384]{3,2,1,0:T(8,128)(2,1)S(1)}, bf16[4,4,24,384]{3,2,1,0:T(8,128)(2,1)S(1)}, u32[]{:S(2)}, u32[]{:S(2)}) collective-permute-start(bf16[4,4,24,384]{3,2,1,0:T(8,128)(2,1)S(1)} %join.14.refs_2_.refs_0_), channel_id=1, source_target_pairs={{0,2},{1,3},{2,0},{3,1},{4,6},{5,7},{6,4},{7,5},{8,10},{9,11},{10,... | collective-permute-start | bytes 884744 | tf_op jit(solution)/shard_map/ppermute | solution.py:458
  24.8 16.8 %collective-permute-start.8 = (bf16[8,24,1536]{2,1,0:T(8,128)(2,1)S(1)}, bf16[8,24,1536]{2,1,0:T(8,128)(2,1)S(1)}, u32[]{:S(2)}, u32[]{:S(2)}) collective-permute-start(bf16[8,24,1536]{2,1,0:T(8,128)(2,1)S(1)} %join.15.refs_0_.refs_2_), channel_id=1, source_target_pairs={{0,4},{1,5},{2,6},{3,7},{4,0},{5,1},{6,2},{7,3},{8,12},{9,13},{10,... | collective-permute-start | bytes 1769480 | tf_op jit(solution)/shard_map/ppermute | solution.py:458
  30.7 11.5 %collective-permute-start.16 = (bf16[8,4,24,384]{3,2,1,0:T(8,128)(2,1)S(1)}, bf16[8,4,24,384]{3,2,1,0:T(8,128)(2,1)S(1)}, u32[]{:S(2)}, u32[]{:S(2)}) collective-permute-start(bf16[8,4,24,384]{3,2,1,0:T(8,128)(2,1)S(1)} %join.17.refs_0_), channel_id=1, source_target_pairs={{0,1},{1,0},{2,3},{3,2},{4,5},{5,4},{6,7},{7,6},{8,9},{9,8},{10,11... | collective-permute-start | bytes 1769480 | tf_op jit(solution)/shard_map/ppermute | solution.py:458
  32.0 12.7 %collective-permute-start.12 = (bf16[8,24,1536]{2,1,0:T(8,128)(2,1)S(1)}, bf16[8,24,1536]{2,1,0:T(8,128)(2,1)S(1)}, u32[]{:S(2)}, u32[]{:S(2)}) collective-permute-start(bf16[8,24,1536]{2,1,0:T(8,128)(2,1)S(1)} %join.16.refs_0_.refs_2_), channel_id=1, source_target_pairs={{0,2},{1,3},{2,0},{3,1},{4,6},{5,7},{6,4},{7,5},{8,10},{9,11},{10,... | collective-permute-start | bytes 1769480 | tf_op jit(solution)/shard_map/ppermute | solution.py:458
  32.3 12.4 %collective-permute-start.9 = (bf16[8,24,1536]{2,1,0:T(8,128)(2,1)S(1)}, bf16[8,24,1536]{2,1,0:T(8,128)(2,1)S(1)}, u32[]{:S(2)}, u32[]{:S(2)}) collective-permute-start(bf16[8,24,1536]{2,1,0:T(8,128)(2,1)S(1)} %join.15.refs_0_.refs_2_), channel_id=1, source_target_pairs={{0,16},{16,0},{1,17},{17,1},{2,18},{18,2},{3,19},{19,3},{4,20},{20... | collective-permute-start | bytes 1769480 | tf_op jit(solution)/shard_map/ppermute | solution.py:452
  41.7 7.1 %collective-permute-start.17 = (bf16[8,4,24,384]{3,2,1,0:T(8,128)(2,1)S(1)}, bf16[8,4,24,384]{3,2,1,0:T(8,128)(2,1)S(1)}, u32[]{:S(2)}, u32[]{:S(2)}) collective-permute-start(bf16[8,4,24,384]{3,2,1,0:T(8,128)(2,1)S(1)} %join.17.refs_0_), channel_id=1, source_target_pairs={{0,16},{16,0},{1,17},{17,1},{2,18},{18,2},{3,19},{19,3},{4,20},{20... | collective-permute-start | bytes 1769480 | tf_op jit(solution)/shard_map/ppermute | solution.py:452
  42.2 6.6 %collective-permute-start.18 = (bf16[8,4,24,384]{3,2,1,0:T(8,128)(2,1)S(1)}, bf16[8,4,24,384]{3,2,1,0:T(8,128)(2,1)S(1)}, u32[]{:S(2)}, u32[]{:S(2)}) collective-permute-start(bf16[8,4,24,384]{3,2,1,0:T(8,128)(2,1)S(1)} %collective-permute-done.16.refs_1_), channel_id=1, source_target_pairs={{0,16},{16,0},{1,17},{17,1},{2,18},{18,2},{3,19},{19,3},{4,20},{20... | collective-permute-start | bytes 1769480 | tf_op jit(solution)/shard_map/ppermute | solution.py:452
  71.4 13.1 %collective-permute-start.21 = (bf16[8,3,24,768]{3,2,1,0:T(8,128)(2,1)S(1)}, bf16[8,3,24,768]{3,2,1,0:T(8,128)(2,1)S(1)}, u32[]{:S(2)}, u32[]{:S(2)}) collective-permute-start(bf16[8,3,24,768]{3,2,1,0:T(8,128)(2,1)S(1)} %get-tuple-element.147), channel_id=1, source_target_pairs={{0,4},{1,5},{2,6},{3,7},{4,0},{5,1},{6,2},{7,3},{8,12},{9,13},{10,... | collective-permute-start | bytes 2654216 | tf_op jit(solution)/shard_map/ppermute | solution.py:458
  76.4 6.1 %collective-permute-start.23 = (bf16[16,2,24,768]{3,2,1,0:T(8,128)(2,1)S(1)}, bf16[16,2,24,768]{3,2,1,0:T(8,128)(2,1)S(1)}, u32[]{:S(2)}, u32[]{:S(2)}) collective-permute-start(bf16[16,2,24,768]{3,2,1,0:T(8,128)(2,1)S(1)} %get-tuple-element.151), channel_id=1, source_target_pairs={{0,16},{16,0},{1,17},{17,1},{2,18},{18,2},{3,19},{19,3},{4,20},{20... | collective-permute-start | bytes 3538952 | tf_op jit(solution)/shard_map/ppermute | solution.py:452
  82.9 13.1 %collective-permute-start.25 = (bf16[8,3,24,768]{3,2,1,0:T(8,128)(2,1)S(1)}, bf16[8,3,24,768]{3,2,1,0:T(8,128)(2,1)S(1)}, u32[]{:S(2)}, u32[]{:S(2)}) collective-permute-start(bf16[8,3,24,768]{3,2,1,0:T(8,128)(2,1)S(1)} %get-tuple-element.157), channel_id=1, source_target_pairs={{0,2},{1,3},{2,0},{3,1},{4,6},{5,7},{6,4},{7,5},{8,10},{9,11},{10,... | collective-permute-start | bytes 2654216 | tf_op jit(solution)/shard_map/ppermute | solution.py:458
  87.0 11.7 %collective-permute-start.24 = (f32[512,384]{1,0:T(8,128)S(1)}, f32[512,384]{1,0:T(8,128)S(1)}, u32[]{:S(2)}, u32[]{:S(2)}) collective-permute-start(f32[512,384]{1,0:T(8,128)S(1)} %get-tuple-element.155), channel_id=1, source_target_pairs={{0,16},{16,0},{1,17},{17,1},{2,18},{18,2},{3,19},{19,3},{4,20},{20... | collective-permute-start | bytes 2359304 | tf_op jit(solution)/shard_map/ppermute | solution.py:452
  87.6 12.9 %collective-permute-start.28 = (bf16[4,3,24,768]{3,2,1,0:T(8,128)(2,1)S(1)}, bf16[4,3,24,768]{3,2,1,0:T(8,128)(2,1)S(1)}, u32[]{:S(2)}, u32[]{:S(2)}) collective-permute-start(bf16[4,3,24,768]{3,2,1,0:T(8,128)(2,1)S(1)} %get-tuple-element.162), channel_id=1, source_target_pairs={{0,1},{1,0},{2,3},{3,2},{4,5},{5,4},{6,7},{7,6},{8,9},{9,8},{10,11... | collective-permute-start | bytes 1327112 | tf_op jit(solution)/shard_map/ppermute | solution.py:458
  96.2 9.0 %collective-permute-start.27 = (bf16[4,3,24,768]{3,2,1,0:T(8,128)(2,1)S(1)}, bf16[4,3,24,768]{3,2,1,0:T(8,128)(2,1)S(1)}, u32[]{:S(2)}, u32[]{:S(2)}) collective-permute-start(bf16[4,3,24,768]{3,2,1,0:T(8,128)(2,1)S(1)} %get-tuple-element.161), channel_id=1, source_target_pairs={{0,1},{1,0},{2,3},{3,2},{4,5},{5,4},{6,7},{7,6},{8,9},{9,8},{10,11... | collective-permute-start | bytes 1327112 | tf_op jit(solution)/shard_map/ppermute | solution.py:458
  100.6 6.0 %collective-permute-start.30 = (bf16[2,3,24,768]{3,2,1,0:T(8,128)(2,1)S(1)}, bf16[2,3,24,768]{3,2,1,0:T(8,128)(2,1)S(1)}, u32[]{:S(2)}, u32[]{:S(2)}) collective-permute-start(bf16[2,3,24,768]{3,2,1,0:T(8,128)(2,1)S(1)} %get-tuple-element.167), channel_id=1, source_target_pairs={{0,2},{1,3},{2,0},{3,1},{4,6},{5,7},{6,4},{7,5},{8,10},{9,11},{10,... | collective-permute-start | bytes 663560 | tf_op jit(solution)/shard_map/ppermute | solution.py:458
  105.5 7.6 %collective-permute-start.29 = (bf16[2,3,24,768]{3,2,1,0:T(8,128)(2,1)S(1)}, bf16[2,3,24,768]{3,2,1,0:T(8,128)(2,1)S(1)}, u32[]{:S(2)}, u32[]{:S(2)}) collective-permute-start(bf16[2,3,24,768]{3,2,1,0:T(8,128)(2,1)S(1)} %get-tuple-element.166), channel_id=1, source_target_pairs={{0,4},{1,5},{2,6},{3,7},{4,0},{5,1},{6,2},{7,3},{8,12},{9,13},{10,... | collective-permute-start | bytes 663560 | tf_op jit(solution)/shard_map/ppermute | solution.py:458
  106.6 8.4 %collective-permute-start.32 = (bf16[1,3,24,768]{3,2,1,0:T(8,128)(2,1)S(1)}, bf16[1,3,24,768]{3,2,1,0:T(8,128)(2,1)S(1)}, u32[]{:S(2)}, u32[]{:S(2)}) collective-permute-start(bf16[1,3,24,768]{3,2,1,0:T(8,128)(2,1)S(1)} %get-tuple-element.171), channel_id=1, source_target_pairs={{0,8},{1,9},{2,10},{3,11},{4,12},{5,13},{6,14},{7,15},{8,0},{9,1},... | collective-permute-start | bytes 331784 | tf_op jit(solution)/shard_map/ppermute | solution.py:458
  113.1 6.9 %collective-permute-start.31 = (bf16[1,3,24,768]{3,2,1,0:T(8,128)(2,1)S(1)}, bf16[1,3,24,768]{3,2,1,0:T(8,128)(2,1)S(1)}, u32[]{:S(2)}, u32[]{:S(2)}) collective-permute-start(bf16[1,3,24,768]{3,2,1,0:T(8,128)(2,1)S(1)} %get-tuple-element.170), channel_id=1, source_target_pairs={{0,8},{1,9},{2,10},{3,11},{4,12},{5,13},{6,14},{7,15},{8,0},{9,1},... | collective-permute-start | bytes 331784 | tf_op jit(solution)/shard_map/ppermute | solution.py:458
  (42 other events, 364.4 us)

commit v6 on v5

--- a/solution.py
+++ b/solution.py
@@ -254,7 +254,7 @@
             ((near, x, far, y), (far, x, near, y)),
             ((near, far, y, x), (far, x, y, near)),
         )
-        scatters = (((y, x, near, far), (near, y, x, far)), ((near, x, y, far), (y, x, far, near)))
+        scatters = (((y, x, near, far), (near, y, x, far)), ((near, x, far, y), (y, x, far, near)))
         self.gather_orders = tuple(tuple(rest + o for o in pair) for pair in gathers)
         self.scatter_orders = tuple(tuple(o + rest for o in pair) for pair in scatters)
         self.thin = (D // self.count) % 8 != 0

time: 137 us -> 139 us (1.015)
  waiting for transfers between devices: 48.1 us -> 51.9 us
  starting transfers between devices: 32.2 us -> 30.7 us
    ppermute x20, waiting for transfers between devices: 41.9 us -> 45.7 us  [swap(): return lax.ppermute(block, ('pipe', 'dp'), route)]
    ppermute x20, starting transfers between devices: 28.7 us -> 27.2 us  [swap(): return lax.ppermute(block, ('pipe', 'dp'), route)]
  transfers between devices with their start and end apart: 34 -> 34, of which waited for: 18 -> 19; matrix products, arithmetic and copies ran while one was open for 1% -> 1% of each run, Pallas kernels for 12% -> 12%
where the time goes in v6:
time: 139 us; the launch traced here: 138 us
  waiting for transfers between devices  51.9 us (37%)
  Pallas kernels  36.3 us (26%)
  starting transfers between devices  30.7 us (22%)
  blocking collectives  12 us (9%)
  other arithmetic  3.53 us (3%)
  local copies, waits for them, and re-layouts  2.56 us (2%)
  between operations  1.42 us (1%)
    ppermute x20, waiting for transfers between devices, swap(): return lax.ppermute(block, ('pipe', 'dp'), route)  45.7 us
    pallas_call x9, Pallas kernels, run_kernel(): pl.pallas_call(kernel, name=name, out_shape=[struct(*v) for v in outs.val...  30.1 us
    ppermute x20, starting transfers between devices, swap(): return lax.ppermute(block, ('pipe', 'dp'), route)  27.2 us
    all_to_all x1, blocking collectives, per_device(): small = lax.all_to_all(small, 'dp', 0, 0)  12 us
    pallas_call x24, Pallas kernels, small_kernel(): pl.pallas_call(run, name=name, out_shape=outs, in_specs=[VM] * len(inputs...  6.19 us
    ppermute x14, waiting for transfers between devices, swap_cores(): return lax.ppermute(block, 'pipe', [(0, 1), (1, 0)])  6.18 us
    convert_element_type x4, other arithmetic, per_device(): low = [m.astype(BF) for m in masters]  3.52 us
    ppermute x14, starting transfers between devices, swap_cores(): return lax.ppermute(block, 'pipe', [(0, 1), (1, 0)])  3.51 us
  transfers between devices with their start and end apart: 34, of which 19 were waited for; matrix products, arithmetic and copies ran while one was open for 1% of the time, Pallas kernels for 12%

profile of v6, /device:TPU:0, one launch (start us, length us, event | category | flops | bytes accessed | tf_op | source)
XLA Modules:
  0.0 138.4 jit_solution(15202725109203753424)
XLA Ops:
  2.4 3.0 %collective-permute-start.1 = (bf16[1,24,1536]{2,1,0:T(8,128)(2,1)S(1)}, bf16[1,24,1536]{2,1,0:T(8,128)(2,1)S(1)}, u32[]{:S(2)}, u32[]{:S(2)}) collective-permute-start(bf16[1,24,1536]{2,1,0:T(8,128)(2,1)S(1)} %maximum_bitcast_fusion.refs_0_), channel_id=1, source_target_pairs={{0,2},{1,3},{2,0},{3,1},{4,6},{5,7},{6,4},{7,5},{8,10},{9,11},{10,... | collective-permute-start | bytes 221192 | tf_op jit(solution)/shard_map/ppermute | solution.py:458
  9.4 2.7 %collective-permute-start.2 = (bf16[2,24,1536]{2,1,0:T(8,128)(2,1)S(1)}, bf16[2,24,1536]{2,1,0:T(8,128)(2,1)S(1)}, u32[]{:S(2)}, u32[]{:S(2)}) collective-permute-start(bf16[2,24,1536]{2,1,0:T(8,128)(2,1)S(1)} %join.9.refs_2_.refs_0_), channel_id=1, source_target_pairs={{0,8},{1,9},{2,10},{3,11},{4,12},{5,13},{6,14},{7,15},{8,0},{9,1},... | collective-permute-start | bytes 442376 | tf_op jit(solution)/shard_map/ppermute | solution.py:458
  13.6 2.2 %collective-permute-done.3.refs_1_ = bf16[1,4,24,384]{3,2,1,0:T(8,128)(2,1)S(1)} collective-permute-done((bf16[1,4,24,384]{3,2,1,0:T(8,128)(2,1)S(1)}, bf16[1,4,24,384]{3,2,1,0:T(8,128)(2,1)S(1)}, u32[]{:S(2)}, u32[]{:S(2)}) %collective-permute-start.3) | collective-permute-done | bytes 73760 | tf_op jit(solution)/shard_map/ppermute | solution.py:458
  19.6 2.1 %collective-permute-start.11 = (bf16[4,24,1536]{2,1,0:T(8,128)(2,1)S(1)}, bf16[4,24,1536]{2,1,0:T(8,128)(2,1)S(1)}, u32[]{:S(2)}, u32[]{:S(2)}) collective-permute-start(bf16[4,24,1536]{2,1,0:T(8,128)(2,1)S(1)} %join.13.refs_2_.refs_0_), channel_id=1, source_target_pairs={{0,8},{1,9},{2,10},{3,11},{4,12},{5,13},{6,14},{7,15},{8,0},{9,1},... | collective-permute-start | bytes 884744 | tf_op jit(solution)/shard_map/ppermute | solution.py:458
  22.6 2.2 %collective-permute-done.5.refs_1_ = bf16[4,24,1536]{2,1,0:T(8,128)(2,1)S(1)} collective-permute-done((bf16[4,24,1536]{2,1,0:T(8,128)(2,1)S(1)}, bf16[4,24,1536]{2,1,0:T(8,128)(2,1)S(1)}, u32[]{:S(2)}, u32[]{:S(2)}) %collective-permute-start.5) | collective-permute-done | bytes 294944 | tf_op jit(solution)/shard_map/ppermute | solution.py:458
  25.8 4.8 %collective-permute-done.11.refs_1_ = bf16[4,24,1536]{2,1,0:T(8,128)(2,1)S(1)} collective-permute-done((bf16[4,24,1536]{2,1,0:T(8,128)(2,1)S(1)}, bf16[4,24,1536]{2,1,0:T(8,128)(2,1)S(1)}, u32[]{:S(2)}, u32[]{:S(2)}) %collective-permute-start.11) | collective-permute-done | bytes 294944 | tf_op jit(solution)/shard_map/ppermute | solution.py:458
  32.3 9.4 %collective-permute-done.8.refs_1_ = bf16[8,24,1536]{2,1,0:T(8,128)(2,1)S(1)} collective-permute-done((bf16[8,24,1536]{2,1,0:T(8,128)(2,1)S(1)}, bf16[8,24,1536]{2,1,0:T(8,128)(2,1)S(1)}, u32[]{:S(2)}, u32[]{:S(2)}) %collective-permute-start.8) | collective-permute-done | bytes 589856 | tf_op jit(solution)/shard_map/ppermute | solution.py:458
  42.8 1.9 %collective-permute-done.12.refs_1_ = bf16[8,24,1536]{2,1,0:T(8,128)(2,1)S(1)} collective-permute-done((bf16[8,24,1536]{2,1,0:T(8,128)(2,1)S(1)}, bf16[8,24,1536]{2,1,0:T(8,128)(2,1)S(1)}, u32[]{:S(2)}, u32[]{:S(2)}) %collective-permute-start.12) | collective-permute-done | bytes 589856 | tf_op jit(solution)/shard_map/ppermute | solution.py:458
  45.4 3.4 %extractor_attention.1 = (bf16[512,384]{1,0:T(8,128)(2,1)S(1)}, bf16[512,1152]{1,0:T(8,128)(2,1)S(1)}, bf16[3,1152,256]{2,1,0:T(8,128)(2,1)S(1)}, bf16[384,512]{...) custom-call(f32[2,384]{1,0:T(2,128)S(1)} %bitcast.77, ...), custom_call_target="tpu_custom_call" | custom-call | flops 10 | bytes 8 | tf_op jit(solution)/shard_map/extractor_attention/pallas_call | solution.py:362
  50.2 3.2 %extractor_feed.1 = (bf16[512,1536]{1,0:T(8,128)(2,1)S(1)}, bf16[512,1536]{1,0:T(8,128)(2,1)S(1)}, f32[512,384]{1,0:T(8,128)S(1)}) custom-call(bf16[512,384]{1,0:T(8,128)(2,1)S(1)} %get-tuple-element.111.refs_4_.refs_0_.refs_5_, f32[512,384]{1,0:T(8,128)S(1)} %get-tuple-element.112.refs_1_.refs_6_, bf16[2,1,512,384]{3,2,1,0:T(8,128)(2,1)S(1)} %copy-done.9, ...), custom_call_target="tpu_custom_call" | custom-call | flops 32000000000 | bytes 8 | tf_op jit(solution)/shard_map/extractor_feed/pallas_call | solution.py:362
  53.4 3.3 %generator_attention.1 = (bf16[512,384]{1,0:T(8,128)(2,1)S(1)}, bf16[512,1152]{1,0:T(8,128)(2,1)S(1)}, bf16[3,1152,256]{2,1,0:T(8,128)(2,1)S(1)}, bf16[384,512]{...) custom-call(f32[2,384]{1,0:T(2,128)S(1)} %bitcast.78, ...), custom_call_target="tpu_custom_call" | custom-call | flops 10 | bytes 8 | tf_op jit(solution)/shard_map/generator_attention/pallas_call | solution.py:362
  56.8 6.3 %generator_feed.1 = (f32[512,384]{1,0:T(8,128)S(1)}, f32[512,384]{1,0:T(8,128)S(1)}, bf16[512,384]{1,0:T(8,128)(2,1)S(1)}, f32[1,384]{1,0:T(1,128)S(1)}, bf16[16...) custom-call(f32[2,384]{1,0:T(2,128)S(1)} %bitcast.79, ...), custom_call_target="tpu_custom_call" | custom-call | flops 99999997952 | bytes 8 | tf_op jit(solution)/shard_map/generator_feed/pallas_call | solution.py:362
  63.1 4.1 %generator_attention_back.1 = (bf16[16,1,24,768]{3,2,1,0:T(8,128)(2,1)S(1)}, bf16[16,1,24,768]{3,2,1,0:T(8,128)(2,1)S(1)}, bf16[512,1152]{1,0:T(8,128)(2,1)S(1)}) custom-call(bf16[512,384]{1,0:T(8,128)(2,1)S(1)} %get-tuple-element.121.refs_0_, bf16[384,512]{1,0:T(8,128)(2,1)S(1)} %get-tuple-element.122.refs_1_, ...), custom_call_target="tpu_custom_call" | custom-call | flops 60000002048 | bytes 8 | tf_op jit(solution)/shard_map/generator_attention_back/pallas_call | solution.py:362
  69.2 1.7 %collective-permute-done.20.refs_3_ = bf16[16,2,24,768]{3,2,1,0:T(8,128)(2,1)S(1)} collective-permute-done((bf16[16,2,24,768]{3,2,1,0:T(8,128)(2,1)S(1)}, bf16[16,2,24,768]{3,2,1,0:T(8,128)(2,1)S(1)}, u32[]{:S(2)}, u32[]{:S(2)}) %collective-permute-start.20) | collective-permute-done | bytes 1179680 | tf_op jit(solution)/shard_map/ppermute | solution.py:452
  72.9 3.5 %extractor_feed_back.1 = (bf16[16,2,24,768]{3,2,1,0:T(8,128)(2,1)S(1)}, bf16[16,2,24,768]{3,2,1,0:T(8,128)(2,1)S(1)}, f32[512,384]{1,0:T(8,128)S(1)}, bf16[512,384]{1,0:T(8,128)(2,1)S(1)}, f32[1,384]{1,0:T(1,128)S(1)}) custom-call(f32[2,384]{1,0:T(2,128)S(1)} %bitcast.81, f32[2,384]{1,0:T(2,128)S(1)} %collective-permute-done.refs_3_.refs_1_, ...), custom_call_target="tpu_custom_call" | custom-call | flops 70000001024 | bytes 8 | tf_op jit(solution)/shard_map/extractor_feed_back/pallas_call | solution.py:362
  76.6 3.8 %extractor_attention_back.1 = (bf16[16,1,24,768]{3,2,1,0:T(8,128)(2,1)S(1)}, bf16[16,1,24,768]{3,2,1,0:T(8,128)(2,1)S(1)}, bf16[512,1152]{1,0:T(8,128)(2,1)S(1)}) custom-call(bf16[512,384]{1,0:T(8,128)(2,1)S(1)} %get-tuple-element.136.refs_0_, bf16[384,512]{1,0:T(8,128)(2,1)S(1)} %get-tuple-element.137.refs_1_, ...), custom_call_target="tpu_custom_call" | custom-call | flops 60000002048 | bytes 8 | tf_op jit(solution)/shard_map/extractor_attention_back/pallas_call | solution.py:362
  87.6 2.4 %collective-permute-start.28 = (bf16[4,3,24,768]{3,2,1,0:T(8,128)(2,1)S(1)}, bf16[4,3,24,768]{3,2,1,0:T(8,128)(2,1)S(1)}, u32[]{:S(2)}, u32[]{:S(2)}) collective-permute-start(bf16[4,3,24,768]{3,2,1,0:T(8,128)(2,1)S(1)} %get-tuple-element.162), channel_id=1, source_target_pairs={{0,1},{1,0},{2,3},{3,2},{4,5},{5,4},{6,7},{7,6},{8,9},{9,8},{10,11... | collective-permute-start | bytes 1327112 | tf_op jit(solution)/shard_map/ppermute | solution.py:458
  90.1 6.0 %collective-permute-done.25.refs_1_ = bf16[8,3,24,768]{3,2,1,0:T(8,128)(2,1)S(1)} collective-permute-done((bf16[8,3,24,768]{3,2,1,0:T(8,128)(2,1)S(1)}, bf16[8,3,24,768]{3,2,1,0:T(8,128)(2,1)S(1)}, u32[]{:S(2)}, u32[]{:S(2)}) %collective-permute-start.25) | collective-permute-done | bytes 884768 | tf_op jit(solution)/shard_map/ppermute | solution.py:458
  96.2 2.5 %collective-permute-start.27 = (bf16[4,3,24,768]{3,2,1,0:T(8,128)(2,1)S(1)}, bf16[4,3,24,768]{3,2,1,0:T(8,128)(2,1)S(1)}, u32[]{:S(2)}, u32[]{:S(2)}) collective-permute-start(bf16[4,3,24,768]{3,2,1,0:T(8,128)(2,1)S(1)} %get-tuple-element.161), channel_id=1, source_target_pairs={{0,1},{1,0},{2,3},{3,2},{4,5},{5,4},{6,7},{7,6},{8,9},{9,8},{10,11... | collective-permute-start | bytes 1327112 | tf_op jit(solution)/shard_map/ppermute | solution.py:458
  100.6 2.2 %collective-permute-start.30 = (bf16[2,3,24,768]{3,2,1,0:T(8,128)(2,1)S(1)}, bf16[2,3,24,768]{3,2,1,0:T(8,128)(2,1)S(1)}, u32[]{:S(2)}, u32[]{:S(2)}) collective-permute-start(bf16[2,3,24,768]{3,2,1,0:T(8,128)(2,1)S(1)} %get-tuple-element.167), channel_id=1, source_target_pairs={{0,8},{1,9},{2,10},{3,11},{4,12},{5,13},{6,14},{7,15},{8,0},{9,1},... | collective-permute-start | bytes 663560 | tf_op jit(solution)/shard_map/ppermute | solution.py:458
  102.8 2.4 %collective-permute-done.27.refs_1_ = bf16[4,3,24,768]{3,2,1,0:T(8,128)(2,1)S(1)} collective-permute-done((bf16[4,3,24,768]{3,2,1,0:T(8,128)(2,1)S(1)}, bf16[4,3,24,768]{3,2,1,0:T(8,128)(2,1)S(1)}, u32[]{:S(2)}, u32[]{:S(2)}) %collective-permute-start.27) | collective-permute-done | bytes 442400 | tf_op jit(solution)/shard_map/ppermute | solution.py:458
  106.1 7.2 %collective-permute-done.30.refs_1_ = bf16[2,3,24,768]{3,2,1,0:T(8,128)(2,1)S(1)} collective-permute-done((bf16[2,3,24,768]{3,2,1,0:T(8,128)(2,1)S(1)}, bf16[2,3,24,768]{3,2,1,0:T(8,128)(2,1)S(1)}, u32[]{:S(2)}, u32[]{:S(2)}) %collective-permute-start.30) | collective-permute-done | bytes 221216 | tf_op jit(solution)/shard_map/ppermute | solution.py:458
  118.2 4.2 %collective-permute-done.31.refs_1_ = bf16[1,3,24,768]{3,2,1,0:T(8,128)(2,1)S(1)} collective-permute-done((bf16[1,3,24,768]{3,2,1,0:T(8,128)(2,1)S(1)}, bf16[1,3,24,768]{3,2,1,0:T(8,128)(2,1)S(1)}, u32[]{:S(2)}, u32[]{:S(2)}) %collective-permute-start.31) | collective-permute-done | bytes 110624 | tf_op jit(solution)/shard_map/ppermute | solution.py:458
  125.2 12.0 %all_to_all.5.refs_0_ = f32[16,3,384]{2,1,0:T(4,128)S(1)} all-to-all(f32[16,3,384]{2,1,0:T(4,128)S(1)} %get-tuple-element.182), channel_id=1, replica_groups=mesh['pipe'=2,'dp'=16] {'dp'}, dimensions={0} | all-to-all | bytes 147456 | tf_op jit(solution)/shard_map/all_to_all | solution.py:869
  (147 shorter events, 40.5 us)
Async XLA Ops:
  2.4 7.0 %collective-permute-start.1 = (bf16[1,24,1536]{2,1,0:T(8,128)(2,1)S(1)}, bf16[1,24,1536]{2,1,0:T(8,128)(2,1)S(1)}, u32[]{:S(2)}, u32[]{:S(2)}) collective-permute-start(bf16[1,24,1536]{2,1,0:T(8,128)(2,1)S(1)} %maximum_bitcast_fusion.refs_0_), channel_id=1, source_target_pairs={{0,2},{1,3},{2,0},{3,1},{4,6},{5,7},{6,4},{7,5},{8,10},{9,11},{10,... | collective-permute-start | bytes 221192 | tf_op jit(solution)/shard_map/ppermute | solution.py:458
  6.3 5.8 %collective-permute-start.4 = (bf16[1,24,1536]{2,1,0:T(8,128)(2,1)S(1)}, bf16[1,24,1536]{2,1,0:T(8,128)(2,1)S(1)}, u32[]{:S(2)}, u32[]{:S(2)}) collective-permute-start(bf16[1,24,1536]{2,1,0:T(8,128)(2,1)S(1)} %convert_element_type.27.refs_0_), channel_id=1, source_target_pairs={{0,4},{1,5},{2,6},{3,7},{4,0},{5,1},{6,2},{7,3},{8,12},{9,13},{10,... | collective-permute-start | bytes 221192 | tf_op jit(solution)/shard_map/ppermute | solution.py:458
  8.9 7.0 %collective-permute-start.3 = (bf16[1,4,24,384]{3,2,1,0:T(8,128)(2,1)S(1)}, bf16[1,4,24,384]{3,2,1,0:T(8,128)(2,1)S(1)}, u32[]{:S(2)}, u32[]{:S(2)}) collective-permute-start(bf16[1,4,24,384]{3,2,1,0:T(8,128)(2,1)S(1)} %bitcast.66), channel_id=1, source_target_pairs={{0,4},{1,5},{2,6},{3,7},{4,0},{5,1},{6,2},{7,3},{8,12},{9,13},{10,... | collective-permute-start | bytes 221192 | tf_op jit(solution)/shard_map/ppermute | solution.py:458
  9.4 8.6 %collective-permute-start.2 = (bf16[2,24,1536]{2,1,0:T(8,128)(2,1)S(1)}, bf16[2,24,1536]{2,1,0:T(8,128)(2,1)S(1)}, u32[]{:S(2)}, u32[]{:S(2)}) collective-permute-start(bf16[2,24,1536]{2,1,0:T(8,128)(2,1)S(1)} %join.9.refs_2_.refs_0_), channel_id=1, source_target_pairs={{0,8},{1,9},{2,10},{3,11},{4,12},{5,13},{6,14},{7,15},{8,0},{9,1},... | collective-permute-start | bytes 442376 | tf_op jit(solution)/shard_map/ppermute | solution.py:458
  12.1 7.5 %collective-permute-start.7 = (bf16[2,24,1536]{2,1,0:T(8,128)(2,1)S(1)}, bf16[2,24,1536]{2,1,0:T(8,128)(2,1)S(1)}, u32[]{:S(2)}, u32[]{:S(2)}) collective-permute-start(bf16[2,24,1536]{2,1,0:T(8,128)(2,1)S(1)} %join.10.refs_2_.refs_0_), channel_id=1, source_target_pairs={{0,1},{1,0},{2,3},{3,2},{4,5},{5,4},{6,7},{7,6},{8,9},{9,8},{10,11... | collective-permute-start | bytes 442376 | tf_op jit(solution)/shard_map/ppermute | solution.py:458
  15.9 6.6 %collective-permute-start.6 = (bf16[2,4,24,384]{3,2,1,0:T(8,128)(2,1)S(1)}, bf16[2,4,24,384]{3,2,1,0:T(8,128)(2,1)S(1)}, u32[]{:S(2)}, u32[]{:S(2)}) collective-permute-start(bf16[2,4,24,384]{3,2,1,0:T(8,128)(2,1)S(1)} %join.11.refs_2_.refs_0_), channel_id=1, source_target_pairs={{0,8},{1,9},{2,10},{3,11},{4,12},{5,13},{6,14},{7,15},{8,0},{9,1},... | collective-permute-start | bytes 442376 | tf_op jit(solution)/shard_map/ppermute | solution.py:458
  18.0 6.8 %collective-permute-start.5 = (bf16[4,24,1536]{2,1,0:T(8,128)(2,1)S(1)}, bf16[4,24,1536]{2,1,0:T(8,128)(2,1)S(1)}, u32[]{:S(2)}, u32[]{:S(2)}) collective-permute-start(bf16[4,24,1536]{2,1,0:T(8,128)(2,1)S(1)} %join.12.refs_2_.refs_0_), channel_id=1, source_target_pairs={{0,1},{1,0},{2,3},{3,2},{4,5},{5,4},{6,7},{7,6},{8,9},{9,8},{10,11... | collective-permute-start | bytes 884744 | tf_op jit(solution)/shard_map/ppermute | solution.py:458
  19.6 11.0 %collective-permute-start.11 = (bf16[4,24,1536]{2,1,0:T(8,128)(2,1)S(1)}, bf16[4,24,1536]{2,1,0:T(8,128)(2,1)S(1)}, u32[]{:S(2)}, u32[]{:S(2)}) collective-permute-start(bf16[4,24,1536]{2,1,0:T(8,128)(2,1)S(1)} %join.13.refs_2_.refs_0_), channel_id=1, source_target_pairs={{0,8},{1,9},{2,10},{3,11},{4,12},{5,13},{6,14},{7,15},{8,0},{9,1},... | collective-permute-start | bytes 884744 | tf_op jit(solution)/shard_map/ppermute | solution.py:458
  22.5 8.1 %collective-permute-start.15 = (bf16[4,4,24,384]{3,2,1,0:T(8,128)(2,1)S(1)}, bf16[4,4,24,384]{3,2,1,0:T(8,128)(2,1)S(1)}, u32[]{:S(2)}, u32[]{:S(2)}) collective-permute-start(bf16[4,4,24,384]{3,2,1,0:T(8,128)(2,1)S(1)} %join.14.refs_2_.refs_0_), channel_id=1, source_target_pairs={{0,2},{1,3},{2,0},{3,1},{4,6},{5,7},{6,4},{7,5},{8,10},{9,11},{10,... | collective-permute-start | bytes 884744 | tf_op jit(solution)/shard_map/ppermute | solution.py:458
  24.8 16.8 %collective-permute-start.8 = (bf16[8,24,1536]{2,1,0:T(8,128)(2,1)S(1)}, bf16[8,24,1536]{2,1,0:T(8,128)(2,1)S(1)}, u32[]{:S(2)}, u32[]{:S(2)}) collective-permute-start(bf16[8,24,1536]{2,1,0:T(8,128)(2,1)S(1)} %join.15.refs_0_.refs_2_), channel_id=1, source_target_pairs={{0,4},{1,5},{2,6},{3,7},{4,0},{5,1},{6,2},{7,3},{8,12},{9,13},{10,... | collective-permute-start | bytes 1769480 | tf_op jit(solution)/shard_map/ppermute | solution.py:458
  30.7 11.5 %collective-permute-start.16 = (bf16[8,4,24,384]{3,2,1,0:T(8,128)(2,1)S(1)}, bf16[8,4,24,384]{3,2,1,0:T(8,128)(2,1)S(1)}, u32[]{:S(2)}, u32[]{:S(2)}) collective-permute-start(bf16[8,4,24,384]{3,2,1,0:T(8,128)(2,1)S(1)} %join.17.refs_0_), channel_id=1, source_target_pairs={{0,1},{1,0},{2,3},{3,2},{4,5},{5,4},{6,7},{7,6},{8,9},{9,8},{10,11... | collective-permute-start | bytes 1769480 | tf_op jit(solution)/shard_map/ppermute | solution.py:458
  32.0 12.7 %collective-permute-start.12 = (bf16[8,24,1536]{2,1,0:T(8,128)(2,1)S(1)}, bf16[8,24,1536]{2,1,0:T(8,128)(2,1)S(1)}, u32[]{:S(2)}, u32[]{:S(2)}) collective-permute-start(bf16[8,24,1536]{2,1,0:T(8,128)(2,1)S(1)} %join.16.refs_0_.refs_2_), channel_id=1, source_target_pairs={{0,2},{1,3},{2,0},{3,1},{4,6},{5,7},{6,4},{7,5},{8,10},{9,11},{10,... | collective-permute-start | bytes 1769480 | tf_op jit(solution)/shard_map/ppermute | solution.py:458
  32.3 12.4 %collective-permute-start.9 = (bf16[8,24,1536]{2,1,0:T(8,128)(2,1)S(1)}, bf16[8,24,1536]{2,1,0:T(8,128)(2,1)S(1)}, u32[]{:S(2)}, u32[]{:S(2)}) collective-permute-start(bf16[8,24,1536]{2,1,0:T(8,128)(2,1)S(1)} %join.15.refs_0_.refs_2_), channel_id=1, source_target_pairs={{0,16},{16,0},{1,17},{17,1},{2,18},{18,2},{3,19},{19,3},{4,20},{20... | collective-permute-start | bytes 1769480 | tf_op jit(solution)/shard_map/ppermute | solution.py:452
  41.7 7.1 %collective-permute-start.17 = (bf16[8,4,24,384]{3,2,1,0:T(8,128)(2,1)S(1)}, bf16[8,4,24,384]{3,2,1,0:T(8,128)(2,1)S(1)}, u32[]{:S(2)}, u32[]{:S(2)}) collective-permute-start(bf16[8,4,24,384]{3,2,1,0:T(8,128)(2,1)S(1)} %join.17.refs_0_), channel_id=1, source_target_pairs={{0,16},{16,0},{1,17},{17,1},{2,18},{18,2},{3,19},{19,3},{4,20},{20... | collective-permute-start | bytes 1769480 | tf_op jit(solution)/shard_map/ppermute | solution.py:452
  42.2 6.6 %collective-permute-start.18 = (bf16[8,4,24,384]{3,2,1,0:T(8,128)(2,1)S(1)}, bf16[8,4,24,384]{3,2,1,0:T(8,128)(2,1)S(1)}, u32[]{:S(2)}, u32[]{:S(2)}) collective-permute-start(bf16[8,4,24,384]{3,2,1,0:T(8,128)(2,1)S(1)} %collective-permute-done.16.refs_1_), channel_id=1, source_target_pairs={{0,16},{16,0},{1,17},{17,1},{2,18},{18,2},{3,19},{19,3},{4,20},{20... | collective-permute-start | bytes 1769480 | tf_op jit(solution)/shard_map/ppermute | solution.py:452
  71.4 13.1 %collective-permute-start.21 = (bf16[8,3,24,768]{3,2,1,0:T(8,128)(2,1)S(1)}, bf16[8,3,24,768]{3,2,1,0:T(8,128)(2,1)S(1)}, u32[]{:S(2)}, u32[]{:S(2)}) collective-permute-start(bf16[8,3,24,768]{3,2,1,0:T(8,128)(2,1)S(1)} %get-tuple-element.147), channel_id=1, source_target_pairs={{0,4},{1,5},{2,6},{3,7},{4,0},{5,1},{6,2},{7,3},{8,12},{9,13},{10,... | collective-permute-start | bytes 2654216 | tf_op jit(solution)/shard_map/ppermute | solution.py:458
  76.4 6.1 %collective-permute-start.23 = (bf16[16,2,24,768]{3,2,1,0:T(8,128)(2,1)S(1)}, bf16[16,2,24,768]{3,2,1,0:T(8,128)(2,1)S(1)}, u32[]{:S(2)}, u32[]{:S(2)}) collective-permute-start(bf16[16,2,24,768]{3,2,1,0:T(8,128)(2,1)S(1)} %get-tuple-element.151), channel_id=1, source_target_pairs={{0,16},{16,0},{1,17},{17,1},{2,18},{18,2},{3,19},{19,3},{4,20},{20... | collective-permute-start | bytes 3538952 | tf_op jit(solution)/shard_map/ppermute | solution.py:452
  82.9 13.1 %collective-permute-start.25 = (bf16[8,3,24,768]{3,2,1,0:T(8,128)(2,1)S(1)}, bf16[8,3,24,768]{3,2,1,0:T(8,128)(2,1)S(1)}, u32[]{:S(2)}, u32[]{:S(2)}) collective-permute-start(bf16[8,3,24,768]{3,2,1,0:T(8,128)(2,1)S(1)} %get-tuple-element.157), channel_id=1, source_target_pairs={{0,2},{1,3},{2,0},{3,1},{4,6},{5,7},{6,4},{7,5},{8,10},{9,11},{10,... | collective-permute-start | bytes 2654216 | tf_op jit(solution)/shard_map/ppermute | solution.py:458
  87.0 11.7 %collective-permute-start.24 = (f32[512,384]{1,0:T(8,128)S(1)}, f32[512,384]{1,0:T(8,128)S(1)}, u32[]{:S(2)}, u32[]{:S(2)}) collective-permute-start(f32[512,384]{1,0:T(8,128)S(1)} %get-tuple-element.155), channel_id=1, source_target_pairs={{0,16},{16,0},{1,17},{17,1},{2,18},{18,2},{3,19},{19,3},{4,20},{20... | collective-permute-start | bytes 2359304 | tf_op jit(solution)/shard_map/ppermute | solution.py:452
  87.6 12.9 %collective-permute-start.28 = (bf16[4,3,24,768]{3,2,1,0:T(8,128)(2,1)S(1)}, bf16[4,3,24,768]{3,2,1,0:T(8,128)(2,1)S(1)}, u32[]{:S(2)}, u32[]{:S(2)}) collective-permute-start(bf16[4,3,24,768]{3,2,1,0:T(8,128)(2,1)S(1)} %get-tuple-element.162), channel_id=1, source_target_pairs={{0,1},{1,0},{2,3},{3,2},{4,5},{5,4},{6,7},{7,6},{8,9},{9,8},{10,11... | collective-permute-start | bytes 1327112 | tf_op jit(solution)/shard_map/ppermute | solution.py:458
  96.2 9.0 %collective-permute-start.27 = (bf16[4,3,24,768]{3,2,1,0:T(8,128)(2,1)S(1)}, bf16[4,3,24,768]{3,2,1,0:T(8,128)(2,1)S(1)}, u32[]{:S(2)}, u32[]{:S(2)}) collective-permute-start(bf16[4,3,24,768]{3,2,1,0:T(8,128)(2,1)S(1)} %get-tuple-element.161), channel_id=1, source_target_pairs={{0,1},{1,0},{2,3},{3,2},{4,5},{5,4},{6,7},{7,6},{8,9},{9,8},{10,11... | collective-permute-start | bytes 1327112 | tf_op jit(solution)/shard_map/ppermute | solution.py:458
  100.6 12.7 %collective-permute-start.30 = (bf16[2,3,24,768]{3,2,1,0:T(8,128)(2,1)S(1)}, bf16[2,3,24,768]{3,2,1,0:T(8,128)(2,1)S(1)}, u32[]{:S(2)}, u32[]{:S(2)}) collective-permute-start(bf16[2,3,24,768]{3,2,1,0:T(8,128)(2,1)S(1)} %get-tuple-element.167), channel_id=1, source_target_pairs={{0,8},{1,9},{2,10},{3,11},{4,12},{5,13},{6,14},{7,15},{8,0},{9,1},... | collective-permute-start | bytes 663560 | tf_op jit(solution)/shard_map/ppermute | solution.py:458
  105.5 10.1 %collective-permute-start.29 = (bf16[2,3,24,768]{3,2,1,0:T(8,128)(2,1)S(1)}, bf16[2,3,24,768]{3,2,1,0:T(8,128)(2,1)S(1)}, u32[]{:S(2)}, u32[]{:S(2)}) collective-permute-start(bf16[2,3,24,768]{3,2,1,0:T(8,128)(2,1)S(1)} %get-tuple-element.166), channel_id=1, source_target_pairs={{0,4},{1,5},{2,6},{3,7},{4,0},{5,1},{6,2},{7,3},{8,12},{9,13},{10,... | collective-permute-start | bytes 663560 | tf_op jit(solution)/shard_map/ppermute | solution.py:458
  115.6 6.7 %collective-permute-start.31 = (bf16[1,3,24,768]{3,2,1,0:T(8,128)(2,1)S(1)}, bf16[1,3,24,768]{3,2,1,0:T(8,128)(2,1)S(1)}, u32[]{:S(2)}, u32[]{:S(2)}) collective-permute-start(bf16[1,3,24,768]{3,2,1,0:T(8,128)(2,1)S(1)} %get-tuple-element.170), channel_id=1, source_target_pairs={{0,8},{1,9},{2,10},{3,11},{4,12},{5,13},{6,14},{7,15},{8,0},{9,1},... | collective-permute-start | bytes 331784 | tf_op jit(solution)/shard_map/ppermute | solution.py:458
  (42 other events, 389.8 us)
